TPU v7x, 32 devices: a whole 2x2x4 slice. The times are simulated.
32 devices in a mesh: grp: 4 (over z), tp: 8 (over y, x, core).
Axes of the slice: x: 2, y: 2, z: 4, core: 2. Of those that a mesh axis runs over, the one named last changes fastest.
Arguments:
- hidden: bfloat16 [4096, 20480], P('grp', 'tp'), may hold values from -6 to 6
- down_weight: bfloat16 [20480, 8192], P('tp'), may hold values from -0.0625 to 0.0625
- adapter_down_factor: bfloat16 [32, 64, 20480], P('grp', None, 'tp'), may hold values from -0.0390625 to 0.0390625
- adapter_up_factor: bfloat16 [32, 64, 8192], P('grp', None, 'tp'), may hold values from -0.75 to 0.75
- row_tile_adapter: int32 [32], P('grp'), may hold values from 0 to 31, as said below
- adapter_pool_slot: int32 [32], replicated, may hold values from 0 to 31, as said below
Outputs:
- output: bfloat16 [4096, 8192], P('grp', 'tp')
Inputs may be any that keep to these rules, and one draw needn't show every extreme that they name: adapter_pool_slot is a permutation; slot s of the pool is held by group s // 8. `row_tile_adapter`: at most 4 tiles of one group have adapters held by one owner group, and in every draw one owner group holds the adapters of exactly 4 tiles of every group.
All inputs are finite; a program needn't handle non-finite values.
Results may differ from a plain program's by a relative error of at most 0.019.
Values may be sent and summed in bfloat16 or wider, within the bound.
No kernel may reach another device: no remote copies, remote signals or barrier semaphores. Data moves between devices by JAX's collectives and lax.ppermute only.
A program may use at most 128 MiB of HBM per device.

v0:
```python
import jax
import jax.numpy as jnp
from jax import lax
from jax.sharding import PartitionSpec as P

adapter_scale = 2.0


def local(
    hidden, down_weight, adapter_down_factor, adapter_up_factor, row_tile_adapter, adapter_pool_slot
):
    tok_rows, feat_cols = hidden.shape
    tile_count = row_tile_adapter.shape[0]
    tile_rows = tok_rows // tile_count
    slot_table = adapter_pool_slot[row_tile_adapter]
    base_cols = lax.psum_scatter(
        lax.dot_general(
            down_weight, hidden, (((0,), (1,)), ((), ())), preferred_element_type=jnp.float32
        ).astype(jnp.bfloat16),
        "tp",
        scatter_dimension=0,
        tiled=True,
    ).astype(jnp.float32)
    pooled_down, pooled_up = (
        lax.all_gather(adapter_down_factor, "grp", axis=0, tiled=True),
        lax.all_gather(adapter_up_factor, "grp", axis=0, tiled=True),
    )
    tile_blocks = hidden.reshape(tile_count, tile_rows, feat_cols)
    rank_part = jnp.einsum(
        "ktf,krf->ktr", tile_blocks, pooled_down[slot_table], preferred_element_type=jnp.float32
    )
    rank_projections = lax.psum(rank_part.astype(jnp.bfloat16), "tp")
    adapted_output = (
        jnp.einsum(
            "pjf,pfb->pjb",
            rank_projections,
            pooled_up[slot_table],
            preferred_element_type=jnp.float32,
        )
        * adapter_scale
    ).astype(jnp.bfloat16)
    adapter_delta = adapted_output.reshape(tok_rows, -1).astype(jnp.float32)
    return (base_cols.T + adapter_delta).astype(jnp.bfloat16)


def solution(mesh):
    placed = (
        P("grp", "tp"),
        P("tp", None),
        P("grp", None, "tp"),
        P("grp", None, "tp"),
        P("grp"),
        P(),
    )
    return jax.shard_map(
        local, mesh=mesh, in_specs=placed, out_specs=P("grp", "tp"), check_vma=False
    )
```

profile of v0, /device:TPU:0, one launch (start us, length us, event | category | flops | bytes accessed | tf_op | source)
XLA Modules:
  0.0 462.6 jit_solution(18365277999326120537)
XLA Ops:
  6.5 0.0 copy-start
  6.5 0.0 all-gather.3.cloned.1.call-start
  6.5 0.7 all-gather.3.cloned.1.call-update
  7.3 0.0 all-gather.5.cloned.1.call-start
  7.3 0.7 all-gather.5.cloned.1.call-update
  8.0 0.0 all-reduce.2.cloned.1.call-start
  8.1 0.7 compare_select_fusion.1
  8.7 0.0 copy-done
  8.7 0.6 gather_fusion
  9.4 186.2 %all-gather.3.cloned.1.call-done = bf16[32,64,2560]{2,1,0:T(8,128)(2,1)} async-done(((bf16[8,64,2560]{2,1,0:T(8,128)(2,1)}), bf16[32,64,2560]{2,1,0:T(8,128)(2,1)}) %all-gather.3.cloned.1.call-update) | async-done | bytes 10485776 | tf_op jit(solution)/shard_map/all_gather | solution.py:25
  195.6 4.7 %gather_fusion.1 = bf16[8,64,2560]{2,1,0:T(8,128)(2,1)S(1)} fusion(bf16[32,64,2560]{2,1,0:T(8,128)(2,1)} %all-gather.3.cloned.1.call-done, s32[1024]{0:T(1024)S(1)} %pad_clamp_fusion), kind=kCustom, calls=%fused_computation.1 | custom fusion | bytes 5242912 | tf_op jit(solution)/shard_map/gather | solution.py:30
  200.3 5.4 %fusion.1 = bf16[8,128,64]{1,2,0:T(8,128)(2,1)} fusion(bf16[8,64,2560]{2,1,0:T(8,128)(2,1)S(1)} %gather_fusion.1, bf16[8,128,2560]{2,1,0:T(8,128)(2,1)} %bitcast.20), kind=kOutput, calls=%fused_computation.9 | convolution fusion | flops 335609856 | bytes 7995392 | tf_op jit(solution)/shard_map/ktf,krf->ktr/dot_general | solution.py:29
  205.7 0.0 all-reduce.2.cloned.1.call-update
  205.7 0.0 reduce-scatter.2.cloned.1.call-start
  205.7 50.5 %convolution_convert_fusion = bf16[8192,1024]{1,0:T(8,128)(2,1)} fusion(bf16[2560,8192]{1,0:T(8,128)(2,1)} %param.7, bf16[1024,2560]{1,0:T(8,128)(2,1)} %param.6), kind=kOutput, calls=%fused_computation.3 | convolution fusion | flops 42958061568 | bytes 63963136 | tf_op jit(solution)/shard_map/dot_general | solution.py:17
  256.2 0.0 reduce-scatter.2.cloned.1.call-update
  256.2 19.9 %all-gather.5.cloned.1.call-done = bf16[32,64,1024]{2,1,0:T(8,128)(2,1)} async-done(((bf16[8,64,1024]{2,1,0:T(8,128)(2,1)}), bf16[32,64,1024]{2,1,0:T(8,128)(2,1)}) %all-gather.5.cloned.1.call-update) | async-done | bytes 4194320 | tf_op jit(solution)/shard_map/all_gather | solution.py:26
  276.1 2.8 gather_fusion.2
  278.9 51.7 %all-reduce.2.cloned.1.call-done = bf16[8,128,64]{1,2,0:T(8,128)(2,1)} async-done(((bf16[8,128,64]{1,2,0:T(8,128)(2,1)}), bf16[8,128,64]{1,2,0:T(8,128)(2,1)}) %all-reduce.2.cloned.1.call-update) | async-done | bytes 131088 | tf_op jit(solution)/shard_map/psum | solution.py:32
  330.7 1.7 multiply_convert_fusion
  332.3 2.6 bitcast_convert_fusion
  334.9 5.3 %copy.13 = f32[1024,1024]{0,1:T(8,128)} copy(f32[1024,1024]{1,0:T(8,128)} %bitcast_convert_fusion) | data formatting | bytes 8388608 | tf_op jit(solution)/shard_map/convert_element_type | solution.py:42
  340.3 109.6 %reduce-scatter.2.cloned.1.call-done = bf16[1024,1024]{1,0:T(8,128)(2,1)} async-done(((bf16[8192,1024]{1,0:T(8,128)(2,1)}), bf16[1024,1024]{1,0:T(8,128)(2,1)}) %reduce-scatter.2.cloned.1.call-update) | async-done | bytes 2097168 | tf_op jit(solution)/shard_map/reduce_scatter | solution.py:16
  449.9 0.0 copy-start.1
  449.9 3.6 fusion
  453.5 2.6 copy.12
  456.1 0.0 copy-done.1
  (3 shorter events, 0.0 us)
Async XLA Ops:
  6.5 2.2 copy-start
  6.5 189.0 %all-gather.3.cloned.1.call-start = ((), (), s32[]{:S(2)}) async-start(), calls=%async_computation.2 | async-start | bytes 13107200 | tf_op jit(solution)/shard_map/all_gather | solution.py:25
  7.3 268.9 %all-gather.5.cloned.1.call-start = ((), (), s32[]{:S(2)}) async-start(), calls=%async_computation.4 | async-start | bytes 5242880 | tf_op jit(solution)/shard_map/all_gather | solution.py:26
  8.0 322.7 %all-reduce.2.cloned.1.call-start = ((), (), s32[]{:S(2)}) async-start(), calls=%async_computation.3 | async-start | bytes 262144 | tf_op jit(solution)/shard_map/psum | solution.py:32
  205.7 244.2 %reduce-scatter.2.cloned.1.call-start = ((), (), s32[]{:S(2)}) async-start(), calls=%async_computation.1 | async-start | bytes 18874368 | tf_op jit(solution)/shard_map/reduce_scatter | solution.py:16
  449.9 6.2 %copy-start.1 = (s32[32]{0:T(128)S(1)}, s32[32]{0:T(128)}, u32[]{:S(2)}) copy-start(s32[32]{0:T(128)} %param.11) | copy-start | bytes 388
Sparse Core Ops, SparseCore 0:
  8.9 186.6 all-gather.2
  197.1 78.9 all-gather.4
  279.2 51.4 all-reduce.1
  334.5 115.3 reduce-scatter.1
where the time goes:
time: 463 us
  waiting for transfers between devices  369 us (80%)
  matrix products  57.5 us (12%)
  local copies, waits for them, and re-layouts  16.1 us (3%)
  between operations  13.2 us (3%)
  other arithmetic  6.91 us (1%)
    all_gather x1, waiting for transfers between devices, local(): lax.all_gather(adapter_down_factor, 'grp', axis=0, tiled=True)  186 us
    reduce_scatter x1, waiting for transfers between devices, local(): lax.psum_scatter(lax.dot_general(down_weight, hidden, (((0,), (1,)), ((),...  110 us
    psum x1, waiting for transfers between devices, local(): rank_projections = lax.psum(rank_part.astype(jnp.bfloat16), 'tp')  51.7 us
    dot_general x1, matrix products, local(): lax.dot_general(down_weight, hidden, (((0,), (1,)), ((), ())), preferred_...  50.5 us
    all_gather x1, waiting for transfers between devices, local(): lax.all_gather(adapter_up_factor, 'grp', axis=0, tiled=True)  19.9 us
  transfers between devices with their start and end apart: 4, of which 4 were waited for; matrix products, arithmetic and copies ran while one was open for 16% of the time, Pallas kernels for 0%

commit v1 on v0

v1 whole, which is shorter than its diff:
```python
import functools

import jax
import jax.numpy as jnp
from jax import lax
from jax.experimental import pallas as pl
from jax.experimental.pallas import tpu as pltpu
from jax.sharding import PartitionSpec as P

adapter_scale = 2.0
OWNER_CAP = 4
CHUNKS = 2
VMEM_LIMIT = 56 * 1024 * 1024
MiB = 1024 * 1024


def params():
    return pltpu.CompilerParams(vmem_limit_bytes=VMEM_LIMIT)


def gemm_kernel(n_add, n_out, per_out, row_parts, order_ref, hidden_ref, weight_ref, *refs):
    adds, outs, (rows, sems) = refs[:n_add], refs[n_add : n_add + n_out], refs[n_add + n_out :]
    step = pl.program_id(0)
    part = rows.shape[0] // row_parts

    def copy(m):
        span = pl.ds(m * part, part)
        return pltpu.make_async_copy(hidden_ref.at[span], rows.at[span], sems.at[m])

    @pl.when(step == 0)
    def _():
        for m in range(row_parts):
            copy(m).start()

    for m in range(row_parts):
        span = pl.ds(m * part, part)

        @pl.when(step == 0)
        def _():
            copy(m).wait()

        value = jnp.dot(rows[span, :], weight_ref[...], preferred_element_type=jnp.float32)
        for add in adds:
            value = value + add[0, span, :].astype(jnp.float32)
        value = value.astype(jnp.bfloat16)
        for o in range(n_out):
            if n_out == 1:
                outs[o][0, span, :] = value
            else:

                @pl.when(step // per_out == o)
                def _():
                    outs[o][0, span, :] = value


def gemm(hidden, weight, order, width, n_cols, offset, tile, blocks_per_out, adds=()):
    tokens, depth = hidden.shape
    count = order.shape[0]
    tiles = n_cols // tile
    n_out = count // blocks_per_out
    per_out = blocks_per_out * tiles

    def weight_at(i, order_ref):
        return 0, (order_ref[i // tiles] * width + offset) // tile + i % tiles

    def add_at(i, order_ref):
        return i // tiles, 0, i % tiles

    def out_at(o, i, order_ref):
        own = jnp.clip(i - o * per_out, 0, per_out - 1)
        return own // tiles, 0, own % tiles

    row_parts = 4
    total = tokens * depth * n_cols * count
    outs = pl.pallas_call(
        functools.partial(gemm_kernel, len(adds), n_out, per_out, row_parts),
        out_shape=[jax.ShapeDtypeStruct((blocks_per_out, tokens, n_cols), jnp.bfloat16)] * n_out,
        grid_spec=pltpu.PrefetchScalarGridSpec(
            num_scalar_prefetch=1,
            grid=(count * tiles,),
            in_specs=[
                pl.BlockSpec(memory_space=pl.ANY),
                pl.BlockSpec((depth, tile), weight_at),
            ]
            + [pl.BlockSpec((1, tokens, tile), add_at)] * len(adds),
            out_specs=[pl.BlockSpec((1, tokens, tile), functools.partial(out_at, o)) for o in range(n_out)],
            scratch_shapes=[
                pltpu.VMEM((tokens, depth), jnp.bfloat16),
                pltpu.SemaphoreType.DMA((row_parts,)),
            ],
        ),
        compiler_params=params(),
        cost_estimate=pl.CostEstimate(
            flops=2 * total, bytes_accessed=2 * (tokens * depth + count * n_cols * (depth + tokens)), transcendentals=0
        ),
        name="base_products",
    )(order, hidden, weight, *adds)
    return outs


def route_kernel(groups, per_owner, dist, slot_ref, me_ref, down_ref, *refs):
    outs, sems = refs[: len(dist)], refs[len(dist)]
    tiles = slot_ref.shape[1]
    me = me_ref[0]

    def each(act):
        for k, (d, out) in enumerate(zip(dist, outs)):
            other = me + d
            inside = jnp.logical_and(other >= 0, other < groups)
            row = jnp.clip(other, 0, groups - 1)
            seen = jnp.int32(0)
            for i in range(tiles):
                slot = slot_ref[row, i]
                mine = jnp.logical_and(slot // per_owner == me, jnp.logical_and(inside, seen < OWNER_CAP))

                @pl.when(mine)
                def _(slot=slot, seen=seen, out=out, k=k, i=i):
                    act(pltpu.make_async_copy(down_ref.at[slot % per_owner], out.at[seen], sems.at[k, i]))

                seen = seen + mine.astype(jnp.int32)

    each(lambda c: c.start())
    each(lambda c: c.wait())


def route(table, me, factor, dist, groups):
    per_owner, rank, width = factor.shape
    return pl.pallas_call(
        functools.partial(route_kernel, groups, per_owner, dist),
        out_shape=[jax.ShapeDtypeStruct((OWNER_CAP, rank, width), factor.dtype)] * len(dist),
        in_specs=[
            pl.BlockSpec(memory_space=pltpu.SMEM),
            pl.BlockSpec(memory_space=pltpu.SMEM),
            pl.BlockSpec(memory_space=pl.ANY),
        ],
        out_specs=[pl.BlockSpec(memory_space=pl.ANY)] * len(dist),
        scratch_shapes=[pltpu.SemaphoreType.DMA((len(dist), table.shape[1]))],
        compiler_params=params(),
        cost_estimate=pl.CostEstimate(
            flops=0, bytes_accessed=4 * len(dist) * OWNER_CAP * rank * width, transcendentals=0
        ),
        name="adapters_to_send",
    )(table, me, factor)


def fetch(slot_ref, me, per_owner, dist, sources, held, sems, act):
    tiles = slot_ref.shape[1]
    for i in range(tiles):
        slot = slot_ref[me, i]
        owner = slot // per_owner
        place = jnp.int32(0)
        for k in range(i):
            place = place + (slot_ref[me, k] // per_owner == owner).astype(jnp.int32)
        for d, source in zip((0,) + dist, sources):
            @pl.when(me - owner == d)
            def _(d=d, source=source, slot=slot, place=place, i=i):
                at = slot % per_owner if d == 0 else place
                act(i, pltpu.make_async_copy(source.at[at], held.at[i], sems.at[i]))


def rank_kernel(per_owner, dist, slot_ref, me_ref, hidden_ref, *refs):
    sources, (out_ref, held, sems) = refs[: len(dist) + 1], refs[len(dist) + 1 :]
    me = me_ref[0]
    tiles = slot_ref.shape[1]
    rows = hidden_ref.shape[0] // tiles
    fetch(slot_ref, me, per_owner, dist, sources, held, sems, lambda i, c: c.start())
    for i in range(tiles):
        pltpu.make_async_copy(sources[0].at[0], held.at[i], sems.at[i]).wait()
        out_ref[i] = lax.dot_general(
            held[i],
            hidden_ref[pl.ds(i * rows, rows), :],
            (((1,), (1,)), ((), ())),
            preferred_element_type=jnp.float32,
        ).astype(jnp.bfloat16)


def rank_values(table, me, hidden, dist, sources):
    per_owner, rank, width = sources[0].shape
    tiles = table.shape[1]
    rows = hidden.shape[0] // tiles
    return pl.pallas_call(
        functools.partial(rank_kernel, per_owner, dist),
        out_shape=jax.ShapeDtypeStruct((tiles, rank, rows), jnp.bfloat16),
        in_specs=[
            pl.BlockSpec(memory_space=pltpu.SMEM),
            pl.BlockSpec(memory_space=pltpu.SMEM),
            pl.BlockSpec(memory_space=pltpu.VMEM),
        ]
        + [pl.BlockSpec(memory_space=pl.ANY)] * len(sources),
        out_specs=pl.BlockSpec(memory_space=pltpu.VMEM),
        scratch_shapes=[
            pltpu.VMEM((tiles, rank, width), jnp.bfloat16),
            pltpu.SemaphoreType.DMA((tiles,)),
        ],
        compiler_params=params(),
        cost_estimate=pl.CostEstimate(
            flops=8 * hidden.size * rank, bytes_accessed=2 * (hidden.size + tiles * rank * width), transcendentals=0
        ),
        name="rank_values",
    )(table, me, hidden, *sources)


def final_kernel(per_owner, dist, n_add, chunks, slot_ref, me_ref, rank_ref, *refs):
    adds, refs = refs[: n_add * chunks], refs[n_add * chunks :]
    sources, (out_ref, held, sems) = refs[: len(dist) + 1], refs[len(dist) + 1 :]
    step = pl.program_id(0)
    width = out_ref.shape[1] // chunks

    @pl.when(step == 0)
    def _():
        fetch(slot_ref, me_ref[0], per_owner, dist, sources, held, sems, lambda i, c: c.start())

    pltpu.make_async_copy(sources[0].at[0], held.at[step], sems.at[step]).wait()
    adapted = lax.dot_general(
        rank_ref[0], held[step], (((0,), (0,)), ((), ())), preferred_element_type=jnp.float32
    )
    adapted = adapter_scale * adapted
    for c in range(chunks):
        span = pl.ds(c * width, width)
        value = adapted[:, c * width : (c + 1) * width].astype(jnp.bfloat16).astype(jnp.float32)
        for add in adds[c * n_add : (c + 1) * n_add]:
            value = value + add[0].astype(jnp.float32)
        out_ref[:, span] = value.astype(jnp.bfloat16)


def final(table, me, ranks, adds, dist, sources):
    per_owner, rank, width = sources[0].shape
    tiles, _, rows = ranks.shape
    chunks, n_add = len(adds), len(adds[0])
    flat = [a for chunk in adds for a in chunk]
    return pl.pallas_call(
        functools.partial(final_kernel, per_owner, dist, n_add, chunks),
        out_shape=jax.ShapeDtypeStruct((tiles * rows, width), jnp.bfloat16),
        grid=(tiles,),
        in_specs=[
            pl.BlockSpec(memory_space=pltpu.SMEM),
            pl.BlockSpec(memory_space=pltpu.SMEM),
            pl.BlockSpec((1, rank, rows), lambda i: (i, 0, 0)),
        ]
        + [pl.BlockSpec((1, rows, a.shape[2]), lambda i: (0, i, 0)) for a in flat]
        + [pl.BlockSpec(memory_space=pl.ANY)] * len(sources),
        out_specs=pl.BlockSpec((rows, width), lambda i: (i, 0)),
        scratch_shapes=[
            pltpu.VMEM((tiles, rank, width), jnp.bfloat16),
            pltpu.SemaphoreType.DMA((tiles,)),
        ],
        compiler_params=params(),
        cost_estimate=pl.CostEstimate(
            flops=4 * tiles * rows * rank * width,
            bytes_accessed=2 * (len(flat) + 2) * tiles * rows * width // chunks,
            transcendentals=0,
        ),
        name="adapted_and_sum",
    )(table, me, ranks, *flat, *sources)


def local(
    groups,
    n_tp,
    hidden,
    down_weight,
    adapter_down_factor,
    adapter_up_factor,
    row_tile_adapter,
    adapter_pool_slot,
):
    chips = n_tp // 2
    width = down_weight.shape[1] // n_tp
    n_cols = width // CHUNKS
    tile = min(512, n_cols)
    grp, tp = lax.axis_index("grp"), lax.axis_index("tp")
    chip, core = tp // 2, tp % 2
    me = grp.reshape(1).astype(jnp.int32)

    table = adapter_pool_slot[row_tile_adapter].reshape(1, -1).astype(jnp.int32)
    step = 1
    while step < groups:
        other = lax.ppermute(table, "grp", [(g, g ^ step) for g in range(groups)])
        upper = (grp // step) % 2 == 1
        table = jnp.where(
            upper, jnp.concatenate([other, table]), jnp.concatenate([table, other])
        )
        step *= 2

    dist = tuple(d for far in range(groups - 1, 0, -1) for d in (far, -far))

    def send(v, d):
        return lax.ppermute(v, "grp", [(g, g + d) for g in range(groups) if 0 <= g + d < groups])

    down_out = route(table, me, adapter_down_factor, dist, groups)
    down_in = [adapter_down_factor] + [send(v, d) for v, d in zip(down_out, dist)]
    up_out = route(table, me, adapter_up_factor, dist, groups)
    up_in = [adapter_up_factor] + [send(v, d) for v, d in zip(up_out, dist)]

    relative = jnp.array(list(range(1, chips)) + [0], jnp.int32)
    far_chips = (chip ^ relative).astype(jnp.int32)
    theirs, ours = far_chips * 2 + (1 - core), far_chips * 2 + core
    adds = []
    for c in range(CHUNKS):
        (first,) = gemm(hidden, down_weight, theirs, width, n_cols, c * n_cols, tile, chips)
        other = lax.ppermute(first, "tp", [(i, i ^ 1) for i in range(n_tp)])
        sums = gemm(hidden, down_weight, ours, width, n_cols, c * n_cols, tile, 1, (other,))
        got = [
            lax.ppermute(sums[r - 1], "tp", [(i, i ^ (2 * r)) for i in range(n_tp)])
            for r in range(1, chips)
        ]
        adds.append([sums[chips - 1]] + got)

    ranks = rank_values(table, me, hidden, dist, down_in)
    bit = 1
    while bit < n_tp:
        ranks = ranks + lax.ppermute(ranks, "tp", [(i, i ^ bit) for i in range(n_tp)])
        bit *= 2

    return final(table, me, ranks, adds, dist, up_in)


def solution(mesh):
    placed = (
        P("grp", "tp"),
        P("tp", None),
        P("grp", None, "tp"),
        P("grp", None, "tp"),
        P("grp"),
        P(),
    )
    return jax.shard_map(
        functools.partial(local, mesh.shape["grp"], mesh.shape["tp"]),
        mesh=mesh,
        in_specs=placed,
        out_specs=P("grp", "tp"),
        check_vma=False,
    )
```

time: 463 us -> 515 us (1.11)
  Pallas kernels: 0 us -> 267 us
  waiting for transfers between devices: 369 us -> 196 us
  matrix products: 57.5 us -> 0 us
  starting transfers between devices: 0.12 us -> 39.5 us
  between operations: 13.2 us -> 0.59 us
  local copies, waits for them, and re-layouts: 16.1 us -> 5.47 us
    pallas_call x0 -> x8, Pallas kernels: none -> 267 us  [the longest x2 171 us: route(): pl.pallas_call(functools.partial(route_kernel, groups, per_owner, dist),...]
    all_gather x2 -> x0, waiting for transfers between devices: 206 us -> none  [the longest x1 186 us: local(): lax.all_gather(adapter_down_factor, 'grp', axis=0, tiled=True)]
    ppermute x0 -> x25, waiting for transfers between devices: none -> 196 us  [the longest x12 110 us: send(): lax.ppermute(v, 'grp', [(g, g + d) for g in range(groups) if 0 <= g + d <...]
    reduce_scatter x1 -> x0, waiting for transfers between devices: 110 us -> none  [local(): lax.psum_scatter(lax.dot_general(down_weight, hidden, (((0,), (1,)), ((),...]
    dot_general x3 -> x0, matrix products: 57.5 us -> none  [the longest x1 50.5 us: local(): lax.dot_general(down_weight, hidden, (((0,), (1,)), ((), ())), preferred_...]
    psum x1 -> x0, waiting for transfers between devices: 51.7 us -> none  [local(): rank_projections = lax.psum(rank_part.astype(jnp.bfloat16), 'tp')]
    ppermute x0 -> x25, starting transfers between devices: none -> 39.5 us  [the longest x12 22.4 us: send(): lax.ppermute(v, 'grp', [(g, g + d) for g in range(groups) if 0 <= g + d <...]
    convert_element_type x2 -> x0, local copies, waits for them, and re-layouts: 7.91 us -> none  [the longest x1 5.35 us: local(): adapter_delta = adapted_output.reshape(tok_rows, -1).astype(jnp.float32)]
  transfers between devices with their start and end apart: 4 -> 25, of which waited for: 4 -> 9; matrix products, arithmetic and copies ran while one was open for 16% -> 1% of each run, Pallas kernels for 0% -> 47%
where the time goes in v1:
time: 515 us; the launch traced here: 512 us
  Pallas kernels  267 us (52%)
  waiting for transfers between devices  196 us (38%)
  starting transfers between devices  39.5 us (8%)
  local copies, waits for them, and re-layouts  5.47 us (1%)
    pallas_call x2, Pallas kernels, route(): pl.pallas_call(functools.partial(route_kernel, groups, per_owner, dist),...  171 us
    ppermute x12, waiting for transfers between devices, send(): lax.ppermute(v, 'grp', [(g, g + d) for g in range(groups) if 0 <= g + d <...  110 us
    ppermute x6, waiting for transfers between devices, local(): lax.ppermute(sums[r - 1], 'tp', [(i, i ^ 2 * r) for i in range(n_tp)])  82.7 us
    pallas_call x4, Pallas kernels, gemm(): pl.pallas_call(functools.partial(gemm_kernel, len(adds), n_out, per_out,...  78.4 us
    ppermute x12, starting transfers between devices, send(): lax.ppermute(v, 'grp', [(g, g + d) for g in range(groups) if 0 <= g + d <...  22.4 us
  transfers between devices with their start and end apart: 25, of which 9 were waited for; matrix products, arithmetic and copies ran while one was open for 1% of the time, Pallas kernels for 47%

profile of v1, /device:TPU:0, one launch (start us, length us, event | category | flops | bytes accessed | tf_op | source)
XLA Modules:
  0.0 512.2 jit_solution(2516209944882784308)
XLA Ops:
  0.0 1.3 fusion
  1.3 18.6 %base_products.4 = bf16[4,1024,512]{2,1,0:T(8,128)(2,1)} custom-call(s32[4]{0:T(128)} %get-tuple-element.45.order_ref, bf16[1024,2560]{1,0:T(8,128)(2,1)} %hidden_ref.9, bf16[2560,8192]{1,0:T(8,128)(2,1)} %weight_ref.7), custom_call_target="tpu_custom_call" | custom-call | flops 10737418240 | bytes 19922944 | tf_op jit(solution)/shard_map/base_products/pallas_call | solution.py:75
  19.8 0.5 collective-permute-start.11
  20.4 18.6 %base_products.6 = bf16[4,1024,512]{2,1,0:T(8,128)(2,1)} custom-call(s32[4]{0:T(128)} %get-tuple-element.45.order_ref, bf16[1024,2560]{1,0:T(8,128)(2,1)} %hidden_ref.9, bf16[2560,8192]{1,0:T(8,128)(2,1)} %weight_ref.7), custom_call_target="tpu_custom_call" | custom-call | flops 10737418240 | bytes 19922944 | tf_op jit(solution)/shard_map/base_products/pallas_call | solution.py:75
  39.1 0.6 gather_fusion
  39.8 3.1 collective-permute-start
  42.9 1.5 collective-permute-done
  44.4 3.1 collective-permute-start.1
  47.5 1.5 collective-permute-done.1
  49.0 0.6 add_select_fusion.slot_ref
  49.6 121.3 %adapters_to_send.2 = (bf16[4,64,2560]{2,1,0:T(8,128)(2,1)}, bf16[4,64,2560]{2,1,0:T(8,128)(2,1)}, bf16[4,64,2560]{2,1,0:T(8,128)(2,1)}, bf16[4,64,2560]{2,1,0:T...) custom-call(s32[4,8]{1,0:T(4,128)} %add_select_fusion.slot_ref, s32[1]{0:T(128)} %bitcast.1.me_ref, ...), custom_call_target="tpu_custom_call" | custom-call | bytes 15728640 | tf_op jit(solution)/shard_map/adapters_to_send/pallas_call | solution.py:128
  171.0 1.4 collective-permute-start.2
  172.4 1.3 collective-permute-start.3
  173.7 1.4 collective-permute-start.4
  175.1 26.8 %collective-permute-done.2.refs_1_ = bf16[4,64,2560]{2,1,0:T(8,128)(2,1)S(1)} collective-permute-done((bf16[4,64,2560]{2,1,0:T(8,128)(2,1)}, bf16[4,64,2560]{2,1,0:T(8,128)(2,1)S(1)}, u32[]{:S(2)}, u32[]{:S(2)}) %collective-permute-start.2) | collective-permute-done | bytes 1310752 | tf_op jit(solution)/shard_map/ppermute | solution.py:288
  201.9 1.3 collective-permute-start.5
  203.2 3.8 collective-permute-done.3.refs_2_
  207.0 1.4 collective-permute-start.6
  208.3 21.6 %collective-permute-done.4.refs_3_ = bf16[4,64,2560]{2,1,0:T(8,128)(2,1)S(1)} collective-permute-done((bf16[4,64,2560]{2,1,0:T(8,128)(2,1)}, bf16[4,64,2560]{2,1,0:T(8,128)(2,1)S(1)}, u32[]{:S(2)}, u32[]{:S(2)}) %collective-permute-start.4) | collective-permute-done | bytes 1310752 | tf_op jit(solution)/shard_map/ppermute | solution.py:288
  230.0 1.3 collective-permute-start.7
  231.2 30.0 %collective-permute-done.5.refs_4_ = bf16[4,64,2560]{2,1,0:T(8,128)(2,1)S(1)} collective-permute-done((bf16[4,64,2560]{2,1,0:T(8,128)(2,1)}, bf16[4,64,2560]{2,1,0:T(8,128)(2,1)S(1)}, u32[]{:S(2)}, u32[]{:S(2)}) %collective-permute-start.5) | collective-permute-done | bytes 1310752 | tf_op jit(solution)/shard_map/ppermute | solution.py:288
  261.3 28.0 %collective-permute-done.7.refs_6_ = bf16[4,64,2560]{2,1,0:T(8,128)(2,1)S(1)} collective-permute-done((bf16[4,64,2560]{2,1,0:T(8,128)(2,1)}, bf16[4,64,2560]{2,1,0:T(8,128)(2,1)S(1)}, u32[]{:S(2)}, u32[]{:S(2)}) %collective-permute-start.7) | collective-permute-done | bytes 1310752 | tf_op jit(solution)/shard_map/ppermute | solution.py:288
  289.3 1.1 copy-done.7
  290.3 8.0 %rank_values.1 = bf16[8,64,128]{2,1,0:T(8,128)(2,1)} custom-call(s32[4,8]{1,0:T(4,128)} %add_select_fusion.slot_ref, s32[1]{0:T(128)} %bitcast.1.me_ref, bf16[1024,2560]{1,0:T(8,128)(2,1)} %hidden_ref.9, bf16[8,64,2560]{2,1,0:T(8,128)(2,1)} %refs_0_.1, bf16[4,64,2560]{2,1,0:T(8,128)(2,1)} %copy-done.2, bf16[4,64,2560]{2,1,0:T(8,128)(2,1)} %copy-done.3, ...), custom_call_target="tpu_custom_call" | custom-call | flops 1342177280 | bytes 7864320 | tf_op jit(solution)/shard_map/rank_values/pallas_call | solution.py:181
  298.4 49.9 %adapters_to_send.3 = (bf16[4,64,1024]{2,1,0:T(8,128)(2,1)}, bf16[4,64,1024]{2,1,0:T(8,128)(2,1)}, bf16[4,64,1024]{2,1,0:T(8,128)(2,1)}, bf16[4,64,1024]{2,1,0:T...) custom-call(s32[4,8]{1,0:T(4,128)} %add_select_fusion.slot_ref, s32[1]{0:T(128)} %bitcast.1.me_ref, ...), custom_call_target="tpu_custom_call" | custom-call | bytes 6291456 | tf_op jit(solution)/shard_map/adapters_to_send/pallas_call | solution.py:128
  348.3 1.3 collective-permute-start.19
  349.6 1.3 collective-permute-start.20
  351.0 1.3 collective-permute-start.21
  352.3 1.0 add.40
  353.3 1.6 collective-permute-start.9
  354.9 20.7 %base_products.5 = (bf16[1,1024,512]{2,1,0:T(8,128)(2,1)}, bf16[1,1024,512]{2,1,0:T(8,128)(2,1)}, bf16[1,1024,512]{2,1,0:T(8,128)(2,1)}, bf16[1,1024,512]{2,1,0:T(8,128)(2,1)}) custom-call(s32[4]{0:T(128)} %get-tuple-element.46.order_ref, bf16[1024,2560]{1,0:T(8,128)(2,1)} %hidden_ref.9, bf16[2560,8192]{1,0:T(8,128)(2,1)} %weight_ref.7, ...), custom_call_target="tpu_custom_call" | custom-call | flops 10737418240 | bytes 19922944 | tf_op jit(solution)/shard_map/base_products/pallas_call | solution.py:75
  375.5 0.6 collective-permute-start.12
  376.2 1.3 collective-permute-start.22
  377.5 7.6 %collective-permute-start.23 = (bf16[4,64,1024]{2,1,0:T(8,128)(2,1)S(1)}, bf16[4,64,1024]{2,1,0:T(8,128)(2,1)S(1)}, u32[]{:S(2)}, u32[]{:S(2)}) collective-permute-start(bf16[4,64,1024]{2,1,0:T(8,128)(2,1)S(1)} %copy-done.22), channel_id=1, source_target_pairs={{0,8},{8,16},{16,24},{1,9},{9,17},{17,25},{2,10},{10,18},{18,26},{... | collective-permute-start | bytes 1572872 | tf_op jit(solution)/shard_map/ppermute | solution.py:288
  385.1 1.6 collective-permute-start.24
  386.8 1.6 collective-permute-start.10
  388.4 20.5 %base_products.7 = (bf16[1,1024,512]{2,1,0:T(8,128)(2,1)}, bf16[1,1024,512]{2,1,0:T(8,128)(2,1)}, bf16[1,1024,512]{2,1,0:T(8,128)(2,1)}, bf16[1,1024,512]{2,1,0:T(8,128)(2,1)}) custom-call(s32[4]{0:T(128)} %get-tuple-element.46.order_ref, bf16[1024,2560]{1,0:T(8,128)(2,1)} %hidden_ref.9, bf16[2560,8192]{1,0:T(8,128)(2,1)} %weight_ref.7, ...), custom_call_target="tpu_custom_call" | custom-call | flops 10737418240 | bytes 19922944 | tf_op jit(solution)/shard_map/base_products/pallas_call | solution.py:75
  409.0 0.8 copy-done.17
  410.2 0.8 copy-done.18
  411.0 2.5 collective-permute-start.14
  413.5 0.8 copy-done.19
  414.3 0.5 collective-permute-start.16
  415.3 2.5 collective-permute-start.18
  417.8 0.7 add.42.rank_ref
  418.5 62.1 %collective-permute-done.13.refs_2_ = bf16[1,1024,512]{2,1,0:T(8,128)(2,1)S(1)} collective-permute-done((bf16[1,1024,512]{2,1,0:T(8,128)(2,1)}, bf16[1,1024,512]{2,1,0:T(8,128)(2,1)S(1)}, u32[]{:S(2)}, u32[]{:S(2)}) %collective-permute-start.13) | collective-permute-done | bytes 1048608 | tf_op jit(solution)/shard_map/ppermute | solution.py:304
  480.6 20.6 %collective-permute-done.17.refs_6_ = bf16[1,1024,512]{2,1,0:T(8,128)(2,1)S(1)} collective-permute-done((bf16[1,1024,512]{2,1,0:T(8,128)(2,1)}, bf16[1,1024,512]{2,1,0:T(8,128)(2,1)S(1)}, u32[]{:S(2)}, u32[]{:S(2)}) %collective-permute-start.17) | collective-permute-done | bytes 1048608 | tf_op jit(solution)/shard_map/ppermute | solution.py:304
  501.3 1.0 copy-done.12
  502.6 9.5 %adapted_and_sum.1 = bf16[1024,1024]{1,0:T(8,128)(2,1)} custom-call(s32[4,8]{1,0:T(4,128)} %add_select_fusion.slot_ref, s32[1]{0:T(128)} %bitcast.1.me_ref, bf16[8,64,128]{2,1,0:T(8,128)(2,1)} %add.42.rank_ref, bf16[1,1024,512]{2,1,0:T(8,128)(2,1)} %get-tuple-element.31.refs_0_, bf16[1,1024,512]{2,1,0:T(8,128)(2,1)} %copy-done.8, ...), custom_call_target="tpu_custom_call" | custom-call | flops 268435456 | bytes 10485760 | tf_op jit(solution)/shard_map/adapted_and_sum/pallas_call | solution.py:231
  (69 shorter events, 1.7 us)
Async XLA Ops:
  0.0 39.1 %copy-start = (s32[32]{0:T(128)S(1)}, s32[32]{0:T(128)}, u32[]{:S(2)}) copy-start(s32[32]{0:T(128)} %param.12) | copy-start | bytes 388
  19.8 19.3 %copy-start.24 = (s32[8]{0:T(128)S(1)}, s32[8]{0:T(128)}, u32[]{:S(2)}) copy-start(s32[8]{0:T(128)} %param.11) | copy-start | bytes 100
  19.8 333.4 %collective-permute-start.11 = (bf16[4,1024,512]{2,1,0:T(8,128)(2,1)}, bf16[4,1024,512]{2,1,0:T(8,128)(2,1)}, u32[]{:S(2)}, u32[]{:S(2)}) collective-permute-start(bf16[4,1024,512]{2,1,0:T(8,128)(2,1)} %base_products.4), channel_id=1, source_target_pairs={{0,1},{1,0},{2,3},{3,2},{4,5},{5,4},{6,7},{7,6},{8,9},{9,8},{10,11... | collective-permute-start | bytes 12582920 | tf_op jit(solution)/shard_map/ppermute | solution.py:301
  39.0 347.8 %collective-permute-start.15 = (bf16[4,1024,512]{2,1,0:T(8,128)(2,1)}, bf16[4,1024,512]{2,1,0:T(8,128)(2,1)}, u32[]{:S(2)}, u32[]{:S(2)}) collective-permute-start(bf16[4,1024,512]{2,1,0:T(8,128)(2,1)} %base_products.6), channel_id=1, source_target_pairs={{0,1},{1,0},{2,3},{3,2},{4,5},{5,4},{6,7},{7,6},{8,9},{9,8},{10,11... | collective-permute-start | bytes 12582920 | tf_op jit(solution)/shard_map/ppermute | solution.py:301
  39.8 4.6 collective-permute-start
  44.4 4.6 collective-permute-start.1
  171.0 30.9 %collective-permute-start.2 = (bf16[4,64,2560]{2,1,0:T(8,128)(2,1)}, bf16[4,64,2560]{2,1,0:T(8,128)(2,1)S(1)}, u32[]{:S(2)}, u32[]{:S(2)}) collective-permute-start(bf16[4,64,2560]{2,1,0:T(8,128)(2,1)} %get-tuple-element.25), channel_id=1, source_target_pairs={{0,24},{1,25},{2,26},{3,27},{4,28},{5,29},{6,30},{7,31}} | collective-permute-start | bytes 3932168 | tf_op jit(solution)/shard_map/ppermute | solution.py:288
  172.4 34.6 %collective-permute-start.3 = (bf16[4,64,2560]{2,1,0:T(8,128)(2,1)}, bf16[4,64,2560]{2,1,0:T(8,128)(2,1)S(1)}, u32[]{:S(2)}, u32[]{:S(2)}) collective-permute-start(bf16[4,64,2560]{2,1,0:T(8,128)(2,1)} %get-tuple-element.26), channel_id=1, source_target_pairs={{24,0},{25,1},{26,2},{27,3},{28,4},{29,5},{30,6},{31,7}} | collective-permute-start | bytes 3932168 | tf_op jit(solution)/shard_map/ppermute | solution.py:288
  173.7 56.3 %collective-permute-start.4 = (bf16[4,64,2560]{2,1,0:T(8,128)(2,1)}, bf16[4,64,2560]{2,1,0:T(8,128)(2,1)S(1)}, u32[]{:S(2)}, u32[]{:S(2)}) collective-permute-start(bf16[4,64,2560]{2,1,0:T(8,128)(2,1)} %get-tuple-element.27), channel_id=1, source_target_pairs={{0,16},{8,24},{1,17},{9,25},{2,18},{10,26},{3,19},{11,27},{4,20},{... | collective-permute-start | bytes 3932168 | tf_op jit(solution)/shard_map/ppermute | solution.py:288
  201.9 87.4 %copy-start.2 = (bf16[4,64,2560]{2,1,0:T(8,128)(2,1)}, bf16[4,64,2560]{2,1,0:T(8,128)(2,1)S(1)}, u32[]{:S(2)}) copy-start(bf16[4,64,2560]{2,1,0:T(8,128)(2,1)S(1)} %collective-permute-done.2.refs_1_) | copy-start | bytes 3932164
  201.9 59.4 %collective-permute-start.5 = (bf16[4,64,2560]{2,1,0:T(8,128)(2,1)}, bf16[4,64,2560]{2,1,0:T(8,128)(2,1)S(1)}, u32[]{:S(2)}, u32[]{:S(2)}) collective-permute-start(bf16[4,64,2560]{2,1,0:T(8,128)(2,1)} %get-tuple-element.28), channel_id=1, source_target_pairs={{16,0},{24,8},{17,1},{25,9},{18,2},{26,10},{19,3},{27,11},{20,4},{... | collective-permute-start | bytes 3932168 | tf_op jit(solution)/shard_map/ppermute | solution.py:288
  207.0 82.3 %copy-start.3 = (bf16[4,64,2560]{2,1,0:T(8,128)(2,1)}, bf16[4,64,2560]{2,1,0:T(8,128)(2,1)S(1)}, u32[]{:S(2)}) copy-start(bf16[4,64,2560]{2,1,0:T(8,128)(2,1)S(1)} %collective-permute-done.3.refs_2_) | copy-start | bytes 3932164
  207.0 54.3 %collective-permute-start.6 = (bf16[4,64,2560]{2,1,0:T(8,128)(2,1)}, bf16[4,64,2560]{2,1,0:T(8,128)(2,1)S(1)}, u32[]{:S(2)}, u32[]{:S(2)}) collective-permute-start(bf16[4,64,2560]{2,1,0:T(8,128)(2,1)} %get-tuple-element.29), channel_id=1, source_target_pairs={{0,8},{8,16},{16,24},{1,9},{9,17},{17,25},{2,10},{10,18},{18,26},{... | collective-permute-start | bytes 3932168 | tf_op jit(solution)/shard_map/ppermute | solution.py:288
  230.0 59.3 %copy-start.4 = (bf16[4,64,2560]{2,1,0:T(8,128)(2,1)}, bf16[4,64,2560]{2,1,0:T(8,128)(2,1)S(1)}, u32[]{:S(2)}) copy-start(bf16[4,64,2560]{2,1,0:T(8,128)(2,1)S(1)} %collective-permute-done.4.refs_3_) | copy-start | bytes 3932164
  230.0 59.3 %collective-permute-start.7 = (bf16[4,64,2560]{2,1,0:T(8,128)(2,1)}, bf16[4,64,2560]{2,1,0:T(8,128)(2,1)S(1)}, u32[]{:S(2)}, u32[]{:S(2)}) collective-permute-start(bf16[4,64,2560]{2,1,0:T(8,128)(2,1)} %get-tuple-element.30), channel_id=1, source_target_pairs={{8,0},{16,8},{24,16},{9,1},{17,9},{25,17},{10,2},{18,10},{26,18},{... | collective-permute-start | bytes 3932168 | tf_op jit(solution)/shard_map/ppermute | solution.py:288
  261.3 28.0 %copy-start.5 = (bf16[4,64,2560]{2,1,0:T(8,128)(2,1)}, bf16[4,64,2560]{2,1,0:T(8,128)(2,1)S(1)}, u32[]{:S(2)}) copy-start(bf16[4,64,2560]{2,1,0:T(8,128)(2,1)S(1)} %collective-permute-done.5.refs_4_) | copy-start | bytes 3932164
  261.3 28.0 %copy-start.6 = (bf16[4,64,2560]{2,1,0:T(8,128)(2,1)}, bf16[4,64,2560]{2,1,0:T(8,128)(2,1)S(1)}, u32[]{:S(2)}) copy-start(bf16[4,64,2560]{2,1,0:T(8,128)(2,1)S(1)} %collective-permute-done.6.refs_5_) | copy-start | bytes 3932164
  289.3 1.1 copy-start.7
  298.3 52.6 %collective-permute-start.8 = (bf16[8,64,128]{2,1,0:T(8,128)(2,1)}, bf16[8,64,128]{2,1,0:T(8,128)(2,1)S(1)}, u32[]{:S(2)}, u32[]{:S(2)}) collective-permute-start(bf16[8,64,128]{2,1,0:T(8,128)(2,1)} %rank_values.1), channel_id=1, source_target_pairs={{0,1},{1,0},{2,3},{3,2},{4,5},{5,4},{6,7},{7,6},{8,9},{9,8},{10,11... | collective-permute-start | bytes 393224 | tf_op jit(solution)/shard_map/ppermute | solution.py:312
  348.3 27.8 %collective-permute-start.19 = (bf16[4,64,1024]{2,1,0:T(8,128)(2,1)}, bf16[4,64,1024]{2,1,0:T(8,128)(2,1)S(1)}, u32[]{:S(2)}, u32[]{:S(2)}) collective-permute-start(bf16[4,64,1024]{2,1,0:T(8,128)(2,1)} %get-tuple-element.39), channel_id=1, source_target_pairs={{0,24},{1,25},{2,26},{3,27},{4,28},{5,29},{6,30},{7,31}} | collective-permute-start | bytes 1572872 | tf_op jit(solution)/shard_map/ppermute | solution.py:288
  349.6 27.8 %collective-permute-start.20 = (bf16[4,64,1024]{2,1,0:T(8,128)(2,1)}, bf16[4,64,1024]{2,1,0:T(8,128)(2,1)S(1)}, u32[]{:S(2)}, u32[]{:S(2)}) collective-permute-start(bf16[4,64,1024]{2,1,0:T(8,128)(2,1)} %get-tuple-element.40), channel_id=1, source_target_pairs={{24,0},{25,1},{26,2},{27,3},{28,4},{29,5},{30,6},{31,7}} | collective-permute-start | bytes 1572872 | tf_op jit(solution)/shard_map/ppermute | solution.py:288
  351.0 34.1 %collective-permute-start.21 = (bf16[4,64,1024]{2,1,0:T(8,128)(2,1)}, bf16[4,64,1024]{2,1,0:T(8,128)(2,1)S(1)}, u32[]{:S(2)}, u32[]{:S(2)}) collective-permute-start(bf16[4,64,1024]{2,1,0:T(8,128)(2,1)} %get-tuple-element.41), channel_id=1, source_target_pairs={{0,16},{8,24},{1,17},{9,25},{2,18},{10,26},{3,19},{11,27},{4,20},{... | collective-permute-start | bytes 1572872 | tf_op jit(solution)/shard_map/ppermute | solution.py:288
  353.3 22.3 %collective-permute-start.9 = (bf16[8,64,128]{2,1,0:T(8,128)(2,1)S(1)}, bf16[8,64,128]{2,1,0:T(8,128)(2,1)S(1)}, u32[]{:S(2)}, u32[]{:S(2)}) collective-permute-start(bf16[8,64,128]{2,1,0:T(8,128)(2,1)S(1)} %add.40), channel_id=1, source_target_pairs={{0,2},{1,3},{2,0},{3,1},{4,6},{5,7},{6,4},{7,5},{8,10},{9,11},{10,... | collective-permute-start | bytes 393224 | tf_op jit(solution)/shard_map/ppermute | solution.py:312
  354.9 21.3 %copy-start.23 = (bf16[4,64,1024]{2,1,0:T(8,128)(2,1)S(1)}, bf16[4,64,1024]{2,1,0:T(8,128)(2,1)}, u32[]{:S(2)}) copy-start(bf16[4,64,1024]{2,1,0:T(8,128)(2,1)} %get-tuple-element.42) | copy-start | bytes 1572868
  354.9 22.6 %copy-start.22 = (bf16[4,64,1024]{2,1,0:T(8,128)(2,1)S(1)}, bf16[4,64,1024]{2,1,0:T(8,128)(2,1)}, u32[]{:S(2)}) copy-start(bf16[4,64,1024]{2,1,0:T(8,128)(2,1)} %get-tuple-element.43) | copy-start | bytes 1572868
  354.9 30.2 %copy-start.21 = (bf16[4,64,1024]{2,1,0:T(8,128)(2,1)S(1)}, bf16[4,64,1024]{2,1,0:T(8,128)(2,1)}, u32[]{:S(2)}) copy-start(bf16[4,64,1024]{2,1,0:T(8,128)(2,1)} %get-tuple-element.44) | copy-start | bytes 1572868
  375.5 39.8 %collective-permute-start.12 = (bf16[1,1024,512]{2,1,0:T(8,128)(2,1)}, bf16[1,1024,512]{2,1,0:T(8,128)(2,1)S(1)}, u32[]{:S(2)}, u32[]{:S(2)}) collective-permute-start(bf16[1,1024,512]{2,1,0:T(8,128)(2,1)} %get-tuple-element.32), channel_id=1, source_target_pairs={{0,2},{1,3},{2,0},{3,1},{4,6},{5,7},{6,4},{7,5},{8,10},{9,11},{10,... | collective-permute-start | bytes 3145736 | tf_op jit(solution)/shard_map/ppermute | solution.py:304
  376.1 32.8 %copy-start.14 = (bf16[4,64,1024]{2,1,0:T(8,128)(2,1)}, bf16[4,64,1024]{2,1,0:T(8,128)(2,1)S(1)}, u32[]{:S(2)}) copy-start(bf16[4,64,1024]{2,1,0:T(8,128)(2,1)S(1)} %collective-permute-done.19.refs_9_) | copy-start | bytes 1572868
  376.2 32.8 %collective-permute-start.22 = (bf16[4,64,1024]{2,1,0:T(8,128)(2,1)S(1)}, bf16[4,64,1024]{2,1,0:T(8,128)(2,1)S(1)}, u32[]{:S(2)}, u32[]{:S(2)}) collective-permute-start(bf16[4,64,1024]{2,1,0:T(8,128)(2,1)S(1)} %copy-done.23), channel_id=1, source_target_pairs={{16,0},{24,8},{17,1},{25,9},{18,2},{26,10},{19,3},{27,11},{20,4},{... | collective-permute-start | bytes 1572872 | tf_op jit(solution)/shard_map/ppermute | solution.py:288
  377.5 31.4 %copy-start.15 = (bf16[4,64,1024]{2,1,0:T(8,128)(2,1)}, bf16[4,64,1024]{2,1,0:T(8,128)(2,1)S(1)}, u32[]{:S(2)}) copy-start(bf16[4,64,1024]{2,1,0:T(8,128)(2,1)S(1)} %collective-permute-done.20.refs_10_) | copy-start | bytes 1572868
  377.5 32.7 %collective-permute-start.23 = (bf16[4,64,1024]{2,1,0:T(8,128)(2,1)S(1)}, bf16[4,64,1024]{2,1,0:T(8,128)(2,1)S(1)}, u32[]{:S(2)}, u32[]{:S(2)}) collective-permute-start(bf16[4,64,1024]{2,1,0:T(8,128)(2,1)S(1)} %copy-done.22), channel_id=1, source_target_pairs={{0,8},{8,16},{16,24},{1,9},{9,17},{17,25},{2,10},{10,18},{18,26},{... | collective-permute-start | bytes 1572872 | tf_op jit(solution)/shard_map/ppermute | solution.py:288
  385.1 23.8 %copy-start.16 = (bf16[4,64,1024]{2,1,0:T(8,128)(2,1)}, bf16[4,64,1024]{2,1,0:T(8,128)(2,1)S(1)}, u32[]{:S(2)}) copy-start(bf16[4,64,1024]{2,1,0:T(8,128)(2,1)S(1)} %collective-permute-done.21.refs_11_) | copy-start | bytes 1572868
  385.1 25.9 %copy-start.20 = (bf16[1,1024,512]{2,1,0:T(8,128)(2,1)S(1)}, bf16[1,1024,512]{2,1,0:T(8,128)(2,1)}, u32[]{:S(2)}) copy-start(bf16[1,1024,512]{2,1,0:T(8,128)(2,1)} %get-tuple-element.34) | copy-start | bytes 3145732
  385.1 28.4 %collective-permute-start.24 = (bf16[4,64,1024]{2,1,0:T(8,128)(2,1)S(1)}, bf16[4,64,1024]{2,1,0:T(8,128)(2,1)S(1)}, u32[]{:S(2)}, u32[]{:S(2)}) collective-permute-start(bf16[4,64,1024]{2,1,0:T(8,128)(2,1)S(1)} %copy-done.21), channel_id=1, source_target_pairs={{8,0},{16,8},{24,16},{9,1},{17,9},{25,17},{10,2},{18,10},{26,18},{... | collective-permute-start | bytes 1572872 | tf_op jit(solution)/shard_map/ppermute | solution.py:288
  386.8 28.1 %collective-permute-start.10 = (bf16[8,64,128]{2,1,0:T(8,128)(2,1)S(1)}, bf16[8,64,128]{2,1,0:T(8,128)(2,1)S(1)}, u32[]{:S(2)}, u32[]{:S(2)}) collective-permute-start(bf16[8,64,128]{2,1,0:T(8,128)(2,1)S(1)} %add.41), channel_id=1, source_target_pairs={{0,4},{1,5},{2,6},{3,7},{4,0},{5,1},{6,2},{7,3},{8,12},{9,13},{10,... | collective-permute-start | bytes 393224 | tf_op jit(solution)/shard_map/ppermute | solution.py:312
  408.9 0.8 copy-start.17
  409.8 70.8 %collective-permute-start.13 = (bf16[1,1024,512]{2,1,0:T(8,128)(2,1)}, bf16[1,1024,512]{2,1,0:T(8,128)(2,1)S(1)}, u32[]{:S(2)}, u32[]{:S(2)}) collective-permute-start(bf16[1,1024,512]{2,1,0:T(8,128)(2,1)} %get-tuple-element.33), channel_id=1, source_target_pairs={{0,4},{1,5},{2,6},{3,7},{4,0},{5,1},{6,2},{7,3},{8,12},{9,13},{10,... | collective-permute-start | bytes 3145736 | tf_op jit(solution)/shard_map/ppermute | solution.py:304
  411.0 69.6 %collective-permute-start.14 = (bf16[1,1024,512]{2,1,0:T(8,128)(2,1)S(1)}, bf16[1,1024,512]{2,1,0:T(8,128)(2,1)S(1)}, u32[]{:S(2)}, u32[]{:S(2)}) collective-permute-start(bf16[1,1024,512]{2,1,0:T(8,128)(2,1)S(1)} %copy-done.20), channel_id=1, source_target_pairs={{0,6},{1,7},{2,4},{3,5},{4,2},{5,3},{6,0},{7,1},{8,14},{9,15},{10,... | collective-permute-start | bytes 3145736 | tf_op jit(solution)/shard_map/ppermute | solution.py:304
  414.3 66.3 %collective-permute-start.16 = (bf16[1,1024,512]{2,1,0:T(8,128)(2,1)}, bf16[1,1024,512]{2,1,0:T(8,128)(2,1)S(1)}, u32[]{:S(2)}, u32[]{:S(2)}) collective-permute-start(bf16[1,1024,512]{2,1,0:T(8,128)(2,1)} %get-tuple-element.36), channel_id=1, source_target_pairs={{0,2},{1,3},{2,0},{3,1},{4,6},{5,7},{6,4},{7,5},{8,10},{9,11},{10,... | collective-permute-start | bytes 3145736 | tf_op jit(solution)/shard_map/ppermute | solution.py:304
  414.9 86.4 %collective-permute-start.17 = (bf16[1,1024,512]{2,1,0:T(8,128)(2,1)}, bf16[1,1024,512]{2,1,0:T(8,128)(2,1)S(1)}, u32[]{:S(2)}, u32[]{:S(2)}) collective-permute-start(bf16[1,1024,512]{2,1,0:T(8,128)(2,1)} %get-tuple-element.37), channel_id=1, source_target_pairs={{0,4},{1,5},{2,6},{3,7},{4,0},{5,1},{6,2},{7,3},{8,12},{9,13},{10,... | collective-permute-start | bytes 3145736 | tf_op jit(solution)/shard_map/ppermute | solution.py:304
  415.3 85.9 %copy-start.8 = (bf16[1,1024,512]{2,1,0:T(8,128)(2,1)}, bf16[1,1024,512]{2,1,0:T(8,128)(2,1)S(1)}, u32[]{:S(2)}) copy-start(bf16[1,1024,512]{2,1,0:T(8,128)(2,1)S(1)} %collective-permute-done.12.refs_1_) | copy-start | bytes 3145732
  415.3 85.9 %collective-permute-start.18 = (bf16[1,1024,512]{2,1,0:T(8,128)(2,1)}, bf16[1,1024,512]{2,1,0:T(8,128)(2,1)S(1)}, u32[]{:S(2)}, u32[]{:S(2)}) collective-permute-start(bf16[1,1024,512]{2,1,0:T(8,128)(2,1)} %get-tuple-element.38), channel_id=1, source_target_pairs={{0,6},{1,7},{2,4},{3,5},{4,2},{5,3},{6,0},{7,1},{8,14},{9,15},{10,... | collective-permute-start | bytes 3145736 | tf_op jit(solution)/shard_map/ppermute | solution.py:304
  480.6 20.7 %copy-start.9 = (bf16[1,1024,512]{2,1,0:T(8,128)(2,1)}, bf16[1,1024,512]{2,1,0:T(8,128)(2,1)S(1)}, u32[]{:S(2)}) copy-start(bf16[1,1024,512]{2,1,0:T(8,128)(2,1)S(1)} %collective-permute-done.13.refs_2_) | copy-start | bytes 3145732
  480.6 20.7 %copy-start.10 = (bf16[1,1024,512]{2,1,0:T(8,128)(2,1)}, bf16[1,1024,512]{2,1,0:T(8,128)(2,1)S(1)}, u32[]{:S(2)}) copy-start(bf16[1,1024,512]{2,1,0:T(8,128)(2,1)S(1)} %collective-permute-done.14.refs_3_) | copy-start | bytes 3145732
  480.6 20.7 %copy-start.11 = (bf16[1,1024,512]{2,1,0:T(8,128)(2,1)}, bf16[1,1024,512]{2,1,0:T(8,128)(2,1)S(1)}, u32[]{:S(2)}) copy-start(bf16[1,1024,512]{2,1,0:T(8,128)(2,1)S(1)} %collective-permute-done.16.refs_5_) | copy-start | bytes 3145732
  501.2 1.0 copy-start.12
  501.2 1.3 copy-start.13
  502.6 9.5 %copy-start.1 = (s32[32]{0:T(128)S(1)}, s32[32]{0:T(128)}, u32[]{:S(2)}) copy-start(s32[32]{0:T(128)} %param.12) | copy-start | bytes 388
  (2 other events, 1.6 us)

commit v2 on v0

v2 whole, which is shorter than its diff:
```python
import functools

import jax
import jax.numpy as jnp
from jax import lax
from jax.experimental import pallas as pl
from jax.experimental.pallas import tpu as pltpu
from jax.sharding import PartitionSpec as P

adapter_scale = 2.0
OWNER_CAP = 4
CHUNKS = 4
UP_GATE = 3
VMEM_LIMIT = 62 * 1024 * 1024


def params():
    return pltpu.CompilerParams(vmem_limit_bytes=VMEM_LIMIT)


def cost(flops, bytes_accessed):
    return pl.CostEstimate(flops=flops, bytes_accessed=bytes_accessed, transcendentals=0)


def after(value, *others):
    return lax.optimization_barrier((value, *others))[0]


def gemm_kernel(n_add, n_out, per_out, row_parts, order_ref, hidden_ref, weight_ref, *refs):
    adds, outs = refs[:n_add], refs[n_add:]
    part = hidden_ref.shape[0] // row_parts

    def products(out):
        for m in range(row_parts):
            span = pl.ds(m * part, part)
            value = jnp.dot(hidden_ref[span, :], weight_ref[...], preferred_element_type=jnp.float32)
            for add in adds:
                value = value + add[0, span, :].astype(jnp.float32)
            out[0, span, :] = value.astype(jnp.bfloat16)

    if n_out == 1:
        products(outs[0])
    else:
        for o in range(n_out):
            pl.when(pl.program_id(0) // per_out == o)(functools.partial(products, outs[o]))


def gemm(hidden, weight, order, width, n_cols, offset, tile, blocks_per_out, adds=()):
    tokens, depth = hidden.shape
    count = order.shape[0]
    tiles = n_cols // tile
    n_out = count // blocks_per_out
    per_out = blocks_per_out * tiles

    def weight_at(i, order_ref):
        return 0, (order_ref[i // tiles] * width + offset) // tile + i % tiles

    def add_at(i, order_ref):
        return i // tiles, 0, i % tiles

    def out_at(o, i, order_ref):
        own = jnp.clip(i - o * per_out, 0, per_out - 1)
        return own // tiles, 0, own % tiles

    row_parts = 4
    total = tokens * depth * n_cols * count
    outs = pl.pallas_call(
        functools.partial(gemm_kernel, len(adds), n_out, per_out, row_parts),
        out_shape=[jax.ShapeDtypeStruct((blocks_per_out, tokens, n_cols), jnp.bfloat16)] * n_out,
        grid_spec=pltpu.PrefetchScalarGridSpec(
            num_scalar_prefetch=1,
            grid=(count * tiles,),
            in_specs=[
                pl.BlockSpec((tokens, depth), lambda i, order_ref: (0, 0)),
                pl.BlockSpec((depth, tile), weight_at),
            ]
            + [pl.BlockSpec((1, tokens, tile), add_at)] * len(adds),
            out_specs=[pl.BlockSpec((1, tokens, tile), functools.partial(out_at, o)) for o in range(n_out)],
        ),
        compiler_params=params(),
        cost_estimate=cost(2 * total, 2 * (tokens * depth + count * n_cols * (depth + tokens))),
        name="base_products",
    )(order, hidden, weight, *adds)
    return outs


def route_kernel(per_owner, slot_ref, me_ref, own_ref, out_ref, sems):
    groups, tiles = slot_ref.shape
    me = me_ref[0]

    def each(act):
        for g in range(groups):
            seen = jnp.int32(0)
            for i in range(tiles):
                slot = slot_ref[g, i]
                mine = jnp.logical_and(slot // per_owner == me, jnp.logical_and(g != me, seen < OWNER_CAP))

                @pl.when(mine)
                def _(slot=slot, seen=seen, g=g, i=i):
                    act(pltpu.make_async_copy(own_ref.at[slot % per_owner], out_ref.at[g, seen], sems.at[g, i]))

                seen = seen + mine.astype(jnp.int32)

    each(lambda c: c.start())
    each(lambda c: c.wait())


def route(table, me, factor):
    per_owner, rank, width = factor.shape
    groups, tiles = table.shape
    return pl.pallas_call(
        functools.partial(route_kernel, per_owner),
        out_shape=jax.ShapeDtypeStruct((groups, OWNER_CAP, rank, width), factor.dtype),
        in_specs=[
            pl.BlockSpec(memory_space=pltpu.SMEM),
            pl.BlockSpec(memory_space=pltpu.SMEM),
            pl.BlockSpec(memory_space=pltpu.VMEM),
        ],
        out_specs=pl.BlockSpec(memory_space=pl.ANY),
        scratch_shapes=[pltpu.SemaphoreType.DMA((groups, tiles))],
        compiler_params=params(),
        cost_estimate=cost(0, 2 * (per_owner + groups * OWNER_CAP) * rank * width),
        name="adapters_to_send",
    )(table, me, factor)


def fetch(slot_ref, me, own_ref, got_ref, held, sems):
    per_owner, tiles = own_ref.shape[0], slot_ref.shape[1]
    for i in range(tiles):
        slot = slot_ref[me, i]
        owner = slot // per_owner
        place = jnp.int32(0)
        for k in range(i):
            place = place + (slot_ref[me, k] // per_owner == owner).astype(jnp.int32)

        @pl.when(owner == me)
        def _(i=i, slot=slot):
            pltpu.make_async_copy(own_ref.at[slot % per_owner], held.at[i], sems.at[i]).start()

        @pl.when(owner != me)
        def _(i=i, owner=owner, place=place):
            pltpu.make_async_copy(got_ref.at[owner, place], held.at[i], sems.at[i]).start()


def rank_kernel(slot_ref, me_ref, hidden_ref, own_ref, got_ref, out_ref, rows_ref, held, row_sems, sems):
    tiles = slot_ref.shape[1]
    rows = rows_ref.shape[1]

    def tile_copy(i):
        return pltpu.make_async_copy(hidden_ref.at[pl.ds(i * rows, rows)], rows_ref.at[i], row_sems.at[i])

    for i in range(tiles):
        tile_copy(i).start()
    fetch(slot_ref, me_ref[0], own_ref, got_ref, held, sems)
    for i in range(tiles):
        tile_copy(i).wait()
        pltpu.make_async_copy(own_ref.at[0], held.at[i], sems.at[i]).wait()
        out_ref[i] = lax.dot_general(
            held[i], rows_ref[i], (((1,), (1,)), ((), ())), preferred_element_type=jnp.float32
        ).astype(jnp.bfloat16)


def rank_values(table, me, hidden, own, got):
    _, rank, width = own.shape
    tiles = table.shape[1]
    rows = hidden.shape[0] // tiles
    return pl.pallas_call(
        rank_kernel,
        out_shape=jax.ShapeDtypeStruct((tiles, rank, rows), jnp.bfloat16),
        in_specs=[pl.BlockSpec(memory_space=pltpu.SMEM)] * 2 + [pl.BlockSpec(memory_space=pl.ANY)] * 3,
        out_specs=pl.BlockSpec(memory_space=pltpu.VMEM),
        scratch_shapes=[
            pltpu.VMEM((tiles, rows, width), jnp.bfloat16),
            pltpu.VMEM((tiles, rank, width), jnp.bfloat16),
            pltpu.SemaphoreType.DMA((tiles,)),
            pltpu.SemaphoreType.DMA((tiles,)),
        ],
        compiler_params=params(),
        cost_estimate=cost(2 * hidden.size * rank, 2 * (hidden.size + tiles * rank * width)),
        name="rank_values",
    )(table, me, hidden, own, got)


def sum_kernel(n_add, *refs):
    out_ref = refs[-1]
    width = out_ref.shape[1] * n_add // (len(refs) - 1)
    for c in range((len(refs) - 1) // n_add):
        adds = refs[c * n_add : (c + 1) * n_add]
        value = adds[0][0].astype(jnp.float32)
        for add in adds[1:]:
            value = value + add[0].astype(jnp.float32)
        out_ref[:, pl.ds(c * width, width)] = value


def sum_base(adds, parts):
    flat = [a for chunk in adds for a in chunk]
    _, tokens, n_cols = flat[0].shape
    rows = tokens // parts
    width = n_cols * len(adds)
    return pl.pallas_call(
        functools.partial(sum_kernel, len(adds[0])),
        out_shape=jax.ShapeDtypeStruct((tokens, width), jnp.float32),
        grid=(parts,),
        in_specs=[pl.BlockSpec((1, rows, n_cols), lambda i: (0, i, 0))] * len(flat),
        out_specs=pl.BlockSpec((rows, width), lambda i: (i, 0)),
        compiler_params=params(),
        cost_estimate=cost(tokens * n_cols * len(flat), tokens * (2 * n_cols * len(flat) + 4 * width)),
        name="base_sum",
    )(*flat)


def final_kernel(per_step, slot_ref, me_ref, base_ref, own_ref, got_ref, *refs):
    ranks, (out_ref, held, sems) = refs[:-3], refs[-3:]
    step = pl.program_id(0)
    rows = ranks[0].shape[2]

    @pl.when(step == 0)
    def _():
        fetch(slot_ref, me_ref[0], own_ref, got_ref, held, sems)

    for t in range(per_step):
        tile = step * per_step + t
        pltpu.make_async_copy(own_ref.at[0], held.at[tile], sems.at[tile]).wait()
        rank = ranks[0][t].astype(jnp.float32)
        for other in ranks[1:]:
            rank = rank + other[t].astype(jnp.float32)
        adapted = lax.dot_general(
            rank.astype(jnp.bfloat16), held[tile], (((0,), (0,)), ((), ())), preferred_element_type=jnp.float32
        )
        adapted = (adapter_scale * adapted).astype(jnp.bfloat16).astype(jnp.float32)
        span = pl.ds(t * rows, rows)
        out_ref[span, :] = (base_ref[span, :] + adapted).astype(jnp.bfloat16)


def final(table, me, ranks, base, own, got):
    _, rank, width = own.shape
    tiles, _, rows = ranks[0].shape
    per_step = 2
    return pl.pallas_call(
        functools.partial(final_kernel, per_step),
        out_shape=jax.ShapeDtypeStruct((tiles * rows, width), jnp.bfloat16),
        grid=(tiles // per_step,),
        in_specs=[
            pl.BlockSpec(memory_space=pltpu.SMEM),
            pl.BlockSpec(memory_space=pltpu.SMEM),
            pl.BlockSpec((per_step * rows, width), lambda i: (i, 0)),
            pl.BlockSpec(memory_space=pl.ANY),
            pl.BlockSpec(memory_space=pl.ANY),
        ]
        + [pl.BlockSpec((per_step, rank, rows), lambda i: (i, 0, 0))] * len(ranks),
        out_specs=pl.BlockSpec((per_step * rows, width), lambda i: (i, 0)),
        scratch_shapes=[
            pltpu.VMEM((tiles, rank, width), jnp.bfloat16),
            pltpu.SemaphoreType.DMA((tiles,)),
        ],
        compiler_params=params(),
        cost_estimate=cost(2 * tiles * rows * rank * width, 6 * tiles * rows * width),
        name="adapted_and_sum",
    )(table, me, base, own, got, *ranks)


def local(
    groups,
    n_tp,
    hidden,
    down_weight,
    adapter_down_factor,
    adapter_up_factor,
    row_tile_adapter,
    adapter_pool_slot,
):
    chips = n_tp // 2
    width = down_weight.shape[1] // n_tp
    chunks = max(1, min(CHUNKS, width // 128))
    n_cols = width // chunks
    tile = min(512, n_cols)
    grp, tp = lax.axis_index("grp"), lax.axis_index("tp")
    chip, core = tp // 2, tp % 2
    me = grp.reshape(1).astype(jnp.int32)

    table = adapter_pool_slot[row_tile_adapter].reshape(1, -1).astype(jnp.int32)
    step = 1
    while step < groups:
        other = lax.ppermute(table, "grp", [(g, g ^ step) for g in range(groups)])
        upper = (grp // step) % 2 == 1
        table = jnp.where(
            upper, jnp.concatenate([other, table]), jnp.concatenate([table, other])
        )
        step *= 2

    def send(v):
        return lax.all_to_all(v, "grp", 0, 0, tiled=True)

    down_out = route(table, me, adapter_down_factor)
    down_in = send(down_out)

    relative = jnp.array(list(range(1, chips)) + [0], jnp.int32)
    far_chips = (chip ^ relative).astype(jnp.int32)
    theirs, ours = far_chips * 2 + (1 - core), far_chips * 2 + core
    done = down_out
    others, adds = {}, []

    def first_core(c, *done):
        (first,) = gemm(hidden, down_weight, after(theirs, *done), width, n_cols, c * n_cols, tile, chips)
        others[c] = lax.ppermute(first, "tp", [(i, i ^ 1) for i in range(n_tp)])
        return first

    done = first_core(0, down_out)
    for c in range(chunks):
        earlier = adds[c - 2] if c >= 2 else []
        if c + 1 < chunks:
            done = first_core(c + 1, done, *earlier)
        sums = gemm(hidden, down_weight, after(ours, done, *earlier), width, n_cols, c * n_cols, tile, 1, (others[c],))
        done = sums[chips - 1]
        got = [
            lax.ppermute(sums[r - 1], "tp", [(i, i ^ (2 * r)) for i in range(n_tp)])
            for r in range(1, chips)
        ]
        adds.append([done] + got)
    up_out = route(after(table, done), me, adapter_up_factor)
    up_in = send(after(up_out, *sum(adds[:-2], []), *adds[-2][:UP_GATE]))

    ranks = rank_values(after(table, up_out), me, hidden, adapter_down_factor, down_in)
    ranks = ranks + lax.ppermute(ranks, "tp", [(i, i ^ 1) for i in range(n_tp)])
    ranks = [ranks] + [lax.ppermute(ranks, "tp", [(i, i ^ (2 * r)) for i in range(n_tp)]) for r in range(1, chips)]

    base = sum_base(adds, table.shape[1])
    return final(table, me, ranks, base, adapter_up_factor, up_in)


def solution(mesh):
    placed = (
        P("grp", "tp"),
        P("tp", None),
        P("grp", None, "tp"),
        P("grp", None, "tp"),
        P("grp"),
        P(),
    )
    return jax.shard_map(
        functools.partial(local, mesh.shape["grp"], mesh.shape["tp"]),
        mesh=mesh,
        in_specs=placed,
        out_specs=P("grp", "tp"),
        check_vma=False,
    )
```

time: 463 us -> 194 us (0.42)
  waiting for transfers between devices: 369 us -> 37.8 us
  Pallas kernels: 0 us -> 115 us
  matrix products: 57.5 us -> 0 us
  starting transfers between devices: 0.12 us -> 35.7 us
  local copies, waits for them, and re-layouts: 16.1 us -> 1.39 us
  between operations: 13.2 us -> 0.35 us
    all_gather x2 -> x0, waiting for transfers between devices: 206 us -> none  [the longest x1 186 us: local(): lax.all_gather(adapter_down_factor, 'grp', axis=0, tiled=True)]
    pallas_call x0 -> x13, Pallas kernels: none -> 115 us  [the longest x8 88.3 us: gemm(): pl.pallas_call(functools.partial(gemm_kernel, len(adds), n_out, per_out,...]
    reduce_scatter x1 -> x0, waiting for transfers between devices: 110 us -> none  [local(): lax.psum_scatter(lax.dot_general(down_weight, hidden, (((0,), (1,)), ((),...]
    dot_general x3 -> x0, matrix products: 57.5 us -> none  [the longest x1 50.5 us: local(): lax.dot_general(down_weight, hidden, (((0,), (1,)), ((), ())), preferred_...]
    psum x1 -> x0, waiting for transfers between devices: 51.7 us -> none  [local(): rank_projections = lax.psum(rank_part.astype(jnp.bfloat16), 'tp')]
    ppermute x0 -> x22, waiting for transfers between devices: none -> 35.1 us  [the longest x12 30.5 us: local(): lax.ppermute(sums[r - 1], 'tp', [(i, i ^ 2 * r) for i in range(n_tp)])]
    ppermute x0 -> x22, starting transfers between devices: none -> 26 us  [the longest x12 15.6 us: local(): lax.ppermute(sums[r - 1], 'tp', [(i, i ^ 2 * r) for i in range(n_tp)])]
    all_to_all x0 -> x2, starting transfers between devices: none -> 9.74 us  [send(): return lax.all_to_all(v, 'grp', 0, 0, tiled=True)]
  transfers between devices with their start and end apart: 4 -> 24, of which waited for: 4 -> 11; matrix products, arithmetic and copies ran while one was open for 16% -> 1% of each run, Pallas kernels for 0% -> 55%
where the time goes in v2:
time: 194 us; the launch traced here: 193 us
  Pallas kernels  115 us (59%)
  waiting for transfers between devices  37.8 us (19%)
  starting transfers between devices  35.7 us (18%)
  other arithmetic  2.8 us (1%)
    pallas_call x8, Pallas kernels, gemm(): pl.pallas_call(functools.partial(gemm_kernel, len(adds), n_out, per_out,...  88.3 us
    ppermute x12, waiting for transfers between devices, local(): lax.ppermute(sums[r - 1], 'tp', [(i, i ^ 2 * r) for i in range(n_tp)])  30.5 us
    ppermute x12, starting transfers between devices, local(): lax.ppermute(sums[r - 1], 'tp', [(i, i ^ 2 * r) for i in range(n_tp)])  15.6 us
    all_to_all x2, starting transfers between devices, send(): return lax.all_to_all(v, 'grp', 0, 0, tiled=True)  9.74 us
    pallas_call x1, Pallas kernels, sum_base(): pl.pallas_call(functools.partial(sum_kernel, len(adds[0])), out_shape=jax...  7.72 us
    pallas_call x1, Pallas kernels, rank_values(): pl.pallas_call(rank_kernel, out_shape=jax.ShapeDtypeStruct((tiles, rank,...  6.67 us
    pallas_call x1, Pallas kernels, final(): pl.pallas_call(functools.partial(final_kernel, per_step), out_shape=jax.S...  6.37 us
    ppermute x2, starting transfers between devices, local(): other = lax.ppermute(table, 'grp', [(g, g ^ step) for g in range(groups)])  6.18 us
  transfers between devices with their start and end apart: 24, of which 11 were waited for; matrix products, arithmetic and copies ran while one was open for 1% of the time, Pallas kernels for 55%

profile of v2, /device:TPU:0, one launch (start us, length us, event | category | flops | bytes accessed | tf_op | source)
XLA Modules:
  0.0 192.8 jit_solution(9538203912644711997)
XLA Ops:
  0.0 0.7 compare_select_fusion
  0.7 0.6 gather_fusion
  1.3 3.1 %collective-permute-start = (s32[1,8]{1,0:T(1,128)S(1)}, s32[1,8]{1,0:T(1,128)S(1)}, u32[]{:S(2)}, u32[]{:S(2)}) collective-permute-start(s32[1,8]{1,0:T(1,128)S(1)} %bitcast.2), channel_id=1, source_target_pairs={{0,8},{8,0},{16,24},{24,16},{1,9},{9,1},{17,25},{25,17},{2,10},{10... | collective-permute-start | bytes 104 | tf_op jit(solution)/shard_map/ppermute | solution.py:284
  4.4 1.5 collective-permute-done
  5.9 3.1 %collective-permute-start.1 = (s32[2,8]{1,0:T(2,128)S(1)}, s32[2,8]{1,0:T(2,128)S(1)}, u32[]{:S(2)}, u32[]{:S(2)}) collective-permute-start(s32[2,8]{1,0:T(2,128)S(1)} %add_select_fusion.1), channel_id=1, source_target_pairs={{0,16},{8,24},{16,0},{24,8},{1,17},{9,25},{17,1},{25,9},{2,18},{10... | collective-permute-start | bytes 200 | tf_op jit(solution)/shard_map/ppermute | solution.py:284
  9.0 1.5 collective-permute-done.1
  10.6 0.6 add_select_fusion.slot_ref
  11.2 3.2 %adapters_to_send.2 = bf16[4,4,64,2560]{3,2,1,0:T(8,128)(2,1)} custom-call(s32[4,8]{1,0:T(4,128)} %add_select_fusion.slot_ref, s32[1]{0:T(128)} %bitcast.1.me_ref, bf16[8,64,2560]{2,1,0:T(8,128)(2,1)} %own_ref.6), custom_call_target="tpu_custom_call" | custom-call | bytes 7864320 | tf_op jit(solution)/shard_map/adapters_to_send/pallas_call | solution.py:111
  14.5 5.3 %all-to-all-start.1 = ((bf16[4,4,64,2560]{3,2,1,0:T(8,128)(2,1)}), bf16[4,4,64,2560]{3,2,1,0:T(8,128)(2,1)}, u32[]{:S(2)}, u32[]{:S(2)}) async-start(bf16[4,4,64,2560]{3,2,1,0:T(8,128)(2,1)} %adapters_to_send.2), calls=%async_computation.1 | async-start | bytes 10485760 | tf_op jit(solution)/shard_map/all_to_all | solution.py:292
  19.7 0.6 fusion
  20.3 10.6 %base_products.8 = bf16[4,1024,256]{2,1,0:T(8,128)(2,1)} custom-call(s32[4]{0:T(128)} %get-tuple-element.45.order_ref, bf16[1024,2560]{1,0:T(8,128)(2,1)} %hidden_ref.17, bf16[2560,8192]{1,0:T(8,128)(2,1)} %weight_ref.15), custom_call_target="tpu_custom_call" | custom-call | flops 5368709120 | bytes 12582912 | tf_op jit(solution)/shard_map/base_products/pallas_call | solution.py:67
  30.9 10.6 %base_products.9 = bf16[4,1024,256]{2,1,0:T(8,128)(2,1)} custom-call(s32[4]{0:T(128)} %get-tuple-element.45.order_ref, bf16[1024,2560]{1,0:T(8,128)(2,1)} %hidden_ref.17, bf16[2560,8192]{1,0:T(8,128)(2,1)} %weight_ref.15), custom_call_target="tpu_custom_call" | custom-call | flops 5368709120 | bytes 12582912 | tf_op jit(solution)/shard_map/base_products/pallas_call | solution.py:67
  41.5 0.5 collective-permute-start.6
  42.1 11.4 %base_products.10 = (bf16[1,1024,256]{2,1,0:T(8,128)(2,1)}, bf16[1,1024,256]{2,1,0:T(8,128)(2,1)}, bf16[1,1024,256]{2,1,0:T(8,128)(2,1)}, bf16[1,1024,256]{2,1,0:T(8,128)(2,1)}) custom-call(s32[4]{0:T(128)} %get-tuple-element.51.order_ref, bf16[1024,2560]{1,0:T(8,128)(2,1)} %hidden_ref.17, bf16[2560,8192]{1,0:T(8,128)(2,1)} %weight_ref.15, ...), custom_call_target="tpu_custom_call" | custom-call | flops 5368709120 | bytes 12582912 | tf_op jit(solution)/shard_map/base_products/pallas_call | solution.py:67
  53.4 1.7 collective-permute-start.3
  55.1 1.5 collective-permute-start.4
  56.9 10.6 %base_products.11 = bf16[4,1024,256]{2,1,0:T(8,128)(2,1)} custom-call(s32[4]{0:T(128)} %get-tuple-element.45.order_ref, bf16[1024,2560]{1,0:T(8,128)(2,1)} %hidden_ref.17, bf16[2560,8192]{1,0:T(8,128)(2,1)} %weight_ref.15), custom_call_target="tpu_custom_call" | custom-call | flops 5368709120 | bytes 12582912 | tf_op jit(solution)/shard_map/base_products/pallas_call | solution.py:67
  67.6 11.4 %base_products.12 = (bf16[1,1024,256]{2,1,0:T(8,128)(2,1)}, bf16[1,1024,256]{2,1,0:T(8,128)(2,1)}, bf16[1,1024,256]{2,1,0:T(8,128)(2,1)}, bf16[1,1024,256]{2,1,0:T(8,128)(2,1)}) custom-call(s32[4]{0:T(128)} %get-tuple-element.51.order_ref, bf16[1024,2560]{1,0:T(8,128)(2,1)} %hidden_ref.17, bf16[2560,8192]{1,0:T(8,128)(2,1)} %weight_ref.15, ...), custom_call_target="tpu_custom_call" | custom-call | flops 5368709120 | bytes 12582912 | tf_op jit(solution)/shard_map/base_products/pallas_call | solution.py:67
  79.0 1.1 collective-permute-done.4.refs_2_
  80.1 10.6 %base_products.13 = bf16[4,1024,256]{2,1,0:T(8,128)(2,1)} custom-call(s32[4]{0:T(128)} %get-tuple-element.45.order_ref, bf16[1024,2560]{1,0:T(8,128)(2,1)} %hidden_ref.17, bf16[2560,8192]{1,0:T(8,128)(2,1)} %weight_ref.15), custom_call_target="tpu_custom_call" | custom-call | flops 5368709120 | bytes 12582912 | tf_op jit(solution)/shard_map/base_products/pallas_call | solution.py:67
  90.8 1.3 collective-permute-start.7
  92.1 1.3 collective-permute-start.8
  93.4 1.0 collective-permute-start.9
  94.4 11.6 %base_products.14 = (bf16[1,1024,256]{2,1,0:T(8,128)(2,1)}, bf16[1,1024,256]{2,1,0:T(8,128)(2,1)}, bf16[1,1024,256]{2,1,0:T(8,128)(2,1)}, bf16[1,1024,256]{2,1,0:T(8,128)(2,1)}) custom-call(s32[4]{0:T(128)} %get-tuple-element.51.order_ref, bf16[1024,2560]{1,0:T(8,128)(2,1)} %hidden_ref.17, bf16[2560,8192]{1,0:T(8,128)(2,1)} %weight_ref.15, ...), custom_call_target="tpu_custom_call" | custom-call | flops 5368709120 | bytes 12582912 | tf_op jit(solution)/shard_map/base_products/pallas_call | solution.py:67
  106.0 1.2 collective-permute-start.11
  107.2 1.3 collective-permute-start.12
  108.5 7.5 %collective-permute-done.8.refs_6_ = bf16[1,1024,256]{2,1,0:T(8,128)(2,1)S(1)} collective-permute-done((bf16[1,1024,256]{2,1,0:T(8,128)(2,1)}, bf16[1,1024,256]{2,1,0:T(8,128)(2,1)S(1)}, u32[]{:S(2)}, u32[]{:S(2)}) %collective-permute-start.8) | collective-permute-done | bytes 524320 | tf_op jit(solution)/shard_map/ppermute | solution.py:316
  116.1 2.0 %collective-permute-done.9.refs_7_ = bf16[1,1024,256]{2,1,0:T(8,128)(2,1)S(1)} collective-permute-done((bf16[1,1024,256]{2,1,0:T(8,128)(2,1)}, bf16[1,1024,256]{2,1,0:T(8,128)(2,1)S(1)}, u32[]{:S(2)}, u32[]{:S(2)}) %collective-permute-start.9) | collective-permute-done | bytes 524320 | tf_op jit(solution)/shard_map/ppermute | solution.py:316
  118.1 11.4 %base_products.15 = (bf16[1,1024,256]{2,1,0:T(8,128)(2,1)}, bf16[1,1024,256]{2,1,0:T(8,128)(2,1)}, bf16[1,1024,256]{2,1,0:T(8,128)(2,1)}, bf16[1,1024,256]{2,1,0:T(8,128)(2,1)}) custom-call(s32[4]{0:T(128)} %get-tuple-element.51.order_ref, bf16[1024,2560]{1,0:T(8,128)(2,1)} %hidden_ref.17, bf16[2560,8192]{1,0:T(8,128)(2,1)} %weight_ref.15, ...), custom_call_target="tpu_custom_call" | custom-call | flops 5368709120 | bytes 12582912 | tf_op jit(solution)/shard_map/base_products/pallas_call | solution.py:67
  129.5 2.4 %adapters_to_send.3 = bf16[4,4,64,1024]{3,2,1,0:T(8,128)(2,1)} custom-call(s32[4,8]{1,0:T(4,128)} %add_select_fusion.slot_ref, s32[1]{0:T(128)} %bitcast.1.me_ref, bf16[8,64,1024]{2,1,0:T(8,128)(2,1)} %own_ref.7), custom_call_target="tpu_custom_call" | custom-call | bytes 3145728 | tf_op jit(solution)/shard_map/adapters_to_send/pallas_call | solution.py:111
  132.0 1.5 all-to-all-done.1.got_ref
  133.5 4.5 %all-to-all-start = ((bf16[4,4,64,1024]{3,2,1,0:T(8,128)(2,1)}), bf16[4,4,64,1024]{3,2,1,0:T(8,128)(2,1)}, u32[]{:S(2)}, u32[]{:S(2)}) async-start(bf16[4,4,64,1024]{3,2,1,0:T(8,128)(2,1)} %adapters_to_send.3), calls=%async_computation | async-start | bytes 4194304 | tf_op jit(solution)/shard_map/all_to_all | solution.py:292
  137.9 2.6 %collective-permute-start.13 = (bf16[1,1024,256]{2,1,0:T(8,128)(2,1)}, bf16[1,1024,256]{2,1,0:T(8,128)(2,1)S(1)}, u32[]{:S(2)}, u32[]{:S(2)}) collective-permute-start(bf16[1,1024,256]{2,1,0:T(8,128)(2,1)} %get-tuple-element.50), channel_id=1, source_target_pairs={{0,6},{1,7},{2,4},{3,5},{4,2},{5,3},{6,0},{7,1},{8,14},{9,15},{10,... | collective-permute-start | bytes 1572872 | tf_op jit(solution)/shard_map/ppermute | solution.py:316
  140.5 0.5 collective-permute-start.15
  141.0 0.5 collective-permute-start.16
  141.5 2.5 %collective-permute-start.17 = (bf16[1,1024,256]{2,1,0:T(8,128)(2,1)}, bf16[1,1024,256]{2,1,0:T(8,128)(2,1)}, u32[]{:S(2)}, u32[]{:S(2)}) collective-permute-start(bf16[1,1024,256]{2,1,0:T(8,128)(2,1)} %get-tuple-element.55), channel_id=1, source_target_pairs={{0,6},{1,7},{2,4},{3,5},{4,2},{5,3},{6,0},{7,1},{8,14},{9,15},{10,... | collective-permute-start | bytes 1572872 | tf_op jit(solution)/shard_map/ppermute | solution.py:316
  144.0 6.7 %rank_values.1 = bf16[8,64,128]{2,1,0:T(8,128)(2,1)} custom-call(s32[4,8]{1,0:T(4,128)} %add_select_fusion.slot_ref, s32[1]{0:T(128)} %bitcast.1.me_ref, bf16[1024,2560]{1,0:T(8,128)(2,1)} %hidden_ref.17, bf16[8,64,2560]{2,1,0:T(8,128)(2,1)} %own_ref.6, bf16[4,4,64,2560]{3,2,1,0:T(8,128)(2,1)} %all-to-all-done.1.got_ref), custom_call_target="tpu_custom_call" | custom-call | flops 335544320 | bytes 7864320 | tf_op jit(solution)/shard_map/rank_values/pallas_call | solution.py:167
  150.8 1.5 collective-permute-done.18
  152.3 0.9 add.39.refs_0_
  153.3 0.5 collective-permute-start.21
  154.0 1.6 collective-permute-start.20
  155.6 9.8 %collective-permute-done.15.refs_13_ = bf16[1,1024,256]{2,1,0:T(8,128)(2,1)S(1)} collective-permute-done((bf16[1,1024,256]{2,1,0:T(8,128)(2,1)}, bf16[1,1024,256]{2,1,0:T(8,128)(2,1)S(1)}, u32[]{:S(2)}, u32[]{:S(2)}) %collective-permute-start.15) | collective-permute-done | bytes 524320 | tf_op jit(solution)/shard_map/ppermute | solution.py:316
  165.4 1.5 collective-permute-start.19
  166.9 9.8 %collective-permute-done.17.refs_15_ = bf16[1,1024,256]{2,1,0:T(8,128)(2,1)} collective-permute-done((bf16[1,1024,256]{2,1,0:T(8,128)(2,1)}, bf16[1,1024,256]{2,1,0:T(8,128)(2,1)}, u32[]{:S(2)}, u32[]{:S(2)}) %collective-permute-start.17) | collective-permute-done | bytes 524320 | tf_op jit(solution)/shard_map/ppermute | solution.py:316
  176.7 7.7 %base_sum.1.base_ref = f32[1024,1024]{1,0:T(8,128)} custom-call(bf16[1,1024,256]{2,1,0:T(8,128)(2,1)} %get-tuple-element.35.refs_0_, bf16[1,1024,256]{2,1,0:T(8,128)(2,1)} %copy-done.3, bf16[1,1024,256]{2,1,0:T(8,128)(2,1)} %copy-done.4, bf16[1,1024,256]{2,1,0:T(8,128)(2,1)} %copy-done.5, bf16[1,1024,256]{2,1,0:T(8,128)(2,1)} %get-tuple-element.41.refs_4_, ...), custom_call_target="tpu_custom_call" | custom-call | flops 4194304 | bytes 12582912 | tf_op jit(solution)/shard_map/base_sum/pallas_call | solution.py:200
  184.4 1.1 all-to-all-done.got_ref
  185.5 0.6 copy-done.12
  186.2 6.4 %adapted_and_sum.1 = bf16[1024,1024]{1,0:T(8,128)(2,1)} custom-call(s32[4,8]{1,0:T(4,128)} %add_select_fusion.slot_ref, s32[1]{0:T(128)} %bitcast.1.me_ref, f32[1024,1024]{1,0:T(8,128)} %base_sum.1.base_ref, bf16[8,64,1024]{2,1,0:T(8,128)(2,1)} %own_ref.7, bf16[4,4,64,1024]{3,2,1,0:T(8,128)(2,1)} %all-to-all-done.got_ref, bf16[8,64,128]{2,1,0:T(8,128)(2,1)} %copy-done.2, ...), custom_call_target="tpu_custom_call" | custom-call | flops 134217728 | bytes 6291456 | tf_op jit(solution)/shard_map/adapted_and_sum/pallas_call | solution.py:239
  (50 shorter events, 0.9 us)
Async XLA Ops:
  0.0 0.7 copy-start
  1.3 4.6 %collective-permute-start = (s32[1,8]{1,0:T(1,128)S(1)}, s32[1,8]{1,0:T(1,128)S(1)}, u32[]{:S(2)}, u32[]{:S(2)}) collective-permute-start(s32[1,8]{1,0:T(1,128)S(1)} %bitcast.2), channel_id=1, source_target_pairs={{0,8},{8,0},{16,24},{24,16},{1,9},{9,1},{17,25},{25,17},{2,10},{10... | collective-permute-start | bytes 104 | tf_op jit(solution)/shard_map/ppermute | solution.py:284
  5.9 4.6 %collective-permute-start.1 = (s32[2,8]{1,0:T(2,128)S(1)}, s32[2,8]{1,0:T(2,128)S(1)}, u32[]{:S(2)}, u32[]{:S(2)}) collective-permute-start(s32[2,8]{1,0:T(2,128)S(1)} %add_select_fusion.1), channel_id=1, source_target_pairs={{0,16},{8,24},{16,0},{24,8},{1,17},{9,25},{17,1},{25,9},{2,18},{10... | collective-permute-start | bytes 200 | tf_op jit(solution)/shard_map/ppermute | solution.py:284
  14.4 5.3 %copy-start.14 = (s32[4]{0:T(128)S(1)}, s32[4]{0:T(128)}, u32[]{:S(2)}) copy-start(s32[4]{0:T(128)} %constant.62.clone) | copy-start | bytes 52
  14.5 119.0 %all-to-all-start.1 = ((bf16[4,4,64,2560]{3,2,1,0:T(8,128)(2,1)}), bf16[4,4,64,2560]{3,2,1,0:T(8,128)(2,1)}, u32[]{:S(2)}, u32[]{:S(2)}) async-start(bf16[4,4,64,2560]{3,2,1,0:T(8,128)(2,1)} %adapters_to_send.2), calls=%async_computation.1 | async-start | bytes 10485760 | tf_op jit(solution)/shard_map/all_to_all | solution.py:292
  30.9 11.1 %collective-permute-start.2 = (bf16[4,1024,256]{2,1,0:T(8,128)(2,1)}, bf16[4,1024,256]{2,1,0:T(8,128)(2,1)}, u32[]{:S(2)}, u32[]{:S(2)}) collective-permute-start(bf16[4,1024,256]{2,1,0:T(8,128)(2,1)} %base_products.8), channel_id=1, source_target_pairs={{0,1},{1,0},{2,3},{3,2},{4,5},{5,4},{6,7},{7,6},{8,9},{9,8},{10,11... | collective-permute-start | bytes 6291464 | tf_op jit(solution)/shard_map/ppermute | solution.py:305
  41.5 26.0 %collective-permute-start.6 = (bf16[4,1024,256]{2,1,0:T(8,128)(2,1)}, bf16[4,1024,256]{2,1,0:T(8,128)(2,1)}, u32[]{:S(2)}, u32[]{:S(2)}) collective-permute-start(bf16[4,1024,256]{2,1,0:T(8,128)(2,1)} %base_products.9), channel_id=1, source_target_pairs={{0,1},{1,0},{2,3},{3,2},{4,5},{5,4},{6,7},{7,6},{8,9},{9,8},{10,11... | collective-permute-start | bytes 6291464 | tf_op jit(solution)/shard_map/ppermute | solution.py:305
  53.4 25.5 %collective-permute-start.3 = (bf16[1,1024,256]{2,1,0:T(8,128)(2,1)}, bf16[1,1024,256]{2,1,0:T(8,128)(2,1)S(1)}, u32[]{:S(2)}, u32[]{:S(2)}) collective-permute-start(bf16[1,1024,256]{2,1,0:T(8,128)(2,1)} %get-tuple-element.36), channel_id=1, source_target_pairs={{0,2},{1,3},{2,0},{3,1},{4,6},{5,7},{6,4},{7,5},{8,10},{9,11},{10,... | collective-permute-start | bytes 1572872 | tf_op jit(solution)/shard_map/ppermute | solution.py:316
  55.1 25.0 %collective-permute-start.4 = (bf16[1,1024,256]{2,1,0:T(8,128)(2,1)}, bf16[1,1024,256]{2,1,0:T(8,128)(2,1)S(1)}, u32[]{:S(2)}, u32[]{:S(2)}) collective-permute-start(bf16[1,1024,256]{2,1,0:T(8,128)(2,1)} %get-tuple-element.37), channel_id=1, source_target_pairs={{0,4},{1,5},{2,6},{3,7},{4,0},{5,1},{6,2},{7,3},{8,12},{9,13},{10,... | collective-permute-start | bytes 1572872 | tf_op jit(solution)/shard_map/ppermute | solution.py:316
  56.6 23.5 %collective-permute-start.5 = (bf16[1,1024,256]{2,1,0:T(8,128)(2,1)}, bf16[1,1024,256]{2,1,0:T(8,128)(2,1)S(1)}, u32[]{:S(2)}, u32[]{:S(2)}) collective-permute-start(bf16[1,1024,256]{2,1,0:T(8,128)(2,1)} %get-tuple-element.38), channel_id=1, source_target_pairs={{0,6},{1,7},{2,4},{3,5},{4,2},{5,3},{6,0},{7,1},{8,14},{9,15},{10,... | collective-permute-start | bytes 1572872 | tf_op jit(solution)/shard_map/ppermute | solution.py:316
  67.5 26.9 %collective-permute-start.10 = (bf16[4,1024,256]{2,1,0:T(8,128)(2,1)}, bf16[4,1024,256]{2,1,0:T(8,128)(2,1)}, u32[]{:S(2)}, u32[]{:S(2)}) collective-permute-start(bf16[4,1024,256]{2,1,0:T(8,128)(2,1)} %base_products.11), channel_id=1, source_target_pairs={{0,1},{1,0},{2,3},{3,2},{4,5},{5,4},{6,7},{7,6},{8,9},{9,8},{10,11... | collective-permute-start | bytes 6291464 | tf_op jit(solution)/shard_map/ppermute | solution.py:305
  79.0 11.8 %copy-start.3 = (bf16[1,1024,256]{2,1,0:T(8,128)(2,1)}, bf16[1,1024,256]{2,1,0:T(8,128)(2,1)S(1)}, u32[]{:S(2)}) copy-start(bf16[1,1024,256]{2,1,0:T(8,128)(2,1)S(1)} %collective-permute-done.3.refs_1_) | copy-start | bytes 1572868
  80.1 10.6 %copy-start.4 = (bf16[1,1024,256]{2,1,0:T(8,128)(2,1)}, bf16[1,1024,256]{2,1,0:T(8,128)(2,1)S(1)}, u32[]{:S(2)}) copy-start(bf16[1,1024,256]{2,1,0:T(8,128)(2,1)S(1)} %collective-permute-done.4.refs_2_) | copy-start | bytes 1572868
  80.1 10.6 %copy-start.5 = (bf16[1,1024,256]{2,1,0:T(8,128)(2,1)}, bf16[1,1024,256]{2,1,0:T(8,128)(2,1)S(1)}, u32[]{:S(2)}) copy-start(bf16[1,1024,256]{2,1,0:T(8,128)(2,1)S(1)} %collective-permute-done.5.refs_3_) | copy-start | bytes 1572868
  90.8 27.3 %collective-permute-start.14 = (bf16[4,1024,256]{2,1,0:T(8,128)(2,1)}, bf16[4,1024,256]{2,1,0:T(8,128)(2,1)}, u32[]{:S(2)}, u32[]{:S(2)}) collective-permute-start(bf16[4,1024,256]{2,1,0:T(8,128)(2,1)} %base_products.13), channel_id=1, source_target_pairs={{0,1},{1,0},{2,3},{3,2},{4,5},{5,4},{6,7},{7,6},{8,9},{9,8},{10,11... | collective-permute-start | bytes 6291464 | tf_op jit(solution)/shard_map/ppermute | solution.py:305
  90.8 16.4 %collective-permute-start.7 = (bf16[1,1024,256]{2,1,0:T(8,128)(2,1)}, bf16[1,1024,256]{2,1,0:T(8,128)(2,1)S(1)}, u32[]{:S(2)}, u32[]{:S(2)}) collective-permute-start(bf16[1,1024,256]{2,1,0:T(8,128)(2,1)} %get-tuple-element.42), channel_id=1, source_target_pairs={{0,2},{1,3},{2,0},{3,1},{4,6},{5,7},{6,4},{7,5},{8,10},{9,11},{10,... | collective-permute-start | bytes 1572872 | tf_op jit(solution)/shard_map/ppermute | solution.py:316
  92.1 23.9 %collective-permute-start.8 = (bf16[1,1024,256]{2,1,0:T(8,128)(2,1)}, bf16[1,1024,256]{2,1,0:T(8,128)(2,1)S(1)}, u32[]{:S(2)}, u32[]{:S(2)}) collective-permute-start(bf16[1,1024,256]{2,1,0:T(8,128)(2,1)} %get-tuple-element.43), channel_id=1, source_target_pairs={{0,4},{1,5},{2,6},{3,7},{4,0},{5,1},{6,2},{7,3},{8,12},{9,13},{10,... | collective-permute-start | bytes 1572872 | tf_op jit(solution)/shard_map/ppermute | solution.py:316
  93.4 24.6 %collective-permute-start.9 = (bf16[1,1024,256]{2,1,0:T(8,128)(2,1)}, bf16[1,1024,256]{2,1,0:T(8,128)(2,1)S(1)}, u32[]{:S(2)}, u32[]{:S(2)}) collective-permute-start(bf16[1,1024,256]{2,1,0:T(8,128)(2,1)} %get-tuple-element.44), channel_id=1, source_target_pairs={{0,6},{1,7},{2,4},{3,5},{4,2},{5,3},{6,0},{7,1},{8,14},{9,15},{10,... | collective-permute-start | bytes 1572872 | tf_op jit(solution)/shard_map/ppermute | solution.py:316
  106.0 26.0 %collective-permute-start.11 = (bf16[1,1024,256]{2,1,0:T(8,128)(2,1)}, bf16[1,1024,256]{2,1,0:T(8,128)(2,1)}, u32[]{:S(2)}, u32[]{:S(2)}) collective-permute-start(bf16[1,1024,256]{2,1,0:T(8,128)(2,1)} %get-tuple-element.48), channel_id=1, source_target_pairs={{0,2},{1,3},{2,0},{3,1},{4,6},{5,7},{6,4},{7,5},{8,10},{9,11},{10,... | collective-permute-start | bytes 1572872 | tf_op jit(solution)/shard_map/ppermute | solution.py:316
  107.2 22.3 %copy-start.6 = (bf16[1,1024,256]{2,1,0:T(8,128)(2,1)}, bf16[1,1024,256]{2,1,0:T(8,128)(2,1)S(1)}, u32[]{:S(2)}) copy-start(bf16[1,1024,256]{2,1,0:T(8,128)(2,1)S(1)} %collective-permute-done.7.refs_5_) | copy-start | bytes 1572868
  107.2 24.8 %collective-permute-start.12 = (bf16[1,1024,256]{2,1,0:T(8,128)(2,1)}, bf16[1,1024,256]{2,1,0:T(8,128)(2,1)}, u32[]{:S(2)}, u32[]{:S(2)}) collective-permute-start(bf16[1,1024,256]{2,1,0:T(8,128)(2,1)} %get-tuple-element.49), channel_id=1, source_target_pairs={{0,4},{1,5},{2,6},{3,7},{4,0},{5,1},{6,2},{7,3},{8,12},{9,13},{10,... | collective-permute-start | bytes 1572872 | tf_op jit(solution)/shard_map/ppermute | solution.py:316
  116.1 13.5 %copy-start.7 = (bf16[1,1024,256]{2,1,0:T(8,128)(2,1)}, bf16[1,1024,256]{2,1,0:T(8,128)(2,1)S(1)}, u32[]{:S(2)}) copy-start(bf16[1,1024,256]{2,1,0:T(8,128)(2,1)S(1)} %collective-permute-done.8.refs_6_) | copy-start | bytes 1572868
  118.1 11.5 %copy-start.8 = (bf16[1,1024,256]{2,1,0:T(8,128)(2,1)}, bf16[1,1024,256]{2,1,0:T(8,128)(2,1)S(1)}, u32[]{:S(2)}) copy-start(bf16[1,1024,256]{2,1,0:T(8,128)(2,1)S(1)} %collective-permute-done.9.refs_7_) | copy-start | bytes 1572868
  133.5 52.0 %all-to-all-start = ((bf16[4,4,64,1024]{3,2,1,0:T(8,128)(2,1)}), bf16[4,4,64,1024]{3,2,1,0:T(8,128)(2,1)}, u32[]{:S(2)}, u32[]{:S(2)}) async-start(bf16[4,4,64,1024]{3,2,1,0:T(8,128)(2,1)} %adapters_to_send.3), calls=%async_computation | async-start | bytes 4194304 | tf_op jit(solution)/shard_map/all_to_all | solution.py:292
  137.9 16.1 %collective-permute-start.13 = (bf16[1,1024,256]{2,1,0:T(8,128)(2,1)}, bf16[1,1024,256]{2,1,0:T(8,128)(2,1)S(1)}, u32[]{:S(2)}, u32[]{:S(2)}) collective-permute-start(bf16[1,1024,256]{2,1,0:T(8,128)(2,1)} %get-tuple-element.50), channel_id=1, source_target_pairs={{0,6},{1,7},{2,4},{3,5},{4,2},{5,3},{6,0},{7,1},{8,14},{9,15},{10,... | collective-permute-start | bytes 1572872 | tf_op jit(solution)/shard_map/ppermute | solution.py:316
  140.5 24.8 %collective-permute-start.15 = (bf16[1,1024,256]{2,1,0:T(8,128)(2,1)}, bf16[1,1024,256]{2,1,0:T(8,128)(2,1)S(1)}, u32[]{:S(2)}, u32[]{:S(2)}) collective-permute-start(bf16[1,1024,256]{2,1,0:T(8,128)(2,1)} %get-tuple-element.53), channel_id=1, source_target_pairs={{0,2},{1,3},{2,0},{3,1},{4,6},{5,7},{6,4},{7,5},{8,10},{9,11},{10,... | collective-permute-start | bytes 1572872 | tf_op jit(solution)/shard_map/ppermute | solution.py:316
  141.0 25.8 %collective-permute-start.16 = (bf16[1,1024,256]{2,1,0:T(8,128)(2,1)}, bf16[1,1024,256]{2,1,0:T(8,128)(2,1)S(1)}, u32[]{:S(2)}, u32[]{:S(2)}) collective-permute-start(bf16[1,1024,256]{2,1,0:T(8,128)(2,1)} %get-tuple-element.54), channel_id=1, source_target_pairs={{0,4},{1,5},{2,6},{3,7},{4,0},{5,1},{6,2},{7,3},{8,12},{9,13},{10,... | collective-permute-start | bytes 1572872 | tf_op jit(solution)/shard_map/ppermute | solution.py:316
  141.5 35.1 %collective-permute-start.17 = (bf16[1,1024,256]{2,1,0:T(8,128)(2,1)}, bf16[1,1024,256]{2,1,0:T(8,128)(2,1)}, u32[]{:S(2)}, u32[]{:S(2)}) collective-permute-start(bf16[1,1024,256]{2,1,0:T(8,128)(2,1)} %get-tuple-element.55), channel_id=1, source_target_pairs={{0,6},{1,7},{2,4},{3,5},{4,2},{5,3},{6,0},{7,1},{8,14},{9,15},{10,... | collective-permute-start | bytes 1572872 | tf_op jit(solution)/shard_map/ppermute | solution.py:316
  150.7 1.6 collective-permute-start.18
  153.2 31.1 %copy-start.2 = (bf16[8,64,128]{2,1,0:T(8,128)(2,1)}, bf16[8,64,128]{2,1,0:T(8,128)(2,1)S(1)}, u32[]{:S(2)}) copy-start(bf16[8,64,128]{2,1,0:T(8,128)(2,1)S(1)} %add.39.refs_0_) | copy-start | bytes 393220
  153.3 32.3 %collective-permute-start.21 = (bf16[8,64,128]{2,1,0:T(8,128)(2,1)S(1)}, bf16[8,64,128]{2,1,0:T(8,128)(2,1)S(1)}, u32[]{:S(2)}, u32[]{:S(2)}) collective-permute-start(bf16[8,64,128]{2,1,0:T(8,128)(2,1)S(1)} %add.39.refs_0_), channel_id=1, source_target_pairs={{0,6},{1,7},{2,4},{3,5},{4,2},{5,3},{6,0},{7,1},{8,14},{9,15},{10,... | collective-permute-start | bytes 393224 | tf_op jit(solution)/shard_map/ppermute | solution.py:325
  154.0 22.6 %copy-start.9 = (bf16[1,1024,256]{2,1,0:T(8,128)(2,1)}, bf16[1,1024,256]{2,1,0:T(8,128)(2,1)S(1)}, u32[]{:S(2)}) copy-start(bf16[1,1024,256]{2,1,0:T(8,128)(2,1)S(1)} %collective-permute-done.13.refs_11_) | copy-start | bytes 1572868
  154.0 31.5 %collective-permute-start.20 = (bf16[8,64,128]{2,1,0:T(8,128)(2,1)S(1)}, bf16[8,64,128]{2,1,0:T(8,128)(2,1)S(1)}, u32[]{:S(2)}, u32[]{:S(2)}) collective-permute-start(bf16[8,64,128]{2,1,0:T(8,128)(2,1)S(1)} %add.39.refs_0_), channel_id=1, source_target_pairs={{0,4},{1,5},{2,6},{3,7},{4,0},{5,1},{6,2},{7,3},{8,12},{9,13},{10,... | collective-permute-start | bytes 393224 | tf_op jit(solution)/shard_map/ppermute | solution.py:325
  165.4 11.3 %copy-start.10 = (bf16[1,1024,256]{2,1,0:T(8,128)(2,1)}, bf16[1,1024,256]{2,1,0:T(8,128)(2,1)S(1)}, u32[]{:S(2)}) copy-start(bf16[1,1024,256]{2,1,0:T(8,128)(2,1)S(1)} %collective-permute-done.15.refs_13_) | copy-start | bytes 1572868
  165.4 20.2 %collective-permute-start.19 = (bf16[8,64,128]{2,1,0:T(8,128)(2,1)S(1)}, bf16[8,64,128]{2,1,0:T(8,128)(2,1)}, u32[]{:S(2)}, u32[]{:S(2)}) collective-permute-start(bf16[8,64,128]{2,1,0:T(8,128)(2,1)S(1)} %add.39.refs_0_), channel_id=1, source_target_pairs={{0,2},{1,3},{2,0},{3,1},{4,6},{5,7},{6,4},{7,5},{8,10},{9,11},{10,... | collective-permute-start | bytes 393224 | tf_op jit(solution)/shard_map/ppermute | solution.py:325
  166.9 9.8 %copy-start.11 = (bf16[1,1024,256]{2,1,0:T(8,128)(2,1)}, bf16[1,1024,256]{2,1,0:T(8,128)(2,1)S(1)}, u32[]{:S(2)}) copy-start(bf16[1,1024,256]{2,1,0:T(8,128)(2,1)S(1)} %collective-permute-done.16.refs_14_) | copy-start | bytes 1572868
  185.5 0.6 copy-start.12
  185.5 0.7 copy-start.13
  186.2 6.4 %copy-start.1 = (s32[32]{0:T(128)S(1)}, s32[32]{0:T(128)}, u32[]{:S(2)}) copy-start(s32[32]{0:T(128)} %param.12) | copy-start | bytes 388

commit v3 on v2

v3 whole, which is shorter than its diff:
```python
import functools

import jax
import jax.numpy as jnp
from jax import lax
from jax.experimental import pallas as pl
from jax.experimental.pallas import tpu as pltpu
from jax.sharding import PartitionSpec as P

adapter_scale = 2.0
OWNER_CAP = 4
CHUNKS = 4
UP_GATE = 3


def params(mib):
    return pltpu.CompilerParams(vmem_limit_bytes=mib * 1024 * 1024)


def cost(flops, bytes_accessed):
    return pl.CostEstimate(flops=flops, bytes_accessed=bytes_accessed, transcendentals=0)


def after(value, *others):
    return lax.optimization_barrier((value, *others))[0]


def gemm_kernel(n_add, n_out, per_out, row_parts, order_ref, hidden_ref, weight_ref, *refs):
    adds, outs = refs[:n_add], refs[n_add:]
    part = hidden_ref.shape[0] // row_parts

    def products(out):
        for m in range(row_parts):
            span = pl.ds(m * part, part)
            value = jnp.dot(hidden_ref[span, :], weight_ref[...], preferred_element_type=jnp.float32)
            for add in adds:
                value = value + add[0, span, :].astype(jnp.float32)
            out[0, span, :] = value.astype(jnp.bfloat16)

    if n_out == 1:
        products(outs[0])
    else:
        for o in range(n_out):
            pl.when(pl.program_id(0) // per_out == o)(functools.partial(products, outs[o]))


def gemm(hidden, weight, order, width, n_cols, offset, tile, blocks_per_out, adds=()):
    tokens, depth = hidden.shape
    count = order.shape[0]
    tiles = n_cols // tile
    n_out = count // blocks_per_out
    per_out = blocks_per_out * tiles

    def weight_at(i, order_ref):
        return 0, (order_ref[i // tiles] * width + offset) // tile + i % tiles

    def add_at(i, order_ref):
        return i // tiles, 0, i % tiles

    def out_at(o, i, order_ref):
        own = jnp.clip(i - o * per_out, 0, per_out - 1)
        return own // tiles, 0, own % tiles

    row_parts = 4
    total = tokens * depth * n_cols * count
    outs = pl.pallas_call(
        functools.partial(gemm_kernel, len(adds), n_out, per_out, row_parts),
        out_shape=[jax.ShapeDtypeStruct((blocks_per_out, tokens, n_cols), jnp.bfloat16)] * n_out,
        grid_spec=pltpu.PrefetchScalarGridSpec(
            num_scalar_prefetch=1,
            grid=(count * tiles,),
            in_specs=[
                pl.BlockSpec((tokens, depth), lambda i, order_ref: (0, 0), pipeline_mode=pl.Buffered(1)),
                pl.BlockSpec((depth, tile), weight_at),
            ]
            + [pl.BlockSpec((1, tokens, tile), add_at)] * len(adds),
            out_specs=[pl.BlockSpec((1, tokens, tile), functools.partial(out_at, o)) for o in range(n_out)],
        ),
        compiler_params=params(32),
        cost_estimate=cost(2 * total, 2 * (tokens * depth + count * n_cols * (depth + tokens))),
        name="base_products",
    )(order, hidden, weight, *adds)
    return outs


def route_kernel(per_owner, me_ref, pool_ref, *refs):
    tables, (own_ref, out_ref, sems) = refs[:-3], refs[-3:]
    tiles = tables[0].shape[1]
    me = me_ref[0]

    def each(act):
        for r, table in enumerate(tables, 1):
            seen = jnp.int32(0)
            for i in range(tiles):
                slot = pool_ref[table[0, i]]
                mine = jnp.logical_and(slot // per_owner == me, seen < OWNER_CAP)

                @pl.when(mine)
                def _(slot=slot, seen=seen, r=r, i=i):
                    act(pltpu.make_async_copy(own_ref.at[slot % per_owner], out_ref.at[me ^ r, seen], sems.at[r - 1, i]))

                seen = seen + mine.astype(jnp.int32)

    each(lambda c: c.start())
    each(lambda c: c.wait())


def route(me, pool, tables, factor):
    per_owner, rank, width = factor.shape
    groups = len(tables) + 1
    return pl.pallas_call(
        functools.partial(route_kernel, per_owner),
        out_shape=jax.ShapeDtypeStruct((groups, OWNER_CAP, rank, width), factor.dtype),
        in_specs=[pl.BlockSpec(memory_space=pltpu.SMEM)] * (groups + 1) + [pl.BlockSpec(memory_space=pltpu.VMEM)],
        out_specs=pl.BlockSpec(memory_space=pl.ANY),
        scratch_shapes=[pltpu.SemaphoreType.DMA((groups - 1, tables[0].shape[1]))],
        compiler_params=params(62),
        cost_estimate=cost(0, 2 * (per_owner + groups * OWNER_CAP) * rank * width),
        name="adapters_to_send",
    )(me, pool, *tables, factor)


def fetch(me_ref, pool_ref, own_table, own_ref, got_ref, held, sems):
    per_owner, tiles = own_ref.shape[0], own_table.shape[1]
    slots = [pool_ref[own_table[0, i]] for i in range(tiles)]
    me = me_ref[0]
    for i in range(tiles):
        owner = slots[i] // per_owner
        place = jnp.int32(0)
        for k in range(i):
            place = place + (slots[k] // per_owner == owner).astype(jnp.int32)

        @pl.when(owner == me)
        def _(i=i):
            pltpu.make_async_copy(own_ref.at[slots[i] % per_owner], held.at[i], sems.at[i]).start()

        @pl.when(owner != me)
        def _(i=i, owner=owner, place=place):
            pltpu.make_async_copy(got_ref.at[owner, place], held.at[i], sems.at[i]).start()


def rank_kernel(me_ref, pool_ref, own_table, hidden_ref, own_ref, got_ref, out_ref, rows_ref, held, row_sems, sems):
    tiles = own_table.shape[1]
    rows = rows_ref.shape[1]

    def tile_copy(i):
        return pltpu.make_async_copy(hidden_ref.at[pl.ds(i * rows, rows)], rows_ref.at[i], row_sems.at[i])

    for i in range(tiles):
        tile_copy(i).start()
    fetch(me_ref, pool_ref, own_table, own_ref, got_ref, held, sems)
    for i in range(tiles):
        tile_copy(i).wait()
        pltpu.make_async_copy(own_ref.at[0], held.at[i], sems.at[i]).wait()
        out_ref[i] = lax.dot_general(
            held[i], rows_ref[i], (((1,), (1,)), ((), ())), preferred_element_type=jnp.float32
        ).astype(jnp.bfloat16)


def rank_values(me, pool, table, hidden, own, got):
    _, rank, width = own.shape
    tiles = table.shape[1]
    rows = hidden.shape[0] // tiles
    return pl.pallas_call(
        rank_kernel,
        out_shape=jax.ShapeDtypeStruct((tiles, rank, rows), jnp.bfloat16),
        in_specs=[pl.BlockSpec(memory_space=pltpu.SMEM)] * 3 + [pl.BlockSpec(memory_space=pl.ANY)] * 3,
        out_specs=pl.BlockSpec(memory_space=pltpu.VMEM),
        scratch_shapes=[
            pltpu.VMEM((tiles, rows, width), jnp.bfloat16),
            pltpu.VMEM((tiles, rank, width), jnp.bfloat16),
            pltpu.SemaphoreType.DMA((tiles,)),
            pltpu.SemaphoreType.DMA((tiles,)),
        ],
        compiler_params=params(62),
        cost_estimate=cost(2 * hidden.size * rank, 2 * (hidden.size + tiles * rank * width)),
        name="rank_values",
    )(me, pool, table, hidden, own, got)


def sum_kernel(n_add, *refs):
    out_ref = refs[-1]
    width = out_ref.shape[1] * n_add // (len(refs) - 1)
    for c in range((len(refs) - 1) // n_add):
        adds = refs[c * n_add : (c + 1) * n_add]
        value = adds[0][0].astype(jnp.float32)
        for add in adds[1:]:
            value = value + add[0].astype(jnp.float32)
        out_ref[:, pl.ds(c * width, width)] = value


def sum_base(adds, parts):
    flat = [a for chunk in adds for a in chunk]
    _, tokens, n_cols = flat[0].shape
    rows = tokens // parts
    width = n_cols * len(adds)
    return pl.pallas_call(
        functools.partial(sum_kernel, len(adds[0])),
        out_shape=jax.ShapeDtypeStruct((tokens, width), jnp.float32),
        grid=(parts,),
        in_specs=[pl.BlockSpec((1, rows, n_cols), lambda i: (0, i, 0))] * len(flat),
        out_specs=pl.BlockSpec((rows, width), lambda i: (i, 0)),
        compiler_params=params(62),
        cost_estimate=cost(tokens * n_cols * len(flat), tokens * (2 * n_cols * len(flat) + 4 * width)),
        name="base_sum",
    )(*flat)


def final_kernel(per_step, n_add, me_ref, pool_ref, own_table, *refs):
    base_ref, own_ref, got_ref = refs[:3]
    adds, ranks, (out_ref, held, sems) = refs[3 : 3 + n_add], refs[3 + n_add : -3], refs[-3:]
    step = pl.program_id(0)
    rows = ranks[0].shape[2]
    summed = base_ref.shape[1]

    @pl.when(step == 0)
    def _():
        fetch(me_ref, pool_ref, own_table, own_ref, got_ref, held, sems)

    for t in range(per_step):
        tile = step * per_step + t
        span = pl.ds(t * rows, rows)
        rank = ranks[0][t].astype(jnp.float32)
        for other in ranks[1:]:
            rank = rank + other[t].astype(jnp.float32)
        rank = rank.astype(jnp.bfloat16)
        last = adds[0][0, span, :].astype(jnp.float32)
        for add in adds[1:]:
            last = last + add[0, span, :].astype(jnp.float32)
        pltpu.make_async_copy(own_ref.at[0], held.at[tile], sems.at[tile]).wait()
        adapted = lax.dot_general(rank, held[tile], (((0,), (0,)), ((), ())), preferred_element_type=jnp.float32)
        adapted = (adapter_scale * adapted).astype(jnp.bfloat16).astype(jnp.float32)
        out_ref[span, pl.ds(0, summed)] = (base_ref[span, :] + adapted[:, :summed]).astype(jnp.bfloat16)
        out_ref[span, pl.ds(summed, last.shape[1])] = (last + adapted[:, summed:]).astype(jnp.bfloat16)


def final(me, pool, table, ranks, base, adds, own, got):
    _, rank, width = own.shape
    tiles, _, rows = ranks[0].shape
    per_step = 4
    step_rows = per_step * rows
    return pl.pallas_call(
        functools.partial(final_kernel, per_step, len(adds)),
        out_shape=jax.ShapeDtypeStruct((tiles * rows, width), jnp.bfloat16),
        grid=(tiles // per_step,),
        in_specs=[pl.BlockSpec(memory_space=pltpu.SMEM)] * 3
        + [pl.BlockSpec((step_rows, base.shape[1]), lambda i: (i, 0))]
        + [pl.BlockSpec(memory_space=pl.ANY)] * 2
        + [pl.BlockSpec((1, step_rows, a.shape[2]), lambda i: (0, i, 0)) for a in adds]
        + [pl.BlockSpec((per_step, rank, rows), lambda i: (i, 0, 0))] * len(ranks),
        out_specs=pl.BlockSpec((step_rows, width), lambda i: (i, 0)),
        scratch_shapes=[
            pltpu.VMEM((tiles, rank, width), jnp.bfloat16),
            pltpu.SemaphoreType.DMA((tiles,)),
        ],
        compiler_params=params(62),
        cost_estimate=cost(2 * tiles * rows * rank * width, 6 * tiles * rows * width),
        name="adapted_and_sum",
    )(me, pool, table, base, own, got, *adds, *ranks)


def local(
    groups,
    n_tp,
    hidden,
    down_weight,
    adapter_down_factor,
    adapter_up_factor,
    row_tile_adapter,
    adapter_pool_slot,
):
    chips = n_tp // 2
    width = down_weight.shape[1] // n_tp
    chunks = max(1, min(CHUNKS, width // 128))
    n_cols = width // chunks
    tile = min(512, n_cols)
    grp, tp = lax.axis_index("grp"), lax.axis_index("tp")
    chip, core = tp // 2, tp % 2
    me = grp.reshape(1).astype(jnp.int32)

    pool = adapter_pool_slot.astype(jnp.int32)
    own_table = row_tile_adapter.reshape(1, -1).astype(jnp.int32)
    tables = [lax.ppermute(own_table, "grp", [(g, g ^ r) for g in range(groups)]) for r in range(1, groups)]

    def send(v):
        return lax.all_to_all(v, "grp", 0, 0, tiled=True)

    down_out = route(me, pool, tables, adapter_down_factor)
    down_in = send(down_out)

    relative = jnp.array(list(range(1, chips)) + [0], jnp.int32)
    far_chips = (chip ^ relative).astype(jnp.int32)
    theirs, ours = far_chips * 2 + (1 - core), far_chips * 2 + core
    done = down_out
    others, adds = {}, []

    def first_core(c, *done):
        (first,) = gemm(hidden, down_weight, after(theirs, *done), width, n_cols, c * n_cols, tile, chips)
        others[c] = lax.ppermute(first, "tp", [(i, i ^ 1) for i in range(n_tp)])
        return first

    done = first_core(0, down_out)
    for c in range(chunks):
        earlier = adds[c - 2] if c >= 2 else []
        if c + 1 < chunks:
            done = first_core(c + 1, done, *earlier)
        if c == chunks - 1:
            up_out = route(after(me, done), pool, tables, adapter_up_factor)
            done = up_out
        sums = gemm(hidden, down_weight, after(ours, done, *earlier), width, n_cols, c * n_cols, tile, 1, (others[c],))
        done = sums[chips - 1]
        got = [
            lax.ppermute(sums[r - 1], "tp", [(i, i ^ (2 * r)) for i in range(n_tp)])
            for r in range(1, chips)
        ]
        adds.append([done] + got)
    up_in = send(after(up_out, done, *sum(adds[:-2], []), *adds[-2][:UP_GATE]))

    ranks = rank_values(after(me, done), pool, own_table, hidden, adapter_down_factor, down_in)
    ranks = ranks + lax.ppermute(ranks, "tp", [(i, i ^ 1) for i in range(n_tp)])
    ranks = [ranks] + [lax.ppermute(ranks, "tp", [(i, i ^ (2 * r)) for i in range(n_tp)]) for r in range(1, chips)]

    base = sum_base(adds[:-1], own_table.shape[1])
    return final(me, pool, own_table, ranks, base, adds[-1], adapter_up_factor, up_in)


def solution(mesh):
    placed = (
        P("grp", "tp"),
        P("tp", None),
        P("grp", None, "tp"),
        P("grp", None, "tp"),
        P("grp"),
        P(),
    )
    return jax.shard_map(
        functools.partial(local, mesh.shape["grp"], mesh.shape["tp"]),
        mesh=mesh,
        in_specs=placed,
        out_specs=P("grp", "tp"),
        check_vma=False,
    )
```

time: 194 us -> 194 us (level)
  Pallas kernels: 115 us -> 92.6 us
  waiting for transfers between devices: 37.8 us -> 53.9 us
  local copies, waits for them, and re-layouts: 1.39 us -> 9.26 us
    pallas_call x8, Pallas kernels: 88.3 us -> 68.1 us  [gemm(): pl.pallas_call(functools.partial(gemm_kernel, len(adds), n_out, per_out,...]
    all_to_all x2, waiting for transfers between devices: 2.62 us -> 21.1 us  [send(): return lax.all_to_all(v, 'grp', 0, 0, tiled=True)]
    unnamed x30 -> x40, local copies, waits for them, and re-layouts: 0.74 us -> 9.26 us
    ppermute x12, waiting for transfers between devices: 30.5 us -> 27.2 us  [local(): lax.ppermute(sums[r - 1], 'tp', [(i, i ^ 2 * r) for i in range(n_tp)])]
    ppermute x2 -> x3, waiting for transfers between devices: 3.07 us -> 4.01 us  [local(): lax.ppermute(own_table, 'grp', [(g, g ^ r) for g in range(groups)])]
    ppermute x2 -> x3, starting transfers between devices: 6.18 us -> 5.62 us  [local(): lax.ppermute(own_table, 'grp', [(g, g ^ r) for g in range(groups)])]
  transfers between devices with their start and end apart: 24 -> 25, of which waited for: 11 -> 11; matrix products, arithmetic and copies ran while one was open for 1% -> 0% of each run, Pallas kernels for 55% -> 43%
where the time goes in v3:
time: 194 us; the launch traced here: 193 us
  Pallas kernels  92.6 us (48%)
  waiting for transfers between devices  53.9 us (28%)
  starting transfers between devices  35.3 us (18%)
  local copies, waits for them, and re-layouts  9.26 us (5%)
    pallas_call x8, Pallas kernels, gemm(): pl.pallas_call(functools.partial(gemm_kernel, len(adds), n_out, per_out,...  68.1 us
    ppermute x12, waiting for transfers between devices, local(): lax.ppermute(sums[r - 1], 'tp', [(i, i ^ 2 * r) for i in range(n_tp)])  27.2 us
    all_to_all x2, waiting for transfers between devices, send(): return lax.all_to_all(v, 'grp', 0, 0, tiled=True)  21.1 us
    ppermute x12, starting transfers between devices, local(): lax.ppermute(sums[r - 1], 'tp', [(i, i ^ 2 * r) for i in range(n_tp)])  15.7 us
    all_to_all x2, starting transfers between devices, send(): return lax.all_to_all(v, 'grp', 0, 0, tiled=True)  9.56 us
    unnamed x40, local copies, waits for them, and re-layouts  9.26 us
    pallas_call x1, Pallas kernels, sum_base(): pl.pallas_call(functools.partial(sum_kernel, len(adds[0])), out_shape=jax...  6.79 us
    pallas_call x1, Pallas kernels, rank_values(): pl.pallas_call(rank_kernel, out_shape=jax.ShapeDtypeStruct((tiles, rank,...  6.46 us
  transfers between devices with their start and end apart: 25, of which 11 were waited for; matrix products, arithmetic and copies ran while one was open for 0% of the time, Pallas kernels for 43%

profile of v3, /device:TPU:0, one launch (start us, length us, event | category | flops | bytes accessed | tf_op | source)
XLA Modules:
  0.0 192.6 jit_solution(13601622592784478196)
XLA Ops:
  0.0 5.0 %collective-permute-start.2 = (s32[1,8]{1,0:T(1,128)}, s32[1,8]{1,0:T(1,128)S(1)}, u32[]{:S(2)}, u32[]{:S(2)}) collective-permute-start(s32[1,8]{1,0:T(1,128)} %bitcast.4), channel_id=1, source_target_pairs={{0,24},{8,16},{16,8},{24,0},{1,25},{9,17},{17,9},{25,1},{2,26},{10... | collective-permute-start | bytes 104 | tf_op jit(solution)/shard_map/ppermute | solution.py:283
  5.1 0.6 collective-permute-start
  5.6 1.1 collective-permute-done.2.refs_2_
  6.7 2.9 %collective-permute-done.1.refs_1_ = s32[1,8]{1,0:T(1,128)S(1)} collective-permute-done((s32[1,8]{1,0:T(1,128)}, s32[1,8]{1,0:T(1,128)S(1)}, u32[]{:S(2)}, u32[]{:S(2)}) %collective-permute-start.1) | collective-permute-done | bytes 64 | tf_op jit(solution)/shard_map/ppermute | solution.py:283
  10.2 3.0 %adapters_to_send.2 = bf16[4,4,64,2560]{3,2,1,0:T(8,128)(2,1)} custom-call(s32[1]{0:T(128)} %bitcast.me_ref, s32[32]{0:T(128)} %pool_ref.7, s32[1,8]{1,0:T(1,128)} %copy-done.16, s32[1,8]{1,0:T(1,128)} %copy-done.15, s32[1,8]{1,0:T(1,128)} %copy-done.14, bf16[8,64,2560]{2,1,0:T(8,128)(2,1)} %own_ref.1), custom_call_target="tpu_custom_call" | custom-call | bytes 7864320 | tf_op jit(solution)/shard_map/adapters_to_send/pallas_call | solution.py:111
  13.2 5.1 %all-to-all-start.1 = ((bf16[4,4,64,2560]{3,2,1,0:T(8,128)(2,1)}), bf16[4,4,64,2560]{3,2,1,0:T(8,128)(2,1)}, u32[]{:S(2)}, u32[]{:S(2)}) async-start(bf16[4,4,64,2560]{3,2,1,0:T(8,128)(2,1)} %adapters_to_send.2), calls=%async_computation.1 | async-start | bytes 10485760 | tf_op jit(solution)/shard_map/all_to_all | solution.py:286
  18.3 2.5 %copy-done = bf16[1024,2560]{1,0:T(8,128)(2,1)S(1)} copy-done((bf16[1024,2560]{1,0:T(8,128)(2,1)S(1)}, bf16[1024,2560]{1,0:T(8,128)(2,1)}, u32[]{:S(2)}) %copy-start) | copy-done | bytes 5242904
  20.8 8.3 %base_products.8 = bf16[4,1024,256]{2,1,0:T(8,128)(2,1)S(1)} custom-call(s32[4]{0:T(128)S(1)} %get-tuple-element.45.order_ref, bf16[1024,2560]{1,0:T(8,128)(2,1)S(1)} %copy-done, bf16[2560,8192]{1,0:T(8,128)(2,1)} %weight_ref.15), custom_call_target="tpu_custom_call" | custom-call | flops 5368709120 | bytes 12582912 | tf_op jit(solution)/shard_map/base_products/pallas_call | solution.py:66
  29.2 8.1 %base_products.9 = bf16[4,1024,256]{2,1,0:T(8,128)(2,1)S(1)} custom-call(s32[4]{0:T(128)S(1)} %get-tuple-element.45.order_ref, bf16[1024,2560]{1,0:T(8,128)(2,1)S(1)} %copy-done, bf16[2560,8192]{1,0:T(8,128)(2,1)} %weight_ref.15), custom_call_target="tpu_custom_call" | custom-call | flops 5368709120 | bytes 12582912 | tf_op jit(solution)/shard_map/base_products/pallas_call | solution.py:66
  37.3 0.6 collective-permute-start.7
  37.9 8.2 %base_products.10 = (bf16[1,1024,256]{2,1,0:T(8,128)(2,1)S(1)}, bf16[1,1024,256]{2,1,0:T(8,128)(2,1)S(1)}, bf16[1,1024,256]{2,1,0:T(8,128)(2,1)S(1)}, bf16[1,1024,256]{2,1,0:T(8,128)(2,1)S(1)}) custom-call(s32[4]{0:T(128)S(1)} %get-tuple-element.52.order_ref, bf16[1024,2560]{1,0:T(8,128)(2,1)S(1)} %bitcast.3, bf16[2560,8192]{1,0:T(8,128)(2,1)} %weight_ref.15, ...), custom_call_target="tpu_custom_call" | custom-call | flops 5368709120 | bytes 12582912 | tf_op jit(solution)/shard_map/base_products/pallas_call | solution.py:66
  46.1 1.6 collective-permute-start.4
  47.6 1.5 collective-permute-start.5
  49.6 8.1 %base_products.11 = bf16[4,1024,256]{2,1,0:T(8,128)(2,1)S(1)} custom-call(s32[4]{0:T(128)S(1)} %get-tuple-element.45.order_ref, bf16[1024,2560]{1,0:T(8,128)(2,1)S(1)} %bitcast.3, bf16[2560,8192]{1,0:T(8,128)(2,1)} %weight_ref.15), custom_call_target="tpu_custom_call" | custom-call | flops 5368709120 | bytes 12582912 | tf_op jit(solution)/shard_map/base_products/pallas_call | solution.py:66
  57.8 8.2 %base_products.12 = (bf16[1,1024,256]{2,1,0:T(8,128)(2,1)S(1)}, bf16[1,1024,256]{2,1,0:T(8,128)(2,1)S(1)}, bf16[1,1024,256]{2,1,0:T(8,128)(2,1)S(1)}, bf16[1,1024,256]{2,1,0:T(8,128)(2,1)S(1)}) custom-call(s32[4]{0:T(128)S(1)} %get-tuple-element.52.order_ref, bf16[1024,2560]{1,0:T(8,128)(2,1)S(1)} %bitcast.3, bf16[2560,8192]{1,0:T(8,128)(2,1)} %weight_ref.15, ...), custom_call_target="tpu_custom_call" | custom-call | flops 5368709120 | bytes 12582912 | tf_op jit(solution)/shard_map/base_products/pallas_call | solution.py:66
  66.0 6.4 %collective-permute-done.5.refs_2_ = bf16[1,1024,256]{2,1,0:T(8,128)(2,1)S(1)} collective-permute-done((bf16[1,1024,256]{2,1,0:T(8,128)(2,1)S(1)}, bf16[1,1024,256]{2,1,0:T(8,128)(2,1)S(1)}, u32[]{:S(2)}, u32[]{:S(2)}) %collective-permute-start.5) | collective-permute-done | bytes 524320 | tf_op jit(solution)/shard_map/ppermute | solution.py:313
  72.4 8.9 %base_products.13 = bf16[4,1024,256]{2,1,0:T(8,128)(2,1)} custom-call(s32[4]{0:T(128)S(1)} %get-tuple-element.45.order_ref, bf16[1024,2560]{1,0:T(8,128)(2,1)S(1)} %bitcast.3, bf16[2560,8192]{1,0:T(8,128)(2,1)} %weight_ref.15), custom_call_target="tpu_custom_call" | custom-call | flops 5368709120 | bytes 12582912 | tf_op jit(solution)/shard_map/base_products/pallas_call | solution.py:66
  81.4 1.3 collective-permute-start.8
  82.7 0.8 collective-permute-start.9
  83.5 1.4 collective-permute-start.10
  85.0 9.3 %base_products.14 = (bf16[1,1024,256]{2,1,0:T(8,128)(2,1)}, bf16[1,1024,256]{2,1,0:T(8,128)(2,1)}, bf16[1,1024,256]{2,1,0:T(8,128)(2,1)S(1)}, bf16[1,1024,256]{2,1,0:T(8,128)(2,1)S(1)}) custom-call(s32[4]{0:T(128)S(1)} %get-tuple-element.52.order_ref, bf16[1024,2560]{1,0:T(8,128)(2,1)S(1)} %bitcast.3, bf16[2560,8192]{1,0:T(8,128)(2,1)} %weight_ref.15, ...), custom_call_target="tpu_custom_call" | custom-call | flops 5368709120 | bytes 12582912 | tf_op jit(solution)/shard_map/base_products/pallas_call | solution.py:66
  94.3 0.8 copy-done.4
  95.1 1.2 collective-permute-start.12
  96.3 0.8 copy-done.10
  97.1 1.4 collective-permute-start.13
  98.5 2.3 %adapters_to_send.3 = bf16[4,4,64,1024]{3,2,1,0:T(8,128)(2,1)} custom-call(s32[1]{0:T(128)} %bitcast.me_ref, s32[32]{0:T(128)} %pool_ref.7, s32[1,8]{1,0:T(1,128)} %copy-done.16, s32[1,8]{1,0:T(1,128)} %copy-done.15, s32[1,8]{1,0:T(1,128)} %copy-done.14, bf16[8,64,1024]{2,1,0:T(8,128)(2,1)} %refs_1_.1), custom_call_target="tpu_custom_call" | custom-call | bytes 3145728 | tf_op jit(solution)/shard_map/adapters_to_send/pallas_call | solution.py:111
  100.8 5.1 %collective-permute-done.9.refs_6_ = bf16[1,1024,256]{2,1,0:T(8,128)(2,1)} collective-permute-done((bf16[1,1024,256]{2,1,0:T(8,128)(2,1)S(1)}, bf16[1,1024,256]{2,1,0:T(8,128)(2,1)}, u32[]{:S(2)}, u32[]{:S(2)}) %collective-permute-start.9) | collective-permute-done | bytes 524320 | tf_op jit(solution)/shard_map/ppermute | solution.py:313
  105.9 2.6 %collective-permute-done.10.refs_7_ = bf16[1,1024,256]{2,1,0:T(8,128)(2,1)} collective-permute-done((bf16[1,1024,256]{2,1,0:T(8,128)(2,1)S(1)}, bf16[1,1024,256]{2,1,0:T(8,128)(2,1)}, u32[]{:S(2)}, u32[]{:S(2)}) %collective-permute-start.10) | collective-permute-done | bytes 524320 | tf_op jit(solution)/shard_map/ppermute | solution.py:313
  108.5 2.5 %copy-done.1 = bf16[1024,2560]{1,0:T(8,128)(2,1)S(1)} copy-done((bf16[1024,2560]{1,0:T(8,128)(2,1)S(1)}, bf16[1024,2560]{1,0:T(8,128)(2,1)}, u32[]{:S(2)}) %copy-start.1) | copy-done | bytes 5242904
  111.0 9.1 %base_products.15 = (bf16[1,1024,256]{2,1,0:T(8,128)(2,1)}, bf16[1,1024,256]{2,1,0:T(8,128)(2,1)S(1)}, bf16[1,1024,256]{2,1,0:T(8,128)(2,1)S(1)}, bf16[1,1024,256]{2,1,0:T(8,128)(2,1)S(1)}) custom-call(s32[4]{0:T(128)S(1)} %get-tuple-element.52.order_ref, bf16[1024,2560]{1,0:T(8,128)(2,1)S(1)} %copy-done.1, bf16[2560,8192]{1,0:T(8,128)(2,1)} %weight_ref.15, ...), custom_call_target="tpu_custom_call" | custom-call | flops 5368709120 | bytes 12582912 | tf_op jit(solution)/shard_map/base_products/pallas_call | solution.py:66
  120.1 0.8 copy-done.5
  120.9 11.9 %all-to-all-done.1.got_ref = bf16[4,4,64,2560]{3,2,1,0:T(8,128)(2,1)} async-done(((bf16[4,4,64,2560]{3,2,1,0:T(8,128)(2,1)}), bf16[4,4,64,2560]{3,2,1,0:T(8,128)(2,1)}, u32[]{:S(2)}, u32[]{:S(2)}) %all-to-all-start.1) | async-done | bytes 5242912 | tf_op jit(solution)/shard_map/all_to_all | solution.py:286
  132.8 4.5 %all-to-all-start = ((bf16[4,4,64,1024]{3,2,1,0:T(8,128)(2,1)}), bf16[4,4,64,1024]{3,2,1,0:T(8,128)(2,1)}, u32[]{:S(2)}, u32[]{:S(2)}) async-start(bf16[4,4,64,1024]{3,2,1,0:T(8,128)(2,1)} %adapters_to_send.3), calls=%async_computation | async-start | bytes 4194304 | tf_op jit(solution)/shard_map/all_to_all | solution.py:286
  137.2 2.5 %collective-permute-start.14 = (bf16[1,1024,256]{2,1,0:T(8,128)(2,1)S(1)}, bf16[1,1024,256]{2,1,0:T(8,128)(2,1)}, u32[]{:S(2)}, u32[]{:S(2)}) collective-permute-start(bf16[1,1024,256]{2,1,0:T(8,128)(2,1)S(1)} %get-tuple-element.50), channel_id=1, source_target_pairs={{0,6},{1,7},{2,4},{3,5},{4,2},{5,3},{6,0},{7,1},{8,14},{9,15},{10,... | collective-permute-start | bytes 1572872 | tf_op jit(solution)/shard_map/ppermute | solution.py:313
  140.8 2.4 %collective-permute-start.18 = (bf16[1,1024,256]{2,1,0:T(8,128)(2,1)S(1)}, bf16[1,1024,256]{2,1,0:T(8,128)(2,1)}, u32[]{:S(2)}, u32[]{:S(2)}) collective-permute-start(bf16[1,1024,256]{2,1,0:T(8,128)(2,1)S(1)} %get-tuple-element.57), channel_id=1, source_target_pairs={{0,6},{1,7},{2,4},{3,5},{4,2},{5,3},{6,0},{7,1},{8,14},{9,15},{10,... | collective-permute-start | bytes 1572872 | tf_op jit(solution)/shard_map/ppermute | solution.py:313
  143.3 6.5 %rank_values.1 = bf16[8,64,128]{2,1,0:T(8,128)(2,1)} custom-call(s32[1]{0:T(128)} %bitcast.me_ref, s32[32]{0:T(128)} %pool_ref.7, s32[1,8]{1,0:T(1,128)} %bitcast.7, bf16[1024,2560]{1,0:T(8,128)(2,1)} %hidden_ref.17, bf16[8,64,2560]{2,1,0:T(8,128)(2,1)} %own_ref.1, bf16[4,4,64,2560]{3,2,1,0:T(8,128)(2,1)} %all-to-all-done.1.got_ref), custom_call_target="tpu_custom_call" | custom-call | flops 335544320 | bytes 7864320 | tf_op jit(solution)/shard_map/rank_values/pallas_call | solution.py:164
  149.8 1.5 collective-permute-done.19
  151.3 0.9 add.25.refs_7_
  152.3 0.5 collective-permute-start.22
  153.2 1.5 collective-permute-start.21
  154.7 9.8 %collective-permute-done.16.refs_4_ = bf16[1,1024,256]{2,1,0:T(8,128)(2,1)} collective-permute-done((bf16[1,1024,256]{2,1,0:T(8,128)(2,1)}, bf16[1,1024,256]{2,1,0:T(8,128)(2,1)}, u32[]{:S(2)}, u32[]{:S(2)}) %collective-permute-start.16) | collective-permute-done | bytes 524320 | tf_op jit(solution)/shard_map/ppermute | solution.py:313
  164.5 1.5 collective-permute-start.20
  166.0 6.8 %base_sum.1.refs_0_ = f32[1024,768]{1,0:T(8,128)} custom-call(bf16[1,1024,256]{2,1,0:T(8,128)(2,1)} %copy-done.2, bf16[1,1024,256]{2,1,0:T(8,128)(2,1)} %copy-done.7, bf16[1,1024,256]{2,1,0:T(8,128)(2,1)} %copy-done.8, bf16[1,1024,256]{2,1,0:T(8,128)(2,1)} %copy-done.9, bf16[1,1024,256]{2,1,0:T(8,128)(2,1)} %copy-done.3, bf16[1,1024,256]{2,1,0:T(8,128)(2,1)} %copy-done.10, ...), custom_call_target="tpu_custom_call" | custom-call | flops 3145728 | bytes 9437184 | tf_op jit(solution)/shard_map/base_sum/pallas_call | solution.py:197
  172.8 2.9 %collective-permute-done.18.refs_6_ = bf16[1,1024,256]{2,1,0:T(8,128)(2,1)} collective-permute-done((bf16[1,1024,256]{2,1,0:T(8,128)(2,1)S(1)}, bf16[1,1024,256]{2,1,0:T(8,128)(2,1)}, u32[]{:S(2)}, u32[]{:S(2)}) %collective-permute-start.18) | collective-permute-done | bytes 524320 | tf_op jit(solution)/shard_map/ppermute | solution.py:313
  175.7 9.3 %all-to-all-done.refs_2_ = bf16[4,4,64,1024]{3,2,1,0:T(8,128)(2,1)} async-done(((bf16[4,4,64,1024]{3,2,1,0:T(8,128)(2,1)}), bf16[4,4,64,1024]{3,2,1,0:T(8,128)(2,1)}, u32[]{:S(2)}, u32[]{:S(2)}) %all-to-all-start) | async-done | bytes 2097184 | tf_op jit(solution)/shard_map/all_to_all | solution.py:286
  185.0 0.6 copy-done.11
  185.7 0.6 copy-done.13
  186.4 6.0 %adapted_and_sum.1 = bf16[1024,1024]{1,0:T(8,128)(2,1)} custom-call(s32[1]{0:T(128)} %bitcast.me_ref, s32[32]{0:T(128)} %pool_ref.7, s32[1,8]{1,0:T(1,128)} %bitcast.8, f32[1024,768]{1,0:T(8,128)} %base_sum.1.refs_0_, bf16[8,64,1024]{2,1,0:T(8,128)(2,1)} %refs_1_.1, bf16[4,4,64,1024]{3,2,1,0:T(8,128)(2,1)} %all-to-all-done.refs_2_, ...), custom_call_target="tpu_custom_call" | custom-call | flops 134217728 | bytes 6291456 | tf_op jit(solution)/shard_map/adapted_and_sum/pallas_call | solution.py:242
  (58 shorter events, 2.9 us)
Async XLA Ops:
  0.0 6.7 %collective-permute-start.2 = (s32[1,8]{1,0:T(1,128)}, s32[1,8]{1,0:T(1,128)S(1)}, u32[]{:S(2)}, u32[]{:S(2)}) collective-permute-start(s32[1,8]{1,0:T(1,128)} %bitcast.4), channel_id=1, source_target_pairs={{0,24},{8,16},{16,8},{24,0},{1,25},{9,17},{17,9},{25,1},{2,26},{10... | collective-permute-start | bytes 104 | tf_op jit(solution)/shard_map/ppermute | solution.py:283
  5.0 4.6 %collective-permute-start.1 = (s32[1,8]{1,0:T(1,128)}, s32[1,8]{1,0:T(1,128)S(1)}, u32[]{:S(2)}, u32[]{:S(2)}) collective-permute-start(s32[1,8]{1,0:T(1,128)} %bitcast.5), channel_id=1, source_target_pairs={{0,16},{8,24},{16,0},{24,8},{1,17},{9,25},{17,1},{25,9},{2,18},{10... | collective-permute-start | bytes 104 | tf_op jit(solution)/shard_map/ppermute | solution.py:283
  5.1 4.6 %collective-permute-start = (s32[1,8]{1,0:T(1,128)}, s32[1,8]{1,0:T(1,128)S(1)}, u32[]{:S(2)}, u32[]{:S(2)}) collective-permute-start(s32[1,8]{1,0:T(1,128)} %bitcast.6), channel_id=1, source_target_pairs={{0,8},{8,0},{16,24},{24,16},{1,9},{9,1},{17,25},{25,17},{2,10},{10... | collective-permute-start | bytes 104 | tf_op jit(solution)/shard_map/ppermute | solution.py:283
  6.7 2.9 %copy-start.14 = (s32[1,8]{1,0:T(1,128)}, s32[1,8]{1,0:T(1,128)S(1)}, u32[]{:S(2)}) copy-start(s32[1,8]{1,0:T(1,128)S(1)} %collective-permute-done.2.refs_2_) | copy-start | bytes 100
  9.6 0.5 copy-start.15
  9.6 0.5 copy-start.16
  13.1 5.1 %copy-start.17 = (s32[4]{0:T(128)S(1)}, s32[4]{0:T(128)}, u32[]{:S(2)}) copy-start(s32[4]{0:T(128)} %constant.36.clone) | copy-start | bytes 52
  13.2 119.6 %all-to-all-start.1 = ((bf16[4,4,64,2560]{3,2,1,0:T(8,128)(2,1)}), bf16[4,4,64,2560]{3,2,1,0:T(8,128)(2,1)}, u32[]{:S(2)}, u32[]{:S(2)}) async-start(bf16[4,4,64,2560]{3,2,1,0:T(8,128)(2,1)} %adapters_to_send.2), calls=%async_computation.1 | async-start | bytes 10485760 | tf_op jit(solution)/shard_map/all_to_all | solution.py:286
  18.3 2.5 %copy-start = (bf16[1024,2560]{1,0:T(8,128)(2,1)S(1)}, bf16[1024,2560]{1,0:T(8,128)(2,1)}, u32[]{:S(2)}) copy-start(bf16[1024,2560]{1,0:T(8,128)(2,1)} %hidden_ref.17) | copy-start | bytes 15728644
  20.8 17.1 %slice-start = ((s8[5242880]{0:T(1024)(128)(4,1)}), s8[4194304]{0:T(1024)(128)(4,1)S(1)}, s32[]{:S(2)}) async-start(s8[5242880]{0:T(1024)(128)(4,1)} %bitcast.2), calls=%async_computation.2 | async-start | bytes 8388608
  29.1 8.7 %slice-start.1 = ((s8[5242880]{0:T(1024)(128)(4,1)}), s8[1048576]{0:T(1024)(128)(4,1)S(1)}, s32[]{:S(2)}) async-start(s8[5242880]{0:T(1024)(128)(4,1)} %bitcast.2), calls=%async_computation.3 | async-start | bytes 2097152
  29.1 8.7 %collective-permute-start.3 = (bf16[4,1024,256]{2,1,0:T(8,128)(2,1)S(1)}, bf16[4,1024,256]{2,1,0:T(8,128)(2,1)S(1)}, u32[]{:S(2)}, u32[]{:S(2)}) collective-permute-start(bf16[4,1024,256]{2,1,0:T(8,128)(2,1)S(1)} %base_products.8), channel_id=1, source_target_pairs={{0,1},{1,0},{2,3},{3,2},{4,5},{5,4},{6,7},{7,6},{8,9},{9,8},{10,11... | collective-permute-start | bytes 6291464 | tf_op jit(solution)/shard_map/ppermute | solution.py:299
  37.3 20.5 %collective-permute-start.7 = (bf16[4,1024,256]{2,1,0:T(8,128)(2,1)S(1)}, bf16[4,1024,256]{2,1,0:T(8,128)(2,1)S(1)}, u32[]{:S(2)}, u32[]{:S(2)}) collective-permute-start(bf16[4,1024,256]{2,1,0:T(8,128)(2,1)S(1)} %base_products.9), channel_id=1, source_target_pairs={{0,1},{1,0},{2,3},{3,2},{4,5},{5,4},{6,7},{7,6},{8,9},{9,8},{10,11... | collective-permute-start | bytes 6291464 | tf_op jit(solution)/shard_map/ppermute | solution.py:299
  46.0 11.6 %copy-start.2 = (bf16[1,1024,256]{2,1,0:T(8,128)(2,1)}, bf16[1,1024,256]{2,1,0:T(8,128)(2,1)S(1)}, u32[]{:S(2)}) copy-start(bf16[1,1024,256]{2,1,0:T(8,128)(2,1)S(1)} %get-tuple-element.35.refs_0_) | copy-start | bytes 1572868
  46.1 19.9 %collective-permute-start.4 = (bf16[1,1024,256]{2,1,0:T(8,128)(2,1)S(1)}, bf16[1,1024,256]{2,1,0:T(8,128)(2,1)S(1)}, u32[]{:S(2)}, u32[]{:S(2)}) collective-permute-start(bf16[1,1024,256]{2,1,0:T(8,128)(2,1)S(1)} %get-tuple-element.36), channel_id=1, source_target_pairs={{0,2},{1,3},{2,0},{3,1},{4,6},{5,7},{6,4},{7,5},{8,10},{9,11},{10,... | collective-permute-start | bytes 1572872 | tf_op jit(solution)/shard_map/ppermute | solution.py:313
  47.6 24.8 %collective-permute-start.5 = (bf16[1,1024,256]{2,1,0:T(8,128)(2,1)S(1)}, bf16[1,1024,256]{2,1,0:T(8,128)(2,1)S(1)}, u32[]{:S(2)}, u32[]{:S(2)}) collective-permute-start(bf16[1,1024,256]{2,1,0:T(8,128)(2,1)S(1)} %get-tuple-element.37), channel_id=1, source_target_pairs={{0,4},{1,5},{2,6},{3,7},{4,0},{5,1},{6,2},{7,3},{8,12},{9,13},{10,... | collective-permute-start | bytes 1572872 | tf_op jit(solution)/shard_map/ppermute | solution.py:313
  49.1 23.3 %collective-permute-start.6 = (bf16[1,1024,256]{2,1,0:T(8,128)(2,1)S(1)}, bf16[1,1024,256]{2,1,0:T(8,128)(2,1)S(1)}, u32[]{:S(2)}, u32[]{:S(2)}) collective-permute-start(bf16[1,1024,256]{2,1,0:T(8,128)(2,1)S(1)} %get-tuple-element.38), channel_id=1, source_target_pairs={{0,6},{1,7},{2,4},{3,5},{4,2},{5,3},{6,0},{7,1},{8,14},{9,15},{10,... | collective-permute-start | bytes 1572872 | tf_op jit(solution)/shard_map/ppermute | solution.py:313
  57.7 27.3 %collective-permute-start.11 = (bf16[4,1024,256]{2,1,0:T(8,128)(2,1)S(1)}, bf16[4,1024,256]{2,1,0:T(8,128)(2,1)S(1)}, u32[]{:S(2)}, u32[]{:S(2)}) collective-permute-start(bf16[4,1024,256]{2,1,0:T(8,128)(2,1)S(1)} %base_products.11), channel_id=1, source_target_pairs={{0,1},{1,0},{2,3},{3,2},{4,5},{5,4},{6,7},{7,6},{8,9},{9,8},{10,11... | collective-permute-start | bytes 6291464 | tf_op jit(solution)/shard_map/ppermute | solution.py:299
  66.0 15.4 %copy-start.3 = (bf16[1,1024,256]{2,1,0:T(8,128)(2,1)}, bf16[1,1024,256]{2,1,0:T(8,128)(2,1)S(1)}, u32[]{:S(2)}) copy-start(bf16[1,1024,256]{2,1,0:T(8,128)(2,1)S(1)} %get-tuple-element.41.refs_4_) | copy-start | bytes 1572868
  66.0 15.3 %copy-start.7 = (bf16[1,1024,256]{2,1,0:T(8,128)(2,1)}, bf16[1,1024,256]{2,1,0:T(8,128)(2,1)S(1)}, u32[]{:S(2)}) copy-start(bf16[1,1024,256]{2,1,0:T(8,128)(2,1)S(1)} %collective-permute-done.4.refs_1_) | copy-start | bytes 1572868
  72.4 8.9 %copy-start.8 = (bf16[1,1024,256]{2,1,0:T(8,128)(2,1)}, bf16[1,1024,256]{2,1,0:T(8,128)(2,1)S(1)}, u32[]{:S(2)}) copy-start(bf16[1,1024,256]{2,1,0:T(8,128)(2,1)S(1)} %collective-permute-done.5.refs_2_) | copy-start | bytes 1572868
  72.4 8.9 %copy-start.9 = (bf16[1,1024,256]{2,1,0:T(8,128)(2,1)}, bf16[1,1024,256]{2,1,0:T(8,128)(2,1)S(1)}, u32[]{:S(2)}) copy-start(bf16[1,1024,256]{2,1,0:T(8,128)(2,1)S(1)} %collective-permute-done.6.refs_3_) | copy-start | bytes 1572868
  81.3 27.2 %collective-permute-start.15 = (bf16[4,1024,256]{2,1,0:T(8,128)(2,1)}, bf16[4,1024,256]{2,1,0:T(8,128)(2,1)}, u32[]{:S(2)}, u32[]{:S(2)}) collective-permute-start(bf16[4,1024,256]{2,1,0:T(8,128)(2,1)} %base_products.13), channel_id=1, source_target_pairs={{0,1},{1,0},{2,3},{3,2},{4,5},{5,4},{6,7},{7,6},{8,9},{9,8},{10,11... | collective-permute-start | bytes 6291464 | tf_op jit(solution)/shard_map/ppermute | solution.py:299
  81.4 14.9 %collective-permute-start.8 = (bf16[1,1024,256]{2,1,0:T(8,128)(2,1)S(1)}, bf16[1,1024,256]{2,1,0:T(8,128)(2,1)S(1)}, u32[]{:S(2)}, u32[]{:S(2)}) collective-permute-start(bf16[1,1024,256]{2,1,0:T(8,128)(2,1)S(1)} %get-tuple-element.42), channel_id=1, source_target_pairs={{0,2},{1,3},{2,0},{3,1},{4,6},{5,7},{6,4},{7,5},{8,10},{9,11},{10,... | collective-permute-start | bytes 1572872 | tf_op jit(solution)/shard_map/ppermute | solution.py:313
  82.7 23.2 %collective-permute-start.9 = (bf16[1,1024,256]{2,1,0:T(8,128)(2,1)S(1)}, bf16[1,1024,256]{2,1,0:T(8,128)(2,1)}, u32[]{:S(2)}, u32[]{:S(2)}) collective-permute-start(bf16[1,1024,256]{2,1,0:T(8,128)(2,1)S(1)} %get-tuple-element.43), channel_id=1, source_target_pairs={{0,4},{1,5},{2,6},{3,7},{4,0},{5,1},{6,2},{7,3},{8,12},{9,13},{10,... | collective-permute-start | bytes 1572872 | tf_op jit(solution)/shard_map/ppermute | solution.py:313
  83.5 25.0 %collective-permute-start.10 = (bf16[1,1024,256]{2,1,0:T(8,128)(2,1)S(1)}, bf16[1,1024,256]{2,1,0:T(8,128)(2,1)}, u32[]{:S(2)}, u32[]{:S(2)}) collective-permute-start(bf16[1,1024,256]{2,1,0:T(8,128)(2,1)S(1)} %get-tuple-element.44), channel_id=1, source_target_pairs={{0,6},{1,7},{2,4},{3,5},{4,2},{5,3},{6,0},{7,1},{8,14},{9,15},{10,... | collective-permute-start | bytes 1572872 | tf_op jit(solution)/shard_map/ppermute | solution.py:313
  94.3 0.8 copy-start.4
  95.1 25.8 %collective-permute-start.12 = (bf16[1,1024,256]{2,1,0:T(8,128)(2,1)}, bf16[1,1024,256]{2,1,0:T(8,128)(2,1)}, u32[]{:S(2)}, u32[]{:S(2)}) collective-permute-start(bf16[1,1024,256]{2,1,0:T(8,128)(2,1)} %get-tuple-element.48), channel_id=1, source_target_pairs={{0,2},{1,3},{2,0},{3,1},{4,6},{5,7},{6,4},{7,5},{8,10},{9,11},{10,... | collective-permute-start | bytes 1572872 | tf_op jit(solution)/shard_map/ppermute | solution.py:313
  96.3 0.8 copy-start.10
  97.1 23.8 %collective-permute-start.13 = (bf16[1,1024,256]{2,1,0:T(8,128)(2,1)}, bf16[1,1024,256]{2,1,0:T(8,128)(2,1)}, u32[]{:S(2)}, u32[]{:S(2)}) collective-permute-start(bf16[1,1024,256]{2,1,0:T(8,128)(2,1)} %get-tuple-element.49), channel_id=1, source_target_pairs={{0,4},{1,5},{2,6},{3,7},{4,0},{5,1},{6,2},{7,3},{8,12},{9,13},{10,... | collective-permute-start | bytes 1572872 | tf_op jit(solution)/shard_map/ppermute | solution.py:313
  108.5 2.5 %copy-start.1 = (bf16[1024,2560]{1,0:T(8,128)(2,1)S(1)}, bf16[1024,2560]{1,0:T(8,128)(2,1)}, u32[]{:S(2)}) copy-start(bf16[1024,2560]{1,0:T(8,128)(2,1)} %hidden_ref.17) | copy-start | bytes 15728644
  120.1 0.8 copy-start.5
  132.8 52.2 %all-to-all-start = ((bf16[4,4,64,1024]{3,2,1,0:T(8,128)(2,1)}), bf16[4,4,64,1024]{3,2,1,0:T(8,128)(2,1)}, u32[]{:S(2)}, u32[]{:S(2)}) async-start(bf16[4,4,64,1024]{3,2,1,0:T(8,128)(2,1)} %adapters_to_send.3), calls=%async_computation | async-start | bytes 4194304 | tf_op jit(solution)/shard_map/all_to_all | solution.py:286
  137.2 16.0 %collective-permute-start.14 = (bf16[1,1024,256]{2,1,0:T(8,128)(2,1)S(1)}, bf16[1,1024,256]{2,1,0:T(8,128)(2,1)}, u32[]{:S(2)}, u32[]{:S(2)}) collective-permute-start(bf16[1,1024,256]{2,1,0:T(8,128)(2,1)S(1)} %get-tuple-element.50), channel_id=1, source_target_pairs={{0,6},{1,7},{2,4},{3,5},{4,2},{5,3},{6,0},{7,1},{8,14},{9,15},{10,... | collective-permute-start | bytes 1572872 | tf_op jit(solution)/shard_map/ppermute | solution.py:313
  139.8 24.8 %collective-permute-start.16 = (bf16[1,1024,256]{2,1,0:T(8,128)(2,1)}, bf16[1,1024,256]{2,1,0:T(8,128)(2,1)}, u32[]{:S(2)}, u32[]{:S(2)}) collective-permute-start(bf16[1,1024,256]{2,1,0:T(8,128)(2,1)} %get-tuple-element.55), channel_id=1, source_target_pairs={{0,2},{1,3},{2,0},{3,1},{4,6},{5,7},{6,4},{7,5},{8,10},{9,11},{10,... | collective-permute-start | bytes 1572872 | tf_op jit(solution)/shard_map/ppermute | solution.py:313
  140.3 32.5 %collective-permute-start.17 = (bf16[1,1024,256]{2,1,0:T(8,128)(2,1)S(1)}, bf16[1,1024,256]{2,1,0:T(8,128)(2,1)}, u32[]{:S(2)}, u32[]{:S(2)}) collective-permute-start(bf16[1,1024,256]{2,1,0:T(8,128)(2,1)S(1)} %get-tuple-element.56), channel_id=1, source_target_pairs={{0,4},{1,5},{2,6},{3,7},{4,0},{5,1},{6,2},{7,3},{8,12},{9,13},{10,... | collective-permute-start | bytes 1572872 | tf_op jit(solution)/shard_map/ppermute | solution.py:313
  140.8 34.9 %collective-permute-start.18 = (bf16[1,1024,256]{2,1,0:T(8,128)(2,1)S(1)}, bf16[1,1024,256]{2,1,0:T(8,128)(2,1)}, u32[]{:S(2)}, u32[]{:S(2)}) collective-permute-start(bf16[1,1024,256]{2,1,0:T(8,128)(2,1)S(1)} %get-tuple-element.57), channel_id=1, source_target_pairs={{0,6},{1,7},{2,4},{3,5},{4,2},{5,3},{6,0},{7,1},{8,14},{9,15},{10,... | collective-permute-start | bytes 1572872 | tf_op jit(solution)/shard_map/ppermute | solution.py:313
  149.7 1.6 collective-permute-start.19
  152.3 20.5 %copy-start.6 = (bf16[8,64,128]{2,1,0:T(8,128)(2,1)}, bf16[8,64,128]{2,1,0:T(8,128)(2,1)S(1)}, u32[]{:S(2)}) copy-start(bf16[8,64,128]{2,1,0:T(8,128)(2,1)S(1)} %add.25.refs_7_) | copy-start | bytes 393220
  152.3 32.7 %collective-permute-start.22 = (bf16[8,64,128]{2,1,0:T(8,128)(2,1)S(1)}, bf16[8,64,128]{2,1,0:T(8,128)(2,1)S(1)}, u32[]{:S(2)}, u32[]{:S(2)}) collective-permute-start(bf16[8,64,128]{2,1,0:T(8,128)(2,1)S(1)} %add.25.refs_7_), channel_id=1, source_target_pairs={{0,6},{1,7},{2,4},{3,5},{4,2},{5,3},{6,0},{7,1},{8,14},{9,15},{10,... | collective-permute-start | bytes 393224 | tf_op jit(solution)/shard_map/ppermute | solution.py:321
  153.2 31.8 %collective-permute-start.21 = (bf16[8,64,128]{2,1,0:T(8,128)(2,1)S(1)}, bf16[8,64,128]{2,1,0:T(8,128)(2,1)S(1)}, u32[]{:S(2)}, u32[]{:S(2)}) collective-permute-start(bf16[8,64,128]{2,1,0:T(8,128)(2,1)S(1)} %add.25.refs_7_), channel_id=1, source_target_pairs={{0,4},{1,5},{2,6},{3,7},{4,0},{5,1},{6,2},{7,3},{8,12},{9,13},{10,... | collective-permute-start | bytes 393224 | tf_op jit(solution)/shard_map/ppermute | solution.py:321
  164.5 20.5 %collective-permute-start.20 = (bf16[8,64,128]{2,1,0:T(8,128)(2,1)S(1)}, bf16[8,64,128]{2,1,0:T(8,128)(2,1)S(1)}, u32[]{:S(2)}, u32[]{:S(2)}) collective-permute-start(bf16[8,64,128]{2,1,0:T(8,128)(2,1)S(1)} %add.25.refs_7_), channel_id=1, source_target_pairs={{0,2},{1,3},{2,0},{3,1},{4,6},{5,7},{6,4},{7,5},{8,10},{9,11},{10,... | collective-permute-start | bytes 393224 | tf_op jit(solution)/shard_map/ppermute | solution.py:321
  185.0 0.6 copy-start.11
  185.0 0.7 copy-start.12
  185.7 0.7 copy-start.13

commit v4 on v3

--- a/solution.py
+++ b/solution.py
@@ -178,39 +178,53 @@
     )(me, pool, table, hidden, own, got)
 
 
-def sum_kernel(n_add, *refs):
-    out_ref = refs[-1]
-    width = out_ref.shape[1] * n_add // (len(refs) - 1)
-    for c in range((len(refs) - 1) // n_add):
-        adds = refs[c * n_add : (c + 1) * n_add]
-        value = adds[0][0].astype(jnp.float32)
-        for add in adds[1:]:
+def sum_kernel(n_add, chunks, *refs):
+    adds, out_ref = refs[: n_add * chunks], refs[-1] if len(refs) == n_add * chunks + 1 else refs[-2]
+    width = adds[0].shape[2]
+    for c in range(chunks):
+        value = adds[c * n_add][0].astype(jnp.float32)
+        for add in adds[c * n_add + 1 : (c + 1) * n_add]:
             value = value + add[0].astype(jnp.float32)
         out_ref[:, pl.ds(c * width, width)] = value
-
-
-def sum_base(adds, parts):
+    if len(refs) > n_add * chunks + 1:
+        ranks, rank_ref = refs[n_add * chunks : -2], refs[-1]
+        for t in range(rank_ref.shape[0]):
+            rank = ranks[0][t].astype(jnp.float32)
+            for other in ranks[1:]:
+                rank = rank + other[t].astype(jnp.float32)
+            rank_ref[t] = rank.astype(jnp.bfloat16).T
+
+
+def sum_base(adds, tiles, per_step, ranks=()):
     flat = [a for chunk in adds for a in chunk]
     _, tokens, n_cols = flat[0].shape
-    rows = tokens // parts
+    steps = tiles // per_step
+    rows = tokens // steps
     width = n_cols * len(adds)
+    out_shape = [jax.ShapeDtypeStruct((tokens, width), jnp.float32)]
+    out_specs = [pl.BlockSpec((rows, width), lambda i: (i, 0))]
+    rank_specs = []
+    for part in ranks:
+        rank_specs.append(pl.BlockSpec((per_step, *part.shape[1:]), lambda i: (i, 0, 0)))
+    if ranks:
+        _, rank, tile = ranks[0].shape
+        out_shape.append(jax.ShapeDtypeStruct((tiles, tile, rank), jnp.bfloat16))
+        out_specs.append(pl.BlockSpec((per_step, tile, rank), lambda i: (i, 0, 0)))
     return pl.pallas_call(
-        functools.partial(sum_kernel, len(adds[0])),
-        out_shape=jax.ShapeDtypeStruct((tokens, width), jnp.float32),
-        grid=(parts,),
-        in_specs=[pl.BlockSpec((1, rows, n_cols), lambda i: (0, i, 0))] * len(flat),
-        out_specs=pl.BlockSpec((rows, width), lambda i: (i, 0)),
+        functools.partial(sum_kernel, len(adds[0]), len(adds)),
+        out_shape=out_shape,
+        grid=(steps,),
+        in_specs=[pl.BlockSpec((1, rows, n_cols), lambda i: (0, i, 0))] * len(flat) + rank_specs,
+        out_specs=out_specs,
         compiler_params=params(62),
         cost_estimate=cost(tokens * n_cols * len(flat), tokens * (2 * n_cols * len(flat) + 4 * width)),
         name="base_sum",
-    )(*flat)
-
-
-def final_kernel(per_step, n_add, me_ref, pool_ref, own_table, *refs):
-    base_ref, own_ref, got_ref = refs[:3]
-    adds, ranks, (out_ref, held, sems) = refs[3 : 3 + n_add], refs[3 + n_add : -3], refs[-3:]
+    )(*flat, *ranks)
+
+
+def final_kernel(per_step, me_ref, pool_ref, own_table, base_ref, last_ref, rank_ref, own_ref, got_ref, out_ref, held, sems):
     step = pl.program_id(0)
-    rows = ranks[0].shape[2]
+    rows = rank_ref.shape[1]
     summed = base_ref.shape[1]
 
     @pl.when(step == 0)
@@ -220,34 +234,27 @@
     for t in range(per_step):
         tile = step * per_step + t
         span = pl.ds(t * rows, rows)
-        rank = ranks[0][t].astype(jnp.float32)
-        for other in ranks[1:]:
-            rank = rank + other[t].astype(jnp.float32)
-        rank = rank.astype(jnp.bfloat16)
-        last = adds[0][0, span, :].astype(jnp.float32)
-        for add in adds[1:]:
-            last = last + add[0, span, :].astype(jnp.float32)
         pltpu.make_async_copy(own_ref.at[0], held.at[tile], sems.at[tile]).wait()
-        adapted = lax.dot_general(rank, held[tile], (((0,), (0,)), ((), ())), preferred_element_type=jnp.float32)
+        adapted = jnp.dot(rank_ref[t], held[tile], preferred_element_type=jnp.float32)
         adapted = (adapter_scale * adapted).astype(jnp.bfloat16).astype(jnp.float32)
         out_ref[span, pl.ds(0, summed)] = (base_ref[span, :] + adapted[:, :summed]).astype(jnp.bfloat16)
-        out_ref[span, pl.ds(summed, last.shape[1])] = (last + adapted[:, summed:]).astype(jnp.bfloat16)
-
-
-def final(me, pool, table, ranks, base, adds, own, got):
+        rest = last_ref[span, :] + adapted[:, summed:]
+        out_ref[span, pl.ds(summed, rest.shape[1])] = rest.astype(jnp.bfloat16)
+
+
+def final(me, pool, table, ranks, base, last, own, got):
     _, rank, width = own.shape
-    tiles, _, rows = ranks[0].shape
+    tiles, rows, _ = ranks.shape
     per_step = 4
     step_rows = per_step * rows
     return pl.pallas_call(
-        functools.partial(final_kernel, per_step, len(adds)),
+        functools.partial(final_kernel, per_step),
         out_shape=jax.ShapeDtypeStruct((tiles * rows, width), jnp.bfloat16),
         grid=(tiles // per_step,),
         in_specs=[pl.BlockSpec(memory_space=pltpu.SMEM)] * 3
-        + [pl.BlockSpec((step_rows, base.shape[1]), lambda i: (i, 0))]
-        + [pl.BlockSpec(memory_space=pl.ANY)] * 2
-        + [pl.BlockSpec((1, step_rows, a.shape[2]), lambda i: (0, i, 0)) for a in adds]
-        + [pl.BlockSpec((per_step, rank, rows), lambda i: (i, 0, 0))] * len(ranks),
+        + [pl.BlockSpec((step_rows, a.shape[1]), lambda i: (i, 0)) for a in (base, last)]
+        + [pl.BlockSpec((per_step, rows, rank), lambda i: (i, 0, 0))]
+        + [pl.BlockSpec(memory_space=pl.ANY)] * 2,
         out_specs=pl.BlockSpec((step_rows, width), lambda i: (i, 0)),
         scratch_shapes=[
             pltpu.VMEM((tiles, rank, width), jnp.bfloat16),
@@ -256,7 +263,7 @@
         compiler_params=params(62),
         cost_estimate=cost(2 * tiles * rows * rank * width, 6 * tiles * rows * width),
         name="adapted_and_sum",
-    )(me, pool, table, base, own, got, *adds, *ranks)
+    )(me, pool, table, base, last, ranks, own, got)
 
 
 def local(
@@ -320,8 +327,10 @@
     ranks = ranks + lax.ppermute(ranks, "tp", [(i, i ^ 1) for i in range(n_tp)])
     ranks = [ranks] + [lax.ppermute(ranks, "tp", [(i, i ^ (2 * r)) for i in range(n_tp)]) for r in range(1, chips)]
 
-    base = sum_base(adds[:-1], own_table.shape[1])
-    return final(me, pool, own_table, ranks, base, adds[-1], adapter_up_factor, up_in)
+    tiles = own_table.shape[1]
+    (base,) = sum_base(adds[:-1], tiles, 2)
+    last, ranks = sum_base(adds[-1:], tiles, 4, ranks)
+    return final(me, pool, own_table, ranks, base, last, adapter_up_factor, up_in)
 
 
 def solution(mesh):

time: 194 us -> 191 us (0.985)
  waiting for transfers between devices: 53.9 us -> 51.7 us
    all_to_all x2, waiting for transfers between devices: 21.1 us -> 13.7 us  [send(): return lax.all_to_all(v, 'grp', 0, 0, tiled=True)]
    ppermute x3, waiting for transfers between devices: 0.01 us -> 3.58 us  [local(): lax.ppermute(ranks, 'tp', [(i, i ^ 2 * r) for i in range(n_tp)])]
    pallas_call x2 -> x3, Pallas kernels: 12.8 us -> 13.3 us  [the longest x2 7.81 us: sum_base(): pl.pallas_call(functools.partial(sum_kernel, len(adds[0]), len(adds)), ou...]
  transfers between devices with their start and end apart: 25 -> 25, of which waited for: 11 -> 14; matrix products, arithmetic and copies ran while one was open for 0% -> 0% of each run, Pallas kernels for 43% -> 44%
where the time goes in v4:
time: 191 us
  Pallas kernels  93.2 us (49%)
  waiting for transfers between devices  51.7 us (27%)
  starting transfers between devices  35.3 us (18%)
  local copies, waits for them, and re-layouts  9.16 us (5%)
    pallas_call x8, Pallas kernels, gemm(): pl.pallas_call(functools.partial(gemm_kernel, len(adds), n_out, per_out,...  68.1 us
    ppermute x12, waiting for transfers between devices, local(): lax.ppermute(sums[r - 1], 'tp', [(i, i ^ 2 * r) for i in range(n_tp)])  28.9 us
    ppermute x12, starting transfers between devices, local(): lax.ppermute(sums[r - 1], 'tp', [(i, i ^ 2 * r) for i in range(n_tp)])  15.7 us
    all_to_all x2, waiting for transfers between devices, send(): return lax.all_to_all(v, 'grp', 0, 0, tiled=True)  13.7 us
    all_to_all x2, starting transfers between devices, send(): return lax.all_to_all(v, 'grp', 0, 0, tiled=True)  9.56 us
    unnamed x40, local copies, waits for them, and re-layouts  9.16 us
    pallas_call x2, Pallas kernels, sum_base(): pl.pallas_call(functools.partial(sum_kernel, len(adds[0]), len(adds)), ou...  7.81 us
    pallas_call x1, Pallas kernels, rank_values(): pl.pallas_call(rank_kernel, out_shape=jax.ShapeDtypeStruct((tiles, rank,...  6.45 us
  transfers between devices with their start and end apart: 25, of which 14 were waited for; matrix products, arithmetic and copies ran while one was open for 0% of the time, Pallas kernels for 44%

profile of v4, /device:TPU:0, one launch (start us, length us, event | category | flops | bytes accessed | tf_op | source)
XLA Modules:
  0.0 190.8 jit_solution(3024248087651540230)
XLA Ops:
  0.0 5.0 %collective-permute-start.2 = (s32[1,8]{1,0:T(1,128)}, s32[1,8]{1,0:T(1,128)S(1)}, u32[]{:S(2)}, u32[]{:S(2)}) collective-permute-start(s32[1,8]{1,0:T(1,128)} %bitcast.4), channel_id=1, source_target_pairs={{0,24},{8,16},{16,8},{24,0},{1,25},{9,17},{17,9},{25,1},{2,26},{10... | collective-permute-start | bytes 104 | tf_op jit(solution)/shard_map/ppermute | solution.py:290
  5.6 1.1 collective-permute-done.2.refs_2_
  6.7 2.9 %collective-permute-done.1.refs_1_ = s32[1,8]{1,0:T(1,128)S(1)} collective-permute-done((s32[1,8]{1,0:T(1,128)}, s32[1,8]{1,0:T(1,128)S(1)}, u32[]{:S(2)}, u32[]{:S(2)}) %collective-permute-start.1) | collective-permute-done | bytes 64 | tf_op jit(solution)/shard_map/ppermute | solution.py:290
  9.6 0.6 copy-done.15
  10.2 3.0 %adapters_to_send.2 = bf16[4,4,64,2560]{3,2,1,0:T(8,128)(2,1)} custom-call(s32[1]{0:T(128)} %bitcast.me_ref, s32[32]{0:T(128)} %pool_ref.7, s32[1,8]{1,0:T(1,128)} %copy-done.16, s32[1,8]{1,0:T(1,128)} %copy-done.15, s32[1,8]{1,0:T(1,128)} %copy-done.14, bf16[8,64,2560]{2,1,0:T(8,128)(2,1)} %own_ref.2), custom_call_target="tpu_custom_call" | custom-call | bytes 7864320 | tf_op jit(solution)/shard_map/adapters_to_send/pallas_call | solution.py:111
  13.3 5.1 %all-to-all-start = ((bf16[4,4,64,2560]{3,2,1,0:T(8,128)(2,1)}), bf16[4,4,64,2560]{3,2,1,0:T(8,128)(2,1)}, u32[]{:S(2)}, u32[]{:S(2)}) async-start(bf16[4,4,64,2560]{3,2,1,0:T(8,128)(2,1)} %adapters_to_send.2), calls=%async_computation | async-start | bytes 10485760 | tf_op jit(solution)/shard_map/all_to_all | solution.py:293
  18.4 2.5 %copy-done = bf16[1024,2560]{1,0:T(8,128)(2,1)S(1)} copy-done((bf16[1024,2560]{1,0:T(8,128)(2,1)S(1)}, bf16[1024,2560]{1,0:T(8,128)(2,1)}, u32[]{:S(2)}) %copy-start) | copy-done | bytes 5242904
  20.9 8.3 %base_products.8 = bf16[4,1024,256]{2,1,0:T(8,128)(2,1)S(1)} custom-call(s32[4]{0:T(128)S(1)} %get-tuple-element.47.order_ref, bf16[1024,2560]{1,0:T(8,128)(2,1)S(1)} %copy-done, bf16[2560,8192]{1,0:T(8,128)(2,1)} %weight_ref.15), custom_call_target="tpu_custom_call" | custom-call | flops 5368709120 | bytes 12582912 | tf_op jit(solution)/shard_map/base_products/pallas_call | solution.py:66
  29.4 8.1 %base_products.9 = bf16[4,1024,256]{2,1,0:T(8,128)(2,1)S(1)} custom-call(s32[4]{0:T(128)S(1)} %get-tuple-element.47.order_ref, bf16[1024,2560]{1,0:T(8,128)(2,1)S(1)} %copy-done, bf16[2560,8192]{1,0:T(8,128)(2,1)} %weight_ref.15), custom_call_target="tpu_custom_call" | custom-call | flops 5368709120 | bytes 12582912 | tf_op jit(solution)/shard_map/base_products/pallas_call | solution.py:66
  38.0 8.2 %base_products.10 = (bf16[1,1024,256]{2,1,0:T(8,128)(2,1)S(1)}, bf16[1,1024,256]{2,1,0:T(8,128)(2,1)S(1)}, bf16[1,1024,256]{2,1,0:T(8,128)(2,1)S(1)}, bf16[1,1024,256]{2,1,0:T(8,128)(2,1)S(1)}) custom-call(s32[4]{0:T(128)S(1)} %get-tuple-element.54.order_ref, bf16[1024,2560]{1,0:T(8,128)(2,1)S(1)} %bitcast.3, bf16[2560,8192]{1,0:T(8,128)(2,1)} %weight_ref.15, ...), custom_call_target="tpu_custom_call" | custom-call | flops 5368709120 | bytes 12582912 | tf_op jit(solution)/shard_map/base_products/pallas_call | solution.py:66
  46.2 1.6 collective-permute-start.4
  47.7 1.5 collective-permute-start.5
  49.7 8.1 %base_products.11 = bf16[4,1024,256]{2,1,0:T(8,128)(2,1)S(1)} custom-call(s32[4]{0:T(128)S(1)} %get-tuple-element.47.order_ref, bf16[1024,2560]{1,0:T(8,128)(2,1)S(1)} %bitcast.3, bf16[2560,8192]{1,0:T(8,128)(2,1)} %weight_ref.15), custom_call_target="tpu_custom_call" | custom-call | flops 5368709120 | bytes 12582912 | tf_op jit(solution)/shard_map/base_products/pallas_call | solution.py:66
  57.9 8.2 %base_products.12 = (bf16[1,1024,256]{2,1,0:T(8,128)(2,1)S(1)}, bf16[1,1024,256]{2,1,0:T(8,128)(2,1)S(1)}, bf16[1,1024,256]{2,1,0:T(8,128)(2,1)S(1)}, bf16[1,1024,256]{2,1,0:T(8,128)(2,1)S(1)}) custom-call(s32[4]{0:T(128)S(1)} %get-tuple-element.54.order_ref, bf16[1024,2560]{1,0:T(8,128)(2,1)S(1)} %bitcast.3, bf16[2560,8192]{1,0:T(8,128)(2,1)} %weight_ref.15, ...), custom_call_target="tpu_custom_call" | custom-call | flops 5368709120 | bytes 12582912 | tf_op jit(solution)/shard_map/base_products/pallas_call | solution.py:66
  66.1 6.4 %collective-permute-done.5.refs_2_ = bf16[1,1024,256]{2,1,0:T(8,128)(2,1)S(1)} collective-permute-done((bf16[1,1024,256]{2,1,0:T(8,128)(2,1)S(1)}, bf16[1,1024,256]{2,1,0:T(8,128)(2,1)S(1)}, u32[]{:S(2)}, u32[]{:S(2)}) %collective-permute-start.5) | collective-permute-done | bytes 524320 | tf_op jit(solution)/shard_map/ppermute | solution.py:320
  72.6 8.9 %base_products.13 = bf16[4,1024,256]{2,1,0:T(8,128)(2,1)} custom-call(s32[4]{0:T(128)S(1)} %get-tuple-element.47.order_ref, bf16[1024,2560]{1,0:T(8,128)(2,1)S(1)} %bitcast.3, bf16[2560,8192]{1,0:T(8,128)(2,1)} %weight_ref.15), custom_call_target="tpu_custom_call" | custom-call | flops 5368709120 | bytes 12582912 | tf_op jit(solution)/shard_map/base_products/pallas_call | solution.py:66
  81.5 1.3 collective-permute-start.8
  82.8 0.8 collective-permute-start.9
  83.7 1.4 collective-permute-start.10
  85.1 9.3 %base_products.14 = (bf16[1,1024,256]{2,1,0:T(8,128)(2,1)}, bf16[1,1024,256]{2,1,0:T(8,128)(2,1)}, bf16[1,1024,256]{2,1,0:T(8,128)(2,1)S(1)}, bf16[1,1024,256]{2,1,0:T(8,128)(2,1)S(1)}) custom-call(s32[4]{0:T(128)S(1)} %get-tuple-element.54.order_ref, bf16[1024,2560]{1,0:T(8,128)(2,1)S(1)} %bitcast.3, bf16[2560,8192]{1,0:T(8,128)(2,1)} %weight_ref.15, ...), custom_call_target="tpu_custom_call" | custom-call | flops 5368709120 | bytes 12582912 | tf_op jit(solution)/shard_map/base_products/pallas_call | solution.py:66
  94.4 0.8 copy-done.4
  95.2 1.2 collective-permute-start.12
  96.5 0.8 copy-done.9
  97.2 1.4 collective-permute-start.13
  98.6 2.3 %adapters_to_send.3 = bf16[4,4,64,1024]{3,2,1,0:T(8,128)(2,1)} custom-call(s32[1]{0:T(128)} %bitcast.me_ref, s32[32]{0:T(128)} %pool_ref.7, s32[1,8]{1,0:T(1,128)} %copy-done.16, s32[1,8]{1,0:T(1,128)} %copy-done.15, s32[1,8]{1,0:T(1,128)} %copy-done.14, bf16[8,64,1024]{2,1,0:T(8,128)(2,1)} %own_ref.3), custom_call_target="tpu_custom_call" | custom-call | bytes 3145728 | tf_op jit(solution)/shard_map/adapters_to_send/pallas_call | solution.py:111
  100.9 5.1 %collective-permute-done.9.refs_6_ = bf16[1,1024,256]{2,1,0:T(8,128)(2,1)} collective-permute-done((bf16[1,1024,256]{2,1,0:T(8,128)(2,1)S(1)}, bf16[1,1024,256]{2,1,0:T(8,128)(2,1)}, u32[]{:S(2)}, u32[]{:S(2)}) %collective-permute-start.9) | collective-permute-done | bytes 524320 | tf_op jit(solution)/shard_map/ppermute | solution.py:320
  106.1 2.6 %collective-permute-done.10.refs_7_ = bf16[1,1024,256]{2,1,0:T(8,128)(2,1)} collective-permute-done((bf16[1,1024,256]{2,1,0:T(8,128)(2,1)S(1)}, bf16[1,1024,256]{2,1,0:T(8,128)(2,1)}, u32[]{:S(2)}, u32[]{:S(2)}) %collective-permute-start.10) | collective-permute-done | bytes 524320 | tf_op jit(solution)/shard_map/ppermute | solution.py:320
  108.7 2.5 %copy-done.1 = bf16[1024,2560]{1,0:T(8,128)(2,1)S(1)} copy-done((bf16[1024,2560]{1,0:T(8,128)(2,1)S(1)}, bf16[1024,2560]{1,0:T(8,128)(2,1)}, u32[]{:S(2)}) %copy-start.1) | copy-done | bytes 5242904
  111.2 9.1 %base_products.15 = (bf16[1,1024,256]{2,1,0:T(8,128)(2,1)}, bf16[1,1024,256]{2,1,0:T(8,128)(2,1)S(1)}, bf16[1,1024,256]{2,1,0:T(8,128)(2,1)S(1)}, bf16[1,1024,256]{2,1,0:T(8,128)(2,1)S(1)}) custom-call(s32[4]{0:T(128)S(1)} %get-tuple-element.54.order_ref, bf16[1024,2560]{1,0:T(8,128)(2,1)S(1)} %copy-done.1, bf16[2560,8192]{1,0:T(8,128)(2,1)} %weight_ref.15, ...), custom_call_target="tpu_custom_call" | custom-call | flops 5368709120 | bytes 12582912 | tf_op jit(solution)/shard_map/base_products/pallas_call | solution.py:66
  120.2 0.8 copy-done.5
  121.0 11.9 %all-to-all-done.got_ref = bf16[4,4,64,2560]{3,2,1,0:T(8,128)(2,1)} async-done(((bf16[4,4,64,2560]{3,2,1,0:T(8,128)(2,1)}), bf16[4,4,64,2560]{3,2,1,0:T(8,128)(2,1)}, u32[]{:S(2)}, u32[]{:S(2)}) %all-to-all-start) | async-done | bytes 5242912 | tf_op jit(solution)/shard_map/all_to_all | solution.py:293
  132.9 4.5 %all-to-all-start.1 = ((bf16[4,4,64,1024]{3,2,1,0:T(8,128)(2,1)}), bf16[4,4,64,1024]{3,2,1,0:T(8,128)(2,1)}, u32[]{:S(2)}, u32[]{:S(2)}) async-start(bf16[4,4,64,1024]{3,2,1,0:T(8,128)(2,1)} %adapters_to_send.3), calls=%async_computation.1 | async-start | bytes 4194304 | tf_op jit(solution)/shard_map/all_to_all | solution.py:293
  137.4 2.5 %collective-permute-start.14 = (bf16[1,1024,256]{2,1,0:T(8,128)(2,1)S(1)}, bf16[1,1024,256]{2,1,0:T(8,128)(2,1)}, u32[]{:S(2)}, u32[]{:S(2)}) collective-permute-start(bf16[1,1024,256]{2,1,0:T(8,128)(2,1)S(1)} %get-tuple-element.52), channel_id=1, source_target_pairs={{0,6},{1,7},{2,4},{3,5},{4,2},{5,3},{6,0},{7,1},{8,14},{9,15},{10,... | collective-permute-start | bytes 1572872 | tf_op jit(solution)/shard_map/ppermute | solution.py:320
  140.9 2.4 %collective-permute-start.18 = (bf16[1,1024,256]{2,1,0:T(8,128)(2,1)S(1)}, bf16[1,1024,256]{2,1,0:T(8,128)(2,1)}, u32[]{:S(2)}, u32[]{:S(2)}) collective-permute-start(bf16[1,1024,256]{2,1,0:T(8,128)(2,1)S(1)} %get-tuple-element.58), channel_id=1, source_target_pairs={{0,6},{1,7},{2,4},{3,5},{4,2},{5,3},{6,0},{7,1},{8,14},{9,15},{10,... | collective-permute-start | bytes 1572872 | tf_op jit(solution)/shard_map/ppermute | solution.py:320
  143.4 6.5 %rank_values.1 = bf16[8,64,128]{2,1,0:T(8,128)(2,1)} custom-call(s32[1]{0:T(128)} %bitcast.me_ref, s32[32]{0:T(128)} %pool_ref.7, s32[1,8]{1,0:T(1,128)} %bitcast.7, bf16[1024,2560]{1,0:T(8,128)(2,1)} %hidden_ref.17, bf16[8,64,2560]{2,1,0:T(8,128)(2,1)} %own_ref.2, bf16[4,4,64,2560]{3,2,1,0:T(8,128)(2,1)} %all-to-all-done.got_ref), custom_call_target="tpu_custom_call" | custom-call | flops 335544320 | bytes 7864320 | tf_op jit(solution)/shard_map/rank_values/pallas_call | solution.py:164
  149.9 1.5 collective-permute-done.19
  151.5 0.9 add.25.refs_4_
  153.3 1.5 collective-permute-start.21
  154.9 9.8 %collective-permute-done.16.refs_1_ = bf16[1,1024,256]{2,1,0:T(8,128)(2,1)} collective-permute-done((bf16[1,1024,256]{2,1,0:T(8,128)(2,1)}, bf16[1,1024,256]{2,1,0:T(8,128)(2,1)}, u32[]{:S(2)}, u32[]{:S(2)}) %collective-permute-start.16) | collective-permute-done | bytes 524320 | tf_op jit(solution)/shard_map/ppermute | solution.py:320
  164.6 1.5 collective-permute-start.20
  166.1 5.2 %base_sum.2.base_ref = f32[1024,768]{1,0:T(8,128)} custom-call(bf16[1,1024,256]{2,1,0:T(8,128)(2,1)} %copy-done.2, bf16[1,1024,256]{2,1,0:T(8,128)(2,1)} %copy-done.6, bf16[1,1024,256]{2,1,0:T(8,128)(2,1)} %copy-done.7, bf16[1,1024,256]{2,1,0:T(8,128)(2,1)} %copy-done.8, bf16[1,1024,256]{2,1,0:T(8,128)(2,1)} %copy-done.3, bf16[1,1024,256]{2,1,0:T(8,128)(2,1)} %copy-done.9, ...), custom_call_target="tpu_custom_call" | custom-call | flops 3145728 | bytes 9437184 | tf_op jit(solution)/shard_map/base_sum/pallas_call | solution.py:213
  171.3 4.6 %collective-permute-done.18.refs_3_ = bf16[1,1024,256]{2,1,0:T(8,128)(2,1)} collective-permute-done((bf16[1,1024,256]{2,1,0:T(8,128)(2,1)S(1)}, bf16[1,1024,256]{2,1,0:T(8,128)(2,1)}, u32[]{:S(2)}, u32[]{:S(2)}) %collective-permute-start.18) | collective-permute-done | bytes 524320 | tf_op jit(solution)/shard_map/ppermute | solution.py:320
  175.9 2.2 %collective-permute-done.22.refs_7_ = bf16[8,64,128]{2,1,0:T(8,128)(2,1)S(1)} collective-permute-done((bf16[8,64,128]{2,1,0:T(8,128)(2,1)S(1)}, bf16[8,64,128]{2,1,0:T(8,128)(2,1)S(1)}, u32[]{:S(2)}, u32[]{:S(2)}) %collective-permute-start.22) | collective-permute-done | bytes 131104 | tf_op jit(solution)/shard_map/ppermute | solution.py:328
  178.0 1.3 collective-permute-done.21.refs_6_
  180.0 0.7 copy-done.13
  180.6 2.7 %base_sum.3 = (f32[1024,256]{1,0:T(8,128)}, bf16[8,128,64]{2,1,0:T(8,128)(2,1)}) custom-call(bf16[1,1024,256]{2,1,0:T(8,128)(2,1)} %copy-done.5, bf16[1,1024,256]{2,1,0:T(8,128)(2,1)} %collective-permute-done.16.refs_1_, bf16[1,1024,256]{2,1,0:T(8,128)(2,1)} %collective-permute-done.17.refs_2_, bf16[1,1024,256]{2,1,0:T(8,128)(2,1)} %collective-permute-done.18.refs_3_, ...), custom_call_target="tpu_custom_call" | custom-call | flops 1048576 | bytes 3145728 | tf_op jit(solution)/shard_map/base_sum/pallas_call | solution.py:213
  183.3 1.8 all-to-all-done.1.got_ref
  185.1 5.5 %adapted_and_sum.1 = bf16[1024,1024]{1,0:T(8,128)(2,1)} custom-call(s32[1]{0:T(128)} %bitcast.me_ref, s32[32]{0:T(128)} %pool_ref.7, s32[1,8]{1,0:T(1,128)} %bitcast.8, f32[1024,768]{1,0:T(8,128)} %base_sum.2.base_ref, f32[1024,256]{1,0:T(8,128)} %get-tuple-element.60.last_ref, bf16[8,128,64]{2,1,0:T(8,128)(2,1)} %get-tuple-element.61.rank_ref, ...), custom_call_target="tpu_custom_call" | custom-call | flops 134217728 | bytes 6291456 | tf_op jit(solution)/shard_map/adapted_and_sum/pallas_call | solution.py:250
  (59 shorter events, 4.6 us)
Async XLA Ops:
  0.0 6.7 %collective-permute-start.2 = (s32[1,8]{1,0:T(1,128)}, s32[1,8]{1,0:T(1,128)S(1)}, u32[]{:S(2)}, u32[]{:S(2)}) collective-permute-start(s32[1,8]{1,0:T(1,128)} %bitcast.4), channel_id=1, source_target_pairs={{0,24},{8,16},{16,8},{24,0},{1,25},{9,17},{17,9},{25,1},{2,26},{10... | collective-permute-start | bytes 104 | tf_op jit(solution)/shard_map/ppermute | solution.py:290
  5.0 4.6 %collective-permute-start.1 = (s32[1,8]{1,0:T(1,128)}, s32[1,8]{1,0:T(1,128)S(1)}, u32[]{:S(2)}, u32[]{:S(2)}) collective-permute-start(s32[1,8]{1,0:T(1,128)} %bitcast.5), channel_id=1, source_target_pairs={{0,16},{8,24},{16,0},{24,8},{1,17},{9,25},{17,1},{25,9},{2,18},{10... | collective-permute-start | bytes 104 | tf_op jit(solution)/shard_map/ppermute | solution.py:290
  5.1 4.6 %collective-permute-start = (s32[1,8]{1,0:T(1,128)}, s32[1,8]{1,0:T(1,128)S(1)}, u32[]{:S(2)}, u32[]{:S(2)}) collective-permute-start(s32[1,8]{1,0:T(1,128)} %bitcast.6), channel_id=1, source_target_pairs={{0,8},{8,0},{16,24},{24,16},{1,9},{9,1},{17,25},{25,17},{2,10},{10... | collective-permute-start | bytes 104 | tf_op jit(solution)/shard_map/ppermute | solution.py:290
  6.7 2.9 %copy-start.14 = (s32[1,8]{1,0:T(1,128)}, s32[1,8]{1,0:T(1,128)S(1)}, u32[]{:S(2)}) copy-start(s32[1,8]{1,0:T(1,128)S(1)} %collective-permute-done.2.refs_2_) | copy-start | bytes 100
  9.6 0.6 copy-start.15
  9.6 0.6 copy-start.16
  13.3 5.1 %copy-start.17 = (s32[4]{0:T(128)S(1)}, s32[4]{0:T(128)}, u32[]{:S(2)}) copy-start(s32[4]{0:T(128)} %constant.36.clone) | copy-start | bytes 52
  13.3 119.6 %all-to-all-start = ((bf16[4,4,64,2560]{3,2,1,0:T(8,128)(2,1)}), bf16[4,4,64,2560]{3,2,1,0:T(8,128)(2,1)}, u32[]{:S(2)}, u32[]{:S(2)}) async-start(bf16[4,4,64,2560]{3,2,1,0:T(8,128)(2,1)} %adapters_to_send.2), calls=%async_computation | async-start | bytes 10485760 | tf_op jit(solution)/shard_map/all_to_all | solution.py:293
  18.4 2.5 %copy-start = (bf16[1024,2560]{1,0:T(8,128)(2,1)S(1)}, bf16[1024,2560]{1,0:T(8,128)(2,1)}, u32[]{:S(2)}) copy-start(bf16[1024,2560]{1,0:T(8,128)(2,1)} %hidden_ref.17) | copy-start | bytes 15728644
  20.9 17.1 %slice-start = ((s8[5242880]{0:T(1024)(128)(4,1)}), s8[4194304]{0:T(1024)(128)(4,1)S(1)}, s32[]{:S(2)}) async-start(s8[5242880]{0:T(1024)(128)(4,1)} %bitcast.2), calls=%async_computation.2 | async-start | bytes 8388608
  29.3 8.7 %slice-start.1 = ((s8[5242880]{0:T(1024)(128)(4,1)}), s8[1048576]{0:T(1024)(128)(4,1)S(1)}, s32[]{:S(2)}) async-start(s8[5242880]{0:T(1024)(128)(4,1)} %bitcast.2), calls=%async_computation.3 | async-start | bytes 2097152
  29.3 8.7 %collective-permute-start.3 = (bf16[4,1024,256]{2,1,0:T(8,128)(2,1)S(1)}, bf16[4,1024,256]{2,1,0:T(8,128)(2,1)S(1)}, u32[]{:S(2)}, u32[]{:S(2)}) collective-permute-start(bf16[4,1024,256]{2,1,0:T(8,128)(2,1)S(1)} %base_products.8), channel_id=1, source_target_pairs={{0,1},{1,0},{2,3},{3,2},{4,5},{5,4},{6,7},{7,6},{8,9},{9,8},{10,11... | collective-permute-start | bytes 6291464 | tf_op jit(solution)/shard_map/ppermute | solution.py:306
  37.4 20.5 %collective-permute-start.7 = (bf16[4,1024,256]{2,1,0:T(8,128)(2,1)S(1)}, bf16[4,1024,256]{2,1,0:T(8,128)(2,1)S(1)}, u32[]{:S(2)}, u32[]{:S(2)}) collective-permute-start(bf16[4,1024,256]{2,1,0:T(8,128)(2,1)S(1)} %base_products.9), channel_id=1, source_target_pairs={{0,1},{1,0},{2,3},{3,2},{4,5},{5,4},{6,7},{7,6},{8,9},{9,8},{10,11... | collective-permute-start | bytes 6291464 | tf_op jit(solution)/shard_map/ppermute | solution.py:306
  46.2 11.6 %copy-start.2 = (bf16[1,1024,256]{2,1,0:T(8,128)(2,1)}, bf16[1,1024,256]{2,1,0:T(8,128)(2,1)S(1)}, u32[]{:S(2)}) copy-start(bf16[1,1024,256]{2,1,0:T(8,128)(2,1)S(1)} %get-tuple-element.37.refs_0_) | copy-start | bytes 1572868
  46.2 19.9 %collective-permute-start.4 = (bf16[1,1024,256]{2,1,0:T(8,128)(2,1)S(1)}, bf16[1,1024,256]{2,1,0:T(8,128)(2,1)S(1)}, u32[]{:S(2)}, u32[]{:S(2)}) collective-permute-start(bf16[1,1024,256]{2,1,0:T(8,128)(2,1)S(1)} %get-tuple-element.38), channel_id=1, source_target_pairs={{0,2},{1,3},{2,0},{3,1},{4,6},{5,7},{6,4},{7,5},{8,10},{9,11},{10,... | collective-permute-start | bytes 1572872 | tf_op jit(solution)/shard_map/ppermute | solution.py:320
  47.7 24.8 %collective-permute-start.5 = (bf16[1,1024,256]{2,1,0:T(8,128)(2,1)S(1)}, bf16[1,1024,256]{2,1,0:T(8,128)(2,1)S(1)}, u32[]{:S(2)}, u32[]{:S(2)}) collective-permute-start(bf16[1,1024,256]{2,1,0:T(8,128)(2,1)S(1)} %get-tuple-element.39), channel_id=1, source_target_pairs={{0,4},{1,5},{2,6},{3,7},{4,0},{5,1},{6,2},{7,3},{8,12},{9,13},{10,... | collective-permute-start | bytes 1572872 | tf_op jit(solution)/shard_map/ppermute | solution.py:320
  49.3 23.3 %collective-permute-start.6 = (bf16[1,1024,256]{2,1,0:T(8,128)(2,1)S(1)}, bf16[1,1024,256]{2,1,0:T(8,128)(2,1)S(1)}, u32[]{:S(2)}, u32[]{:S(2)}) collective-permute-start(bf16[1,1024,256]{2,1,0:T(8,128)(2,1)S(1)} %get-tuple-element.40), channel_id=1, source_target_pairs={{0,6},{1,7},{2,4},{3,5},{4,2},{5,3},{6,0},{7,1},{8,14},{9,15},{10,... | collective-permute-start | bytes 1572872 | tf_op jit(solution)/shard_map/ppermute | solution.py:320
  57.8 27.3 %collective-permute-start.11 = (bf16[4,1024,256]{2,1,0:T(8,128)(2,1)S(1)}, bf16[4,1024,256]{2,1,0:T(8,128)(2,1)S(1)}, u32[]{:S(2)}, u32[]{:S(2)}) collective-permute-start(bf16[4,1024,256]{2,1,0:T(8,128)(2,1)S(1)} %base_products.11), channel_id=1, source_target_pairs={{0,1},{1,0},{2,3},{3,2},{4,5},{5,4},{6,7},{7,6},{8,9},{9,8},{10,11... | collective-permute-start | bytes 6291464 | tf_op jit(solution)/shard_map/ppermute | solution.py:306
  66.1 15.3 %copy-start.3 = (bf16[1,1024,256]{2,1,0:T(8,128)(2,1)}, bf16[1,1024,256]{2,1,0:T(8,128)(2,1)S(1)}, u32[]{:S(2)}) copy-start(bf16[1,1024,256]{2,1,0:T(8,128)(2,1)S(1)} %get-tuple-element.43.refs_4_) | copy-start | bytes 1572868
  66.1 15.3 %copy-start.6 = (bf16[1,1024,256]{2,1,0:T(8,128)(2,1)}, bf16[1,1024,256]{2,1,0:T(8,128)(2,1)S(1)}, u32[]{:S(2)}) copy-start(bf16[1,1024,256]{2,1,0:T(8,128)(2,1)S(1)} %collective-permute-done.4.refs_1_) | copy-start | bytes 1572868
  72.6 8.9 %copy-start.7 = (bf16[1,1024,256]{2,1,0:T(8,128)(2,1)}, bf16[1,1024,256]{2,1,0:T(8,128)(2,1)S(1)}, u32[]{:S(2)}) copy-start(bf16[1,1024,256]{2,1,0:T(8,128)(2,1)S(1)} %collective-permute-done.5.refs_2_) | copy-start | bytes 1572868
  72.6 8.9 %copy-start.8 = (bf16[1,1024,256]{2,1,0:T(8,128)(2,1)}, bf16[1,1024,256]{2,1,0:T(8,128)(2,1)S(1)}, u32[]{:S(2)}) copy-start(bf16[1,1024,256]{2,1,0:T(8,128)(2,1)S(1)} %collective-permute-done.6.refs_3_) | copy-start | bytes 1572868
  81.5 27.2 %collective-permute-start.15 = (bf16[4,1024,256]{2,1,0:T(8,128)(2,1)}, bf16[4,1024,256]{2,1,0:T(8,128)(2,1)}, u32[]{:S(2)}, u32[]{:S(2)}) collective-permute-start(bf16[4,1024,256]{2,1,0:T(8,128)(2,1)} %base_products.13), channel_id=1, source_target_pairs={{0,1},{1,0},{2,3},{3,2},{4,5},{5,4},{6,7},{7,6},{8,9},{9,8},{10,11... | collective-permute-start | bytes 6291464 | tf_op jit(solution)/shard_map/ppermute | solution.py:306
  81.5 14.9 %collective-permute-start.8 = (bf16[1,1024,256]{2,1,0:T(8,128)(2,1)S(1)}, bf16[1,1024,256]{2,1,0:T(8,128)(2,1)S(1)}, u32[]{:S(2)}, u32[]{:S(2)}) collective-permute-start(bf16[1,1024,256]{2,1,0:T(8,128)(2,1)S(1)} %get-tuple-element.44), channel_id=1, source_target_pairs={{0,2},{1,3},{2,0},{3,1},{4,6},{5,7},{6,4},{7,5},{8,10},{9,11},{10,... | collective-permute-start | bytes 1572872 | tf_op jit(solution)/shard_map/ppermute | solution.py:320
  82.8 23.2 %collective-permute-start.9 = (bf16[1,1024,256]{2,1,0:T(8,128)(2,1)S(1)}, bf16[1,1024,256]{2,1,0:T(8,128)(2,1)}, u32[]{:S(2)}, u32[]{:S(2)}) collective-permute-start(bf16[1,1024,256]{2,1,0:T(8,128)(2,1)S(1)} %get-tuple-element.45), channel_id=1, source_target_pairs={{0,4},{1,5},{2,6},{3,7},{4,0},{5,1},{6,2},{7,3},{8,12},{9,13},{10,... | collective-permute-start | bytes 1572872 | tf_op jit(solution)/shard_map/ppermute | solution.py:320
  83.7 25.0 %collective-permute-start.10 = (bf16[1,1024,256]{2,1,0:T(8,128)(2,1)S(1)}, bf16[1,1024,256]{2,1,0:T(8,128)(2,1)}, u32[]{:S(2)}, u32[]{:S(2)}) collective-permute-start(bf16[1,1024,256]{2,1,0:T(8,128)(2,1)S(1)} %get-tuple-element.46), channel_id=1, source_target_pairs={{0,6},{1,7},{2,4},{3,5},{4,2},{5,3},{6,0},{7,1},{8,14},{9,15},{10,... | collective-permute-start | bytes 1572872 | tf_op jit(solution)/shard_map/ppermute | solution.py:320
  94.4 0.8 copy-start.4
  95.2 25.8 %collective-permute-start.12 = (bf16[1,1024,256]{2,1,0:T(8,128)(2,1)}, bf16[1,1024,256]{2,1,0:T(8,128)(2,1)}, u32[]{:S(2)}, u32[]{:S(2)}) collective-permute-start(bf16[1,1024,256]{2,1,0:T(8,128)(2,1)} %get-tuple-element.50), channel_id=1, source_target_pairs={{0,2},{1,3},{2,0},{3,1},{4,6},{5,7},{6,4},{7,5},{8,10},{9,11},{10,... | collective-permute-start | bytes 1572872 | tf_op jit(solution)/shard_map/ppermute | solution.py:320
  96.5 0.8 copy-start.9
  97.2 23.8 %collective-permute-start.13 = (bf16[1,1024,256]{2,1,0:T(8,128)(2,1)}, bf16[1,1024,256]{2,1,0:T(8,128)(2,1)}, u32[]{:S(2)}, u32[]{:S(2)}) collective-permute-start(bf16[1,1024,256]{2,1,0:T(8,128)(2,1)} %get-tuple-element.51), channel_id=1, source_target_pairs={{0,4},{1,5},{2,6},{3,7},{4,0},{5,1},{6,2},{7,3},{8,12},{9,13},{10,... | collective-permute-start | bytes 1572872 | tf_op jit(solution)/shard_map/ppermute | solution.py:320
  108.7 2.5 %copy-start.1 = (bf16[1024,2560]{1,0:T(8,128)(2,1)S(1)}, bf16[1024,2560]{1,0:T(8,128)(2,1)}, u32[]{:S(2)}) copy-start(bf16[1024,2560]{1,0:T(8,128)(2,1)} %hidden_ref.17) | copy-start | bytes 15728644
  120.2 0.8 copy-start.5
  132.9 52.2 %all-to-all-start.1 = ((bf16[4,4,64,1024]{3,2,1,0:T(8,128)(2,1)}), bf16[4,4,64,1024]{3,2,1,0:T(8,128)(2,1)}, u32[]{:S(2)}, u32[]{:S(2)}) async-start(bf16[4,4,64,1024]{3,2,1,0:T(8,128)(2,1)} %adapters_to_send.3), calls=%async_computation.1 | async-start | bytes 4194304 | tf_op jit(solution)/shard_map/all_to_all | solution.py:293
  137.4 16.0 %collective-permute-start.14 = (bf16[1,1024,256]{2,1,0:T(8,128)(2,1)S(1)}, bf16[1,1024,256]{2,1,0:T(8,128)(2,1)}, u32[]{:S(2)}, u32[]{:S(2)}) collective-permute-start(bf16[1,1024,256]{2,1,0:T(8,128)(2,1)S(1)} %get-tuple-element.52), channel_id=1, source_target_pairs={{0,6},{1,7},{2,4},{3,5},{4,2},{5,3},{6,0},{7,1},{8,14},{9,15},{10,... | collective-permute-start | bytes 1572872 | tf_op jit(solution)/shard_map/ppermute | solution.py:320
  139.9 24.8 %collective-permute-start.16 = (bf16[1,1024,256]{2,1,0:T(8,128)(2,1)}, bf16[1,1024,256]{2,1,0:T(8,128)(2,1)}, u32[]{:S(2)}, u32[]{:S(2)}) collective-permute-start(bf16[1,1024,256]{2,1,0:T(8,128)(2,1)} %get-tuple-element.56), channel_id=1, source_target_pairs={{0,2},{1,3},{2,0},{3,1},{4,6},{5,7},{6,4},{7,5},{8,10},{9,11},{10,... | collective-permute-start | bytes 1572872 | tf_op jit(solution)/shard_map/ppermute | solution.py:320
  140.4 30.9 %collective-permute-start.17 = (bf16[1,1024,256]{2,1,0:T(8,128)(2,1)S(1)}, bf16[1,1024,256]{2,1,0:T(8,128)(2,1)}, u32[]{:S(2)}, u32[]{:S(2)}) collective-permute-start(bf16[1,1024,256]{2,1,0:T(8,128)(2,1)S(1)} %get-tuple-element.57), channel_id=1, source_target_pairs={{0,4},{1,5},{2,6},{3,7},{4,0},{5,1},{6,2},{7,3},{8,12},{9,13},{10,... | collective-permute-start | bytes 1572872 | tf_op jit(solution)/shard_map/ppermute | solution.py:320
  140.9 34.9 %collective-permute-start.18 = (bf16[1,1024,256]{2,1,0:T(8,128)(2,1)S(1)}, bf16[1,1024,256]{2,1,0:T(8,128)(2,1)}, u32[]{:S(2)}, u32[]{:S(2)}) collective-permute-start(bf16[1,1024,256]{2,1,0:T(8,128)(2,1)S(1)} %get-tuple-element.58), channel_id=1, source_target_pairs={{0,6},{1,7},{2,4},{3,5},{4,2},{5,3},{6,0},{7,1},{8,14},{9,15},{10,... | collective-permute-start | bytes 1572872 | tf_op jit(solution)/shard_map/ppermute | solution.py:320
  149.8 1.6 collective-permute-start.19
  152.4 18.9 %copy-start.10 = (bf16[8,64,128]{2,1,0:T(8,128)(2,1)}, bf16[8,64,128]{2,1,0:T(8,128)(2,1)S(1)}, u32[]{:S(2)}) copy-start(bf16[8,64,128]{2,1,0:T(8,128)(2,1)S(1)} %add.25.refs_4_) | copy-start | bytes 393220
  152.4 25.6 %collective-permute-start.22 = (bf16[8,64,128]{2,1,0:T(8,128)(2,1)S(1)}, bf16[8,64,128]{2,1,0:T(8,128)(2,1)S(1)}, u32[]{:S(2)}, u32[]{:S(2)}) collective-permute-start(bf16[8,64,128]{2,1,0:T(8,128)(2,1)S(1)} %add.25.refs_4_), channel_id=1, source_target_pairs={{0,6},{1,7},{2,4},{3,5},{4,2},{5,3},{6,0},{7,1},{8,14},{9,15},{10,... | collective-permute-start | bytes 393224 | tf_op jit(solution)/shard_map/ppermute | solution.py:328
  153.3 26.0 %collective-permute-start.21 = (bf16[8,64,128]{2,1,0:T(8,128)(2,1)S(1)}, bf16[8,64,128]{2,1,0:T(8,128)(2,1)S(1)}, u32[]{:S(2)}, u32[]{:S(2)}) collective-permute-start(bf16[8,64,128]{2,1,0:T(8,128)(2,1)S(1)} %add.25.refs_4_), channel_id=1, source_target_pairs={{0,4},{1,5},{2,6},{3,7},{4,0},{5,1},{6,2},{7,3},{8,12},{9,13},{10,... | collective-permute-start | bytes 393224 | tf_op jit(solution)/shard_map/ppermute | solution.py:328
  164.6 14.8 %collective-permute-start.20 = (bf16[8,64,128]{2,1,0:T(8,128)(2,1)S(1)}, bf16[8,64,128]{2,1,0:T(8,128)(2,1)S(1)}, u32[]{:S(2)}, u32[]{:S(2)}) collective-permute-start(bf16[8,64,128]{2,1,0:T(8,128)(2,1)S(1)} %add.25.refs_4_), channel_id=1, source_target_pairs={{0,2},{1,3},{2,0},{3,1},{4,6},{5,7},{6,4},{7,5},{8,10},{9,11},{10,... | collective-permute-start | bytes 393224 | tf_op jit(solution)/shard_map/ppermute | solution.py:328
  178.0 1.4 copy-start.11
  179.3 0.7 copy-start.12
  180.0 0.7 copy-start.13

commit v5 on v4

--- a/solution.py
+++ b/solution.py
@@ -185,7 +185,7 @@
         value = adds[c * n_add][0].astype(jnp.float32)
         for add in adds[c * n_add + 1 : (c + 1) * n_add]:
             value = value + add[0].astype(jnp.float32)
-        out_ref[:, pl.ds(c * width, width)] = value
+        out_ref[:, pl.ds(c * width, width)] = value.astype(out_ref.dtype)
     if len(refs) > n_add * chunks + 1:
         ranks, rank_ref = refs[n_add * chunks : -2], refs[-1]
         for t in range(rank_ref.shape[0]):
@@ -201,7 +201,7 @@
     steps = tiles // per_step
     rows = tokens // steps
     width = n_cols * len(adds)
-    out_shape = [jax.ShapeDtypeStruct((tokens, width), jnp.float32)]
+    out_shape = [jax.ShapeDtypeStruct((tokens, width), jnp.bfloat16)]
     out_specs = [pl.BlockSpec((rows, width), lambda i: (i, 0))]
     rank_specs = []
     for part in ranks:
@@ -217,7 +217,7 @@
         in_specs=[pl.BlockSpec((1, rows, n_cols), lambda i: (0, i, 0))] * len(flat) + rank_specs,
         out_specs=out_specs,
         compiler_params=params(62),
-        cost_estimate=cost(tokens * n_cols * len(flat), tokens * (2 * n_cols * len(flat) + 4 * width)),
+        cost_estimate=cost(tokens * n_cols * len(flat), tokens * (2 * n_cols * len(flat) + 2 * width)),
         name="base_sum",
     )(*flat, *ranks)
 
@@ -237,8 +237,8 @@
         pltpu.make_async_copy(own_ref.at[0], held.at[tile], sems.at[tile]).wait()
         adapted = jnp.dot(rank_ref[t], held[tile], preferred_element_type=jnp.float32)
         adapted = (adapter_scale * adapted).astype(jnp.bfloat16).astype(jnp.float32)
-        out_ref[span, pl.ds(0, summed)] = (base_ref[span, :] + adapted[:, :summed]).astype(jnp.bfloat16)
-        rest = last_ref[span, :] + adapted[:, summed:]
+        out_ref[span, pl.ds(0, summed)] = (base_ref[span, :].astype(jnp.float32) + adapted[:, :summed]).astype(jnp.bfloat16)
+        rest = last_ref[span, :].astype(jnp.float32) + adapted[:, summed:]
         out_ref[span, pl.ds(summed, rest.shape[1])] = rest.astype(jnp.bfloat16)
 
 
@@ -261,7 +261,7 @@
             pltpu.SemaphoreType.DMA((tiles,)),
         ],
         compiler_params=params(62),
-        cost_estimate=cost(2 * tiles * rows * rank * width, 6 * tiles * rows * width),
+        cost_estimate=cost(2 * tiles * rows * rank * width, 4 * tiles * rows * width),
         name="adapted_and_sum",
     )(me, pool, table, base, last, ranks, own, got)
 

time: 191 us -> 192 us (level)
  no operation moved by 1% of the time
where the time goes in v5:
time: 192 us; the launch traced here: 191 us
  Pallas kernels  93.8 us (49%)
  waiting for transfers between devices  51.6 us (27%)
  starting transfers between devices  35.3 us (18%)
  local copies, waits for them, and re-layouts  9.14 us (5%)
    pallas_call x8, Pallas kernels, gemm(): pl.pallas_call(functools.partial(gemm_kernel, len(adds), n_out, per_out,...  68.1 us
    ppermute x12, waiting for transfers between devices, local(): lax.ppermute(sums[r - 1], 'tp', [(i, i ^ 2 * r) for i in range(n_tp)])  28.7 us
    ppermute x12, starting transfers between devices, local(): lax.ppermute(sums[r - 1], 'tp', [(i, i ^ 2 * r) for i in range(n_tp)])  15.7 us
    all_to_all x2, waiting for transfers between devices, send(): return lax.all_to_all(v, 'grp', 0, 0, tiled=True)  13.8 us
    all_to_all x2, starting transfers between devices, send(): return lax.all_to_all(v, 'grp', 0, 0, tiled=True)  9.56 us
    unnamed x40, local copies, waits for them, and re-layouts  9.14 us
    pallas_call x2, Pallas kernels, sum_base(): pl.pallas_call(functools.partial(sum_kernel, len(adds[0]), len(adds)), ou...  7.4 us
    pallas_call x2, Pallas kernels, route(): pl.pallas_call(functools.partial(route_kernel, per_owner), out_shape=jax....  6.71 us
  transfers between devices with their start and end apart: 25, of which 14 were waited for; matrix products, arithmetic and copies ran while one was open for 0% of the time, Pallas kernels for 44%

profile of v5, /device:TPU:0, one launch (start us, length us, event | category | flops | bytes accessed | tf_op | source)
XLA Modules:
  0.0 191.3 jit_solution(11148941627718250626)
XLA Ops:
  0.0 5.0 %collective-permute-start.2 = (s32[1,8]{1,0:T(1,128)}, s32[1,8]{1,0:T(1,128)S(1)}, u32[]{:S(2)}, u32[]{:S(2)}) collective-permute-start(s32[1,8]{1,0:T(1,128)} %bitcast.4), channel_id=1, source_target_pairs={{0,24},{8,16},{16,8},{24,0},{1,25},{9,17},{17,9},{25,1},{2,26},{10... | collective-permute-start | bytes 104 | tf_op jit(solution)/shard_map/ppermute | solution.py:290
  5.6 1.1 collective-permute-done.2.refs_2_
  6.7 2.9 %collective-permute-done.1.refs_1_ = s32[1,8]{1,0:T(1,128)S(1)} collective-permute-done((s32[1,8]{1,0:T(1,128)}, s32[1,8]{1,0:T(1,128)S(1)}, u32[]{:S(2)}, u32[]{:S(2)}) %collective-permute-start.1) | collective-permute-done | bytes 64 | tf_op jit(solution)/shard_map/ppermute | solution.py:290
  9.6 0.6 copy-done.15
  10.2 4.0 %adapters_to_send.2 = bf16[4,4,64,2560]{3,2,1,0:T(8,128)(2,1)} custom-call(s32[1]{0:T(128)} %bitcast.me_ref, s32[32]{0:T(128)} %pool_ref.7, s32[1,8]{1,0:T(1,128)} %copy-done.16, s32[1,8]{1,0:T(1,128)} %copy-done.15, s32[1,8]{1,0:T(1,128)} %copy-done.14, bf16[8,64,2560]{2,1,0:T(8,128)(2,1)} %own_ref.2), custom_call_target="tpu_custom_call" | custom-call | bytes 7864320 | tf_op jit(solution)/shard_map/adapters_to_send/pallas_call | solution.py:111
  14.2 5.1 %all-to-all-start = ((bf16[4,4,64,2560]{3,2,1,0:T(8,128)(2,1)}), bf16[4,4,64,2560]{3,2,1,0:T(8,128)(2,1)}, u32[]{:S(2)}, u32[]{:S(2)}) async-start(bf16[4,4,64,2560]{3,2,1,0:T(8,128)(2,1)} %adapters_to_send.2), calls=%async_computation | async-start | bytes 10485760 | tf_op jit(solution)/shard_map/all_to_all | solution.py:293
  19.4 2.5 %copy-done = bf16[1024,2560]{1,0:T(8,128)(2,1)S(1)} copy-done((bf16[1024,2560]{1,0:T(8,128)(2,1)S(1)}, bf16[1024,2560]{1,0:T(8,128)(2,1)}, u32[]{:S(2)}) %copy-start) | copy-done | bytes 5242904
  21.9 8.3 %base_products.8 = bf16[4,1024,256]{2,1,0:T(8,128)(2,1)S(1)} custom-call(s32[4]{0:T(128)S(1)} %get-tuple-element.47.order_ref, bf16[1024,2560]{1,0:T(8,128)(2,1)S(1)} %copy-done, bf16[2560,8192]{1,0:T(8,128)(2,1)} %weight_ref.15), custom_call_target="tpu_custom_call" | custom-call | flops 5368709120 | bytes 12582912 | tf_op jit(solution)/shard_map/base_products/pallas_call | solution.py:66
  30.3 8.1 %base_products.9 = bf16[4,1024,256]{2,1,0:T(8,128)(2,1)S(1)} custom-call(s32[4]{0:T(128)S(1)} %get-tuple-element.47.order_ref, bf16[1024,2560]{1,0:T(8,128)(2,1)S(1)} %copy-done, bf16[2560,8192]{1,0:T(8,128)(2,1)} %weight_ref.15), custom_call_target="tpu_custom_call" | custom-call | flops 5368709120 | bytes 12582912 | tf_op jit(solution)/shard_map/base_products/pallas_call | solution.py:66
  38.9 8.2 %base_products.10 = (bf16[1,1024,256]{2,1,0:T(8,128)(2,1)S(1)}, bf16[1,1024,256]{2,1,0:T(8,128)(2,1)S(1)}, bf16[1,1024,256]{2,1,0:T(8,128)(2,1)S(1)}, bf16[1,1024,256]{2,1,0:T(8,128)(2,1)S(1)}) custom-call(s32[4]{0:T(128)S(1)} %get-tuple-element.54.order_ref, bf16[1024,2560]{1,0:T(8,128)(2,1)S(1)} %bitcast.3, bf16[2560,8192]{1,0:T(8,128)(2,1)} %weight_ref.15, ...), custom_call_target="tpu_custom_call" | custom-call | flops 5368709120 | bytes 12582912 | tf_op jit(solution)/shard_map/base_products/pallas_call | solution.py:66
  47.1 1.6 collective-permute-start.4
  48.7 1.5 collective-permute-start.5
  50.7 8.1 %base_products.11 = bf16[4,1024,256]{2,1,0:T(8,128)(2,1)S(1)} custom-call(s32[4]{0:T(128)S(1)} %get-tuple-element.47.order_ref, bf16[1024,2560]{1,0:T(8,128)(2,1)S(1)} %bitcast.3, bf16[2560,8192]{1,0:T(8,128)(2,1)} %weight_ref.15), custom_call_target="tpu_custom_call" | custom-call | flops 5368709120 | bytes 12582912 | tf_op jit(solution)/shard_map/base_products/pallas_call | solution.py:66
  58.8 8.2 %base_products.12 = (bf16[1,1024,256]{2,1,0:T(8,128)(2,1)S(1)}, bf16[1,1024,256]{2,1,0:T(8,128)(2,1)S(1)}, bf16[1,1024,256]{2,1,0:T(8,128)(2,1)S(1)}, bf16[1,1024,256]{2,1,0:T(8,128)(2,1)S(1)}) custom-call(s32[4]{0:T(128)S(1)} %get-tuple-element.54.order_ref, bf16[1024,2560]{1,0:T(8,128)(2,1)S(1)} %bitcast.3, bf16[2560,8192]{1,0:T(8,128)(2,1)} %weight_ref.15, ...), custom_call_target="tpu_custom_call" | custom-call | flops 5368709120 | bytes 12582912 | tf_op jit(solution)/shard_map/base_products/pallas_call | solution.py:66
  67.1 6.4 %collective-permute-done.5.refs_2_ = bf16[1,1024,256]{2,1,0:T(8,128)(2,1)S(1)} collective-permute-done((bf16[1,1024,256]{2,1,0:T(8,128)(2,1)S(1)}, bf16[1,1024,256]{2,1,0:T(8,128)(2,1)S(1)}, u32[]{:S(2)}, u32[]{:S(2)}) %collective-permute-start.5) | collective-permute-done | bytes 524320 | tf_op jit(solution)/shard_map/ppermute | solution.py:320
  73.5 8.9 %base_products.13 = bf16[4,1024,256]{2,1,0:T(8,128)(2,1)} custom-call(s32[4]{0:T(128)S(1)} %get-tuple-element.47.order_ref, bf16[1024,2560]{1,0:T(8,128)(2,1)S(1)} %bitcast.3, bf16[2560,8192]{1,0:T(8,128)(2,1)} %weight_ref.15), custom_call_target="tpu_custom_call" | custom-call | flops 5368709120 | bytes 12582912 | tf_op jit(solution)/shard_map/base_products/pallas_call | solution.py:66
  82.5 1.3 collective-permute-start.8
  83.8 0.8 collective-permute-start.9
  84.6 1.4 collective-permute-start.10
  86.0 9.3 %base_products.14 = (bf16[1,1024,256]{2,1,0:T(8,128)(2,1)}, bf16[1,1024,256]{2,1,0:T(8,128)(2,1)}, bf16[1,1024,256]{2,1,0:T(8,128)(2,1)S(1)}, bf16[1,1024,256]{2,1,0:T(8,128)(2,1)S(1)}) custom-call(s32[4]{0:T(128)S(1)} %get-tuple-element.54.order_ref, bf16[1024,2560]{1,0:T(8,128)(2,1)S(1)} %bitcast.3, bf16[2560,8192]{1,0:T(8,128)(2,1)} %weight_ref.15, ...), custom_call_target="tpu_custom_call" | custom-call | flops 5368709120 | bytes 12582912 | tf_op jit(solution)/shard_map/base_products/pallas_call | solution.py:66
  95.4 0.8 copy-done.5
  96.2 1.2 collective-permute-start.12
  97.4 0.8 copy-done.10
  98.2 1.4 collective-permute-start.13
  99.6 2.7 %adapters_to_send.3 = bf16[4,4,64,1024]{3,2,1,0:T(8,128)(2,1)} custom-call(s32[1]{0:T(128)} %bitcast.me_ref, s32[32]{0:T(128)} %pool_ref.7, s32[1,8]{1,0:T(1,128)} %copy-done.16, s32[1,8]{1,0:T(1,128)} %copy-done.15, s32[1,8]{1,0:T(1,128)} %copy-done.14, bf16[8,64,1024]{2,1,0:T(8,128)(2,1)} %own_ref.3), custom_call_target="tpu_custom_call" | custom-call | bytes 3145728 | tf_op jit(solution)/shard_map/adapters_to_send/pallas_call | solution.py:111
  102.3 4.7 %collective-permute-done.9.refs_6_ = bf16[1,1024,256]{2,1,0:T(8,128)(2,1)} collective-permute-done((bf16[1,1024,256]{2,1,0:T(8,128)(2,1)S(1)}, bf16[1,1024,256]{2,1,0:T(8,128)(2,1)}, u32[]{:S(2)}, u32[]{:S(2)}) %collective-permute-start.9) | collective-permute-done | bytes 524320 | tf_op jit(solution)/shard_map/ppermute | solution.py:320
  107.0 2.6 %collective-permute-done.10.refs_7_ = bf16[1,1024,256]{2,1,0:T(8,128)(2,1)} collective-permute-done((bf16[1,1024,256]{2,1,0:T(8,128)(2,1)S(1)}, bf16[1,1024,256]{2,1,0:T(8,128)(2,1)}, u32[]{:S(2)}, u32[]{:S(2)}) %collective-permute-start.10) | collective-permute-done | bytes 524320 | tf_op jit(solution)/shard_map/ppermute | solution.py:320
  109.6 2.5 %copy-done.1 = bf16[1024,2560]{1,0:T(8,128)(2,1)S(1)} copy-done((bf16[1024,2560]{1,0:T(8,128)(2,1)S(1)}, bf16[1024,2560]{1,0:T(8,128)(2,1)}, u32[]{:S(2)}) %copy-start.1) | copy-done | bytes 5242904
  112.1 9.1 %base_products.15 = (bf16[1,1024,256]{2,1,0:T(8,128)(2,1)}, bf16[1,1024,256]{2,1,0:T(8,128)(2,1)S(1)}, bf16[1,1024,256]{2,1,0:T(8,128)(2,1)S(1)}, bf16[1,1024,256]{2,1,0:T(8,128)(2,1)S(1)}) custom-call(s32[4]{0:T(128)S(1)} %get-tuple-element.54.order_ref, bf16[1024,2560]{1,0:T(8,128)(2,1)S(1)} %copy-done.1, bf16[2560,8192]{1,0:T(8,128)(2,1)} %weight_ref.15, ...), custom_call_target="tpu_custom_call" | custom-call | flops 5368709120 | bytes 12582912 | tf_op jit(solution)/shard_map/base_products/pallas_call | solution.py:66
  121.2 0.8 copy-done.2
  122.0 11.9 %all-to-all-done.got_ref = bf16[4,4,64,2560]{3,2,1,0:T(8,128)(2,1)} async-done(((bf16[4,4,64,2560]{3,2,1,0:T(8,128)(2,1)}), bf16[4,4,64,2560]{3,2,1,0:T(8,128)(2,1)}, u32[]{:S(2)}, u32[]{:S(2)}) %all-to-all-start) | async-done | bytes 5242912 | tf_op jit(solution)/shard_map/all_to_all | solution.py:293
  133.8 4.5 %all-to-all-start.1 = ((bf16[4,4,64,1024]{3,2,1,0:T(8,128)(2,1)}), bf16[4,4,64,1024]{3,2,1,0:T(8,128)(2,1)}, u32[]{:S(2)}, u32[]{:S(2)}) async-start(bf16[4,4,64,1024]{3,2,1,0:T(8,128)(2,1)} %adapters_to_send.3), calls=%async_computation.1 | async-start | bytes 4194304 | tf_op jit(solution)/shard_map/all_to_all | solution.py:293
  138.3 2.5 %collective-permute-start.14 = (bf16[1,1024,256]{2,1,0:T(8,128)(2,1)S(1)}, bf16[1,1024,256]{2,1,0:T(8,128)(2,1)}, u32[]{:S(2)}, u32[]{:S(2)}) collective-permute-start(bf16[1,1024,256]{2,1,0:T(8,128)(2,1)S(1)} %get-tuple-element.52), channel_id=1, source_target_pairs={{0,6},{1,7},{2,4},{3,5},{4,2},{5,3},{6,0},{7,1},{8,14},{9,15},{10,... | collective-permute-start | bytes 1572872 | tf_op jit(solution)/shard_map/ppermute | solution.py:320
  141.9 2.4 %collective-permute-start.18 = (bf16[1,1024,256]{2,1,0:T(8,128)(2,1)S(1)}, bf16[1,1024,256]{2,1,0:T(8,128)(2,1)}, u32[]{:S(2)}, u32[]{:S(2)}) collective-permute-start(bf16[1,1024,256]{2,1,0:T(8,128)(2,1)S(1)} %get-tuple-element.58), channel_id=1, source_target_pairs={{0,6},{1,7},{2,4},{3,5},{4,2},{5,3},{6,0},{7,1},{8,14},{9,15},{10,... | collective-permute-start | bytes 1572872 | tf_op jit(solution)/shard_map/ppermute | solution.py:320
  144.3 6.6 %rank_values.1 = bf16[8,64,128]{2,1,0:T(8,128)(2,1)} custom-call(s32[1]{0:T(128)} %bitcast.me_ref, s32[32]{0:T(128)} %pool_ref.7, s32[1,8]{1,0:T(1,128)} %bitcast.7, bf16[1024,2560]{1,0:T(8,128)(2,1)} %hidden_ref.17, bf16[8,64,2560]{2,1,0:T(8,128)(2,1)} %own_ref.2, bf16[4,4,64,2560]{3,2,1,0:T(8,128)(2,1)} %all-to-all-done.got_ref), custom_call_target="tpu_custom_call" | custom-call | flops 335544320 | bytes 7864320 | tf_op jit(solution)/shard_map/rank_values/pallas_call | solution.py:164
  151.0 1.5 collective-permute-done.19
  152.5 0.9 add.25.refs_4_
  154.3 1.5 collective-permute-start.21
  155.8 9.8 %collective-permute-done.16.refs_1_ = bf16[1,1024,256]{2,1,0:T(8,128)(2,1)} collective-permute-done((bf16[1,1024,256]{2,1,0:T(8,128)(2,1)}, bf16[1,1024,256]{2,1,0:T(8,128)(2,1)}, u32[]{:S(2)}, u32[]{:S(2)}) %collective-permute-start.16) | collective-permute-done | bytes 524320 | tf_op jit(solution)/shard_map/ppermute | solution.py:320
  165.6 1.5 collective-permute-start.20
  167.1 4.8 %base_sum.2.base_ref = bf16[1024,768]{1,0:T(8,128)(2,1)} custom-call(bf16[1,1024,256]{2,1,0:T(8,128)(2,1)} %copy-done.3, bf16[1,1024,256]{2,1,0:T(8,128)(2,1)} %copy-done.7, bf16[1,1024,256]{2,1,0:T(8,128)(2,1)} %copy-done.8, bf16[1,1024,256]{2,1,0:T(8,128)(2,1)} %copy-done.9, bf16[1,1024,256]{2,1,0:T(8,128)(2,1)} %copy-done.4, ...), custom_call_target="tpu_custom_call" | custom-call | flops 3145728 | bytes 7864320 | tf_op jit(solution)/shard_map/base_sum/pallas_call | solution.py:213
  171.9 4.9 %collective-permute-done.18.refs_3_ = bf16[1,1024,256]{2,1,0:T(8,128)(2,1)} collective-permute-done((bf16[1,1024,256]{2,1,0:T(8,128)(2,1)S(1)}, bf16[1,1024,256]{2,1,0:T(8,128)(2,1)}, u32[]{:S(2)}, u32[]{:S(2)}) %collective-permute-start.18) | collective-permute-done | bytes 524320 | tf_op jit(solution)/shard_map/ppermute | solution.py:320
  176.8 2.2 %collective-permute-done.22.refs_7_ = bf16[8,64,128]{2,1,0:T(8,128)(2,1)S(1)} collective-permute-done((bf16[8,64,128]{2,1,0:T(8,128)(2,1)S(1)}, bf16[8,64,128]{2,1,0:T(8,128)(2,1)S(1)}, u32[]{:S(2)}, u32[]{:S(2)}) %collective-permute-start.22) | collective-permute-done | bytes 131104 | tf_op jit(solution)/shard_map/ppermute | solution.py:328
  179.0 1.3 collective-permute-done.21.refs_6_
  180.9 0.7 copy-done.13
  181.6 2.6 %base_sum.3 = (bf16[1024,256]{1,0:T(8,128)(2,1)}, bf16[8,128,64]{2,1,0:T(8,128)(2,1)}) custom-call(bf16[1,1024,256]{2,1,0:T(8,128)(2,1)} %copy-done.2, bf16[1,1024,256]{2,1,0:T(8,128)(2,1)} %collective-permute-done.16.refs_1_, bf16[1,1024,256]{2,1,0:T(8,128)(2,1)} %collective-permute-done.17.refs_2_, bf16[1,1024,256]{2,1,0:T(8,128)(2,1)} %collective-permute-done.18.refs_3_, ...), custom_call_target="tpu_custom_call" | custom-call | flops 1048576 | bytes 2621440 | tf_op jit(solution)/shard_map/base_sum/pallas_call | solution.py:213
  184.1 1.9 %all-to-all-done.1.got_ref = bf16[4,4,64,1024]{3,2,1,0:T(8,128)(2,1)} async-done(((bf16[4,4,64,1024]{3,2,1,0:T(8,128)(2,1)}), bf16[4,4,64,1024]{3,2,1,0:T(8,128)(2,1)}, u32[]{:S(2)}, u32[]{:S(2)}) %all-to-all-start.1) | async-done | bytes 2097184 | tf_op jit(solution)/shard_map/all_to_all | solution.py:293
  186.1 5.1 %adapted_and_sum.1 = bf16[1024,1024]{1,0:T(8,128)(2,1)} custom-call(s32[1]{0:T(128)} %bitcast.me_ref, s32[32]{0:T(128)} %pool_ref.7, s32[1,8]{1,0:T(1,128)} %bitcast.8, bf16[1024,768]{1,0:T(8,128)(2,1)} %base_sum.2.base_ref, bf16[1024,256]{1,0:T(8,128)(2,1)} %get-tuple-element.60.last_ref, bf16[8,128,64]{2,1,0:T(8,128)(2,1)} %get-tuple-element.61.rank_ref, ...), custom_call_target="tpu_custom_call" | custom-call | flops 134217728 | bytes 4194304 | tf_op jit(solution)/shard_map/adapted_and_sum/pallas_call | solution.py:250
  (59 shorter events, 4.5 us)
Async XLA Ops:
  0.0 6.7 %collective-permute-start.2 = (s32[1,8]{1,0:T(1,128)}, s32[1,8]{1,0:T(1,128)S(1)}, u32[]{:S(2)}, u32[]{:S(2)}) collective-permute-start(s32[1,8]{1,0:T(1,128)} %bitcast.4), channel_id=1, source_target_pairs={{0,24},{8,16},{16,8},{24,0},{1,25},{9,17},{17,9},{25,1},{2,26},{10... | collective-permute-start | bytes 104 | tf_op jit(solution)/shard_map/ppermute | solution.py:290
  5.0 4.6 %collective-permute-start.1 = (s32[1,8]{1,0:T(1,128)}, s32[1,8]{1,0:T(1,128)S(1)}, u32[]{:S(2)}, u32[]{:S(2)}) collective-permute-start(s32[1,8]{1,0:T(1,128)} %bitcast.5), channel_id=1, source_target_pairs={{0,16},{8,24},{16,0},{24,8},{1,17},{9,25},{17,1},{25,9},{2,18},{10... | collective-permute-start | bytes 104 | tf_op jit(solution)/shard_map/ppermute | solution.py:290
  5.1 4.6 %collective-permute-start = (s32[1,8]{1,0:T(1,128)}, s32[1,8]{1,0:T(1,128)S(1)}, u32[]{:S(2)}, u32[]{:S(2)}) collective-permute-start(s32[1,8]{1,0:T(1,128)} %bitcast.6), channel_id=1, source_target_pairs={{0,8},{8,0},{16,24},{24,16},{1,9},{9,1},{17,25},{25,17},{2,10},{10... | collective-permute-start | bytes 104 | tf_op jit(solution)/shard_map/ppermute | solution.py:290
  6.7 2.9 %copy-start.14 = (s32[1,8]{1,0:T(1,128)}, s32[1,8]{1,0:T(1,128)S(1)}, u32[]{:S(2)}) copy-start(s32[1,8]{1,0:T(1,128)S(1)} %collective-permute-done.2.refs_2_) | copy-start | bytes 100
  9.6 0.6 copy-start.15
  9.6 0.6 copy-start.16
  14.2 5.1 %copy-start.17 = (s32[4]{0:T(128)S(1)}, s32[4]{0:T(128)}, u32[]{:S(2)}) copy-start(s32[4]{0:T(128)} %constant.36.clone) | copy-start | bytes 52
  14.2 119.6 %all-to-all-start = ((bf16[4,4,64,2560]{3,2,1,0:T(8,128)(2,1)}), bf16[4,4,64,2560]{3,2,1,0:T(8,128)(2,1)}, u32[]{:S(2)}, u32[]{:S(2)}) async-start(bf16[4,4,64,2560]{3,2,1,0:T(8,128)(2,1)} %adapters_to_send.2), calls=%async_computation | async-start | bytes 10485760 | tf_op jit(solution)/shard_map/all_to_all | solution.py:293
  19.4 2.5 %copy-start = (bf16[1024,2560]{1,0:T(8,128)(2,1)S(1)}, bf16[1024,2560]{1,0:T(8,128)(2,1)}, u32[]{:S(2)}) copy-start(bf16[1024,2560]{1,0:T(8,128)(2,1)} %hidden_ref.17) | copy-start | bytes 15728644
  21.9 17.1 %slice-start = ((s8[5242880]{0:T(1024)(128)(4,1)}), s8[4194304]{0:T(1024)(128)(4,1)S(1)}, s32[]{:S(2)}) async-start(s8[5242880]{0:T(1024)(128)(4,1)} %bitcast.2), calls=%async_computation.2 | async-start | bytes 8388608
  30.2 8.7 %slice-start.1 = ((s8[5242880]{0:T(1024)(128)(4,1)}), s8[1048576]{0:T(1024)(128)(4,1)S(1)}, s32[]{:S(2)}) async-start(s8[5242880]{0:T(1024)(128)(4,1)} %bitcast.2), calls=%async_computation.3 | async-start | bytes 2097152
  30.2 8.7 %collective-permute-start.3 = (bf16[4,1024,256]{2,1,0:T(8,128)(2,1)S(1)}, bf16[4,1024,256]{2,1,0:T(8,128)(2,1)S(1)}, u32[]{:S(2)}, u32[]{:S(2)}) collective-permute-start(bf16[4,1024,256]{2,1,0:T(8,128)(2,1)S(1)} %base_products.8), channel_id=1, source_target_pairs={{0,1},{1,0},{2,3},{3,2},{4,5},{5,4},{6,7},{7,6},{8,9},{9,8},{10,11... | collective-permute-start | bytes 6291464 | tf_op jit(solution)/shard_map/ppermute | solution.py:306
  38.4 20.5 %collective-permute-start.7 = (bf16[4,1024,256]{2,1,0:T(8,128)(2,1)S(1)}, bf16[4,1024,256]{2,1,0:T(8,128)(2,1)S(1)}, u32[]{:S(2)}, u32[]{:S(2)}) collective-permute-start(bf16[4,1024,256]{2,1,0:T(8,128)(2,1)S(1)} %base_products.9), channel_id=1, source_target_pairs={{0,1},{1,0},{2,3},{3,2},{4,5},{5,4},{6,7},{7,6},{8,9},{9,8},{10,11... | collective-permute-start | bytes 6291464 | tf_op jit(solution)/shard_map/ppermute | solution.py:306
  47.1 11.6 %copy-start.3 = (bf16[1,1024,256]{2,1,0:T(8,128)(2,1)}, bf16[1,1024,256]{2,1,0:T(8,128)(2,1)S(1)}, u32[]{:S(2)}) copy-start(bf16[1,1024,256]{2,1,0:T(8,128)(2,1)S(1)} %get-tuple-element.37.refs_0_) | copy-start | bytes 1572868
  47.1 19.9 %collective-permute-start.4 = (bf16[1,1024,256]{2,1,0:T(8,128)(2,1)S(1)}, bf16[1,1024,256]{2,1,0:T(8,128)(2,1)S(1)}, u32[]{:S(2)}, u32[]{:S(2)}) collective-permute-start(bf16[1,1024,256]{2,1,0:T(8,128)(2,1)S(1)} %get-tuple-element.38), channel_id=1, source_target_pairs={{0,2},{1,3},{2,0},{3,1},{4,6},{5,7},{6,4},{7,5},{8,10},{9,11},{10,... | collective-permute-start | bytes 1572872 | tf_op jit(solution)/shard_map/ppermute | solution.py:320
  48.7 24.8 %collective-permute-start.5 = (bf16[1,1024,256]{2,1,0:T(8,128)(2,1)S(1)}, bf16[1,1024,256]{2,1,0:T(8,128)(2,1)S(1)}, u32[]{:S(2)}, u32[]{:S(2)}) collective-permute-start(bf16[1,1024,256]{2,1,0:T(8,128)(2,1)S(1)} %get-tuple-element.39), channel_id=1, source_target_pairs={{0,4},{1,5},{2,6},{3,7},{4,0},{5,1},{6,2},{7,3},{8,12},{9,13},{10,... | collective-permute-start | bytes 1572872 | tf_op jit(solution)/shard_map/ppermute | solution.py:320
  50.2 23.3 %collective-permute-start.6 = (bf16[1,1024,256]{2,1,0:T(8,128)(2,1)S(1)}, bf16[1,1024,256]{2,1,0:T(8,128)(2,1)S(1)}, u32[]{:S(2)}, u32[]{:S(2)}) collective-permute-start(bf16[1,1024,256]{2,1,0:T(8,128)(2,1)S(1)} %get-tuple-element.40), channel_id=1, source_target_pairs={{0,6},{1,7},{2,4},{3,5},{4,2},{5,3},{6,0},{7,1},{8,14},{9,15},{10,... | collective-permute-start | bytes 1572872 | tf_op jit(solution)/shard_map/ppermute | solution.py:320
  58.8 27.3 %collective-permute-start.11 = (bf16[4,1024,256]{2,1,0:T(8,128)(2,1)S(1)}, bf16[4,1024,256]{2,1,0:T(8,128)(2,1)S(1)}, u32[]{:S(2)}, u32[]{:S(2)}) collective-permute-start(bf16[4,1024,256]{2,1,0:T(8,128)(2,1)S(1)} %base_products.11), channel_id=1, source_target_pairs={{0,1},{1,0},{2,3},{3,2},{4,5},{5,4},{6,7},{7,6},{8,9},{9,8},{10,11... | collective-permute-start | bytes 6291464 | tf_op jit(solution)/shard_map/ppermute | solution.py:306
  67.0 15.3 %copy-start.4 = (bf16[1,1024,256]{2,1,0:T(8,128)(2,1)}, bf16[1,1024,256]{2,1,0:T(8,128)(2,1)S(1)}, u32[]{:S(2)}) copy-start(bf16[1,1024,256]{2,1,0:T(8,128)(2,1)S(1)} %get-tuple-element.43.refs_4_) | copy-start | bytes 1572868
  67.0 15.3 %copy-start.7 = (bf16[1,1024,256]{2,1,0:T(8,128)(2,1)}, bf16[1,1024,256]{2,1,0:T(8,128)(2,1)S(1)}, u32[]{:S(2)}) copy-start(bf16[1,1024,256]{2,1,0:T(8,128)(2,1)S(1)} %collective-permute-done.4.refs_1_) | copy-start | bytes 1572868
  73.5 8.9 %copy-start.8 = (bf16[1,1024,256]{2,1,0:T(8,128)(2,1)}, bf16[1,1024,256]{2,1,0:T(8,128)(2,1)S(1)}, u32[]{:S(2)}) copy-start(bf16[1,1024,256]{2,1,0:T(8,128)(2,1)S(1)} %collective-permute-done.5.refs_2_) | copy-start | bytes 1572868
  73.5 8.9 %copy-start.9 = (bf16[1,1024,256]{2,1,0:T(8,128)(2,1)}, bf16[1,1024,256]{2,1,0:T(8,128)(2,1)S(1)}, u32[]{:S(2)}) copy-start(bf16[1,1024,256]{2,1,0:T(8,128)(2,1)S(1)} %collective-permute-done.6.refs_3_) | copy-start | bytes 1572868
  82.4 27.2 %collective-permute-start.15 = (bf16[4,1024,256]{2,1,0:T(8,128)(2,1)}, bf16[4,1024,256]{2,1,0:T(8,128)(2,1)}, u32[]{:S(2)}, u32[]{:S(2)}) collective-permute-start(bf16[4,1024,256]{2,1,0:T(8,128)(2,1)} %base_products.13), channel_id=1, source_target_pairs={{0,1},{1,0},{2,3},{3,2},{4,5},{5,4},{6,7},{7,6},{8,9},{9,8},{10,11... | collective-permute-start | bytes 6291464 | tf_op jit(solution)/shard_map/ppermute | solution.py:306
  82.5 14.9 %collective-permute-start.8 = (bf16[1,1024,256]{2,1,0:T(8,128)(2,1)S(1)}, bf16[1,1024,256]{2,1,0:T(8,128)(2,1)S(1)}, u32[]{:S(2)}, u32[]{:S(2)}) collective-permute-start(bf16[1,1024,256]{2,1,0:T(8,128)(2,1)S(1)} %get-tuple-element.44), channel_id=1, source_target_pairs={{0,2},{1,3},{2,0},{3,1},{4,6},{5,7},{6,4},{7,5},{8,10},{9,11},{10,... | collective-permute-start | bytes 1572872 | tf_op jit(solution)/shard_map/ppermute | solution.py:320
  83.8 23.2 %collective-permute-start.9 = (bf16[1,1024,256]{2,1,0:T(8,128)(2,1)S(1)}, bf16[1,1024,256]{2,1,0:T(8,128)(2,1)}, u32[]{:S(2)}, u32[]{:S(2)}) collective-permute-start(bf16[1,1024,256]{2,1,0:T(8,128)(2,1)S(1)} %get-tuple-element.45), channel_id=1, source_target_pairs={{0,4},{1,5},{2,6},{3,7},{4,0},{5,1},{6,2},{7,3},{8,12},{9,13},{10,... | collective-permute-start | bytes 1572872 | tf_op jit(solution)/shard_map/ppermute | solution.py:320
  84.6 25.0 %collective-permute-start.10 = (bf16[1,1024,256]{2,1,0:T(8,128)(2,1)S(1)}, bf16[1,1024,256]{2,1,0:T(8,128)(2,1)}, u32[]{:S(2)}, u32[]{:S(2)}) collective-permute-start(bf16[1,1024,256]{2,1,0:T(8,128)(2,1)S(1)} %get-tuple-element.46), channel_id=1, source_target_pairs={{0,6},{1,7},{2,4},{3,5},{4,2},{5,3},{6,0},{7,1},{8,14},{9,15},{10,... | collective-permute-start | bytes 1572872 | tf_op jit(solution)/shard_map/ppermute | solution.py:320
  95.4 0.8 copy-start.5
  96.2 25.8 %collective-permute-start.12 = (bf16[1,1024,256]{2,1,0:T(8,128)(2,1)}, bf16[1,1024,256]{2,1,0:T(8,128)(2,1)}, u32[]{:S(2)}, u32[]{:S(2)}) collective-permute-start(bf16[1,1024,256]{2,1,0:T(8,128)(2,1)} %get-tuple-element.50), channel_id=1, source_target_pairs={{0,2},{1,3},{2,0},{3,1},{4,6},{5,7},{6,4},{7,5},{8,10},{9,11},{10,... | collective-permute-start | bytes 1572872 | tf_op jit(solution)/shard_map/ppermute | solution.py:320
  97.4 0.8 copy-start.10
  98.2 23.8 %collective-permute-start.13 = (bf16[1,1024,256]{2,1,0:T(8,128)(2,1)}, bf16[1,1024,256]{2,1,0:T(8,128)(2,1)}, u32[]{:S(2)}, u32[]{:S(2)}) collective-permute-start(bf16[1,1024,256]{2,1,0:T(8,128)(2,1)} %get-tuple-element.51), channel_id=1, source_target_pairs={{0,4},{1,5},{2,6},{3,7},{4,0},{5,1},{6,2},{7,3},{8,12},{9,13},{10,... | collective-permute-start | bytes 1572872 | tf_op jit(solution)/shard_map/ppermute | solution.py:320
  109.6 2.5 %copy-start.1 = (bf16[1024,2560]{1,0:T(8,128)(2,1)S(1)}, bf16[1024,2560]{1,0:T(8,128)(2,1)}, u32[]{:S(2)}) copy-start(bf16[1024,2560]{1,0:T(8,128)(2,1)} %hidden_ref.17) | copy-start | bytes 15728644
  121.2 0.8 copy-start.2
  133.8 52.2 %all-to-all-start.1 = ((bf16[4,4,64,1024]{3,2,1,0:T(8,128)(2,1)}), bf16[4,4,64,1024]{3,2,1,0:T(8,128)(2,1)}, u32[]{:S(2)}, u32[]{:S(2)}) async-start(bf16[4,4,64,1024]{3,2,1,0:T(8,128)(2,1)} %adapters_to_send.3), calls=%async_computation.1 | async-start | bytes 4194304 | tf_op jit(solution)/shard_map/all_to_all | solution.py:293
  138.3 16.0 %collective-permute-start.14 = (bf16[1,1024,256]{2,1,0:T(8,128)(2,1)S(1)}, bf16[1,1024,256]{2,1,0:T(8,128)(2,1)}, u32[]{:S(2)}, u32[]{:S(2)}) collective-permute-start(bf16[1,1024,256]{2,1,0:T(8,128)(2,1)S(1)} %get-tuple-element.52), channel_id=1, source_target_pairs={{0,6},{1,7},{2,4},{3,5},{4,2},{5,3},{6,0},{7,1},{8,14},{9,15},{10,... | collective-permute-start | bytes 1572872 | tf_op jit(solution)/shard_map/ppermute | solution.py:320
  140.8 24.8 %collective-permute-start.16 = (bf16[1,1024,256]{2,1,0:T(8,128)(2,1)}, bf16[1,1024,256]{2,1,0:T(8,128)(2,1)}, u32[]{:S(2)}, u32[]{:S(2)}) collective-permute-start(bf16[1,1024,256]{2,1,0:T(8,128)(2,1)} %get-tuple-element.56), channel_id=1, source_target_pairs={{0,2},{1,3},{2,0},{3,1},{4,6},{5,7},{6,4},{7,5},{8,10},{9,11},{10,... | collective-permute-start | bytes 1572872 | tf_op jit(solution)/shard_map/ppermute | solution.py:320
  141.4 30.5 %collective-permute-start.17 = (bf16[1,1024,256]{2,1,0:T(8,128)(2,1)S(1)}, bf16[1,1024,256]{2,1,0:T(8,128)(2,1)}, u32[]{:S(2)}, u32[]{:S(2)}) collective-permute-start(bf16[1,1024,256]{2,1,0:T(8,128)(2,1)S(1)} %get-tuple-element.57), channel_id=1, source_target_pairs={{0,4},{1,5},{2,6},{3,7},{4,0},{5,1},{6,2},{7,3},{8,12},{9,13},{10,... | collective-permute-start | bytes 1572872 | tf_op jit(solution)/shard_map/ppermute | solution.py:320
  141.9 34.9 %collective-permute-start.18 = (bf16[1,1024,256]{2,1,0:T(8,128)(2,1)S(1)}, bf16[1,1024,256]{2,1,0:T(8,128)(2,1)}, u32[]{:S(2)}, u32[]{:S(2)}) collective-permute-start(bf16[1,1024,256]{2,1,0:T(8,128)(2,1)S(1)} %get-tuple-element.58), channel_id=1, source_target_pairs={{0,6},{1,7},{2,4},{3,5},{4,2},{5,3},{6,0},{7,1},{8,14},{9,15},{10,... | collective-permute-start | bytes 1572872 | tf_op jit(solution)/shard_map/ppermute | solution.py:320
  150.9 1.6 collective-permute-start.19
  153.5 18.4 %copy-start.6 = (bf16[8,64,128]{2,1,0:T(8,128)(2,1)}, bf16[8,64,128]{2,1,0:T(8,128)(2,1)S(1)}, u32[]{:S(2)}) copy-start(bf16[8,64,128]{2,1,0:T(8,128)(2,1)S(1)} %add.25.refs_4_) | copy-start | bytes 393220
  153.5 25.5 %collective-permute-start.22 = (bf16[8,64,128]{2,1,0:T(8,128)(2,1)S(1)}, bf16[8,64,128]{2,1,0:T(8,128)(2,1)S(1)}, u32[]{:S(2)}, u32[]{:S(2)}) collective-permute-start(bf16[8,64,128]{2,1,0:T(8,128)(2,1)S(1)} %add.25.refs_4_), channel_id=1, source_target_pairs={{0,6},{1,7},{2,4},{3,5},{4,2},{5,3},{6,0},{7,1},{8,14},{9,15},{10,... | collective-permute-start | bytes 393224 | tf_op jit(solution)/shard_map/ppermute | solution.py:328
  154.3 26.0 %collective-permute-start.21 = (bf16[8,64,128]{2,1,0:T(8,128)(2,1)S(1)}, bf16[8,64,128]{2,1,0:T(8,128)(2,1)S(1)}, u32[]{:S(2)}, u32[]{:S(2)}) collective-permute-start(bf16[8,64,128]{2,1,0:T(8,128)(2,1)S(1)} %add.25.refs_4_), channel_id=1, source_target_pairs={{0,4},{1,5},{2,6},{3,7},{4,0},{5,1},{6,2},{7,3},{8,12},{9,13},{10,... | collective-permute-start | bytes 393224 | tf_op jit(solution)/shard_map/ppermute | solution.py:328
  165.6 14.8 %collective-permute-start.20 = (bf16[8,64,128]{2,1,0:T(8,128)(2,1)S(1)}, bf16[8,64,128]{2,1,0:T(8,128)(2,1)S(1)}, u32[]{:S(2)}, u32[]{:S(2)}) collective-permute-start(bf16[8,64,128]{2,1,0:T(8,128)(2,1)S(1)} %add.25.refs_4_), channel_id=1, source_target_pairs={{0,2},{1,3},{2,0},{3,1},{4,6},{5,7},{6,4},{7,5},{8,10},{9,11},{10,... | collective-permute-start | bytes 393224 | tf_op jit(solution)/shard_map/ppermute | solution.py:328
  179.0 1.4 copy-start.11
  180.2 0.7 copy-start.12
  180.9 0.7 copy-start.13
